TPU v7x, 256 devices: a whole 4x4x8 slice. The times are simulated.
256 devices in a mesh: gx: 16 (over x, z_lo), gy: 16 (over z_hi, y, core).
Axes of the slice: x: 4, y: 4, z: 8 (z_hi: 2, z_lo: 4; z = z_hi * 4 + z_lo), core: 2. Of those that a mesh axis runs over, the one named last changes fastest.
Arguments:
- ensemble: bfloat16 [128, 128, 64, 128], P('gx', 'gy'), may hold values from -6 to 6
- obs_anom: bfloat16 [16, 16, 128, 128], P('gx', 'gy'), may hold values from -7 to 7
- obs_innov: bfloat16 [16, 16, 128], P('gx', 'gy'), may hold values from -8 to 8
- obs_prec: bfloat16 [16, 16, 128], P('gx', 'gy'), may hold values from 0.099609375 to 2
- obs_pos: int32 [16, 16, 2, 128], P('gx', 'gy'), may hold values from 0 to 7
- obs_count: int32 [16, 16], P('gx', 'gy'), may hold values from 16 to 128, as said below
Outputs:
- analysis: bfloat16 [128, 128, 64, 128], P('gx', 'gy')
Inputs may be any that keep to these rules, and one draw needn't show every extreme that they name: `obs_count`: some tile holds exactly the most and some tile exactly the least.
All inputs are finite; a program needn't handle non-finite values.
Results may differ from a plain program's by a relative error of at most 0.0022.
The roundings to bfloat16 on the way count: a program that leaves them out, or rounds other values in their place, can miss the bound.
Values may be sent and summed in bfloat16 or wider, within the bound.
No kernel may reach another device: no remote copies, remote signals or barrier semaphores. Data moves between devices by JAX's collectives and lax.ppermute only.
A program may use at most 128 MiB of HBM per device.

v0:
```python
import functools

import jax
import jax.numpy as jnp
from jax import lax
from jax.experimental import pallas as pl
from jax.experimental.pallas import tpu as pltpu
from jax.sharding import PartitionSpec as P

K = 128
APX = 4
CT = 8
SPACING = 2
RLOC = 12
NHALF = 32
ROWS = K + 16
VMEM = 50 << 20

NT = (((1,), (1,)), ((), ()))
NN = (((1,), (0,)), ((), ()))
F32 = jnp.float32
BF16 = jnp.bfloat16


def center(a):
    return SPACING * a + (SPACING - 1) / 2.0


def least_distance(offset, point):
    return min(abs(offset * CT + s - center(point)) for s in range(CT))


def tiles_of(point):
    a, b = point
    return [
        (ox, oy)
        for oy in range(-2, 3)
        for ox in range(-2, 3)
        if least_distance(ox, a) ** 2 + least_distance(oy, b) ** 2 < RLOC * RLOC
    ]


def split(x):
    hi = x.astype(BF16)
    lo = (x - hi.astype(F32)).astype(BF16)
    return hi, lo


def mm(a, b):
    left = jnp.concatenate([a[0], a[1]], 1)
    right = jnp.concatenate([b[0], b[1]], 1)
    right = jnp.concatenate([right, right], 0)
    out = lax.dot_general(left, right, NN, preferred_element_type=F32)
    return out[:, :K] + out[:, K:]


C0, C1, C2, C3, C4 = 2.25, -2.4375, 1.6875, -0.5625, 0.0625


def two_steps(xs, parts, eye):
    n = range(len(xs))
    sq = [mm(parts[i], parts[i]) for i in n]
    high = [mm(split(sq[i]), split(C3 * xs[i] + C4 * sq[i])) for i in n]
    return [C0 * eye + C1 * xs[i] + C2 * sq[i] + high[i] for i in n]


def four_steps(xs, eye):
    n = range(len(xs))
    x_parts = [split(x) for x in xs]
    z = two_steps(xs, x_parts, eye)
    z_parts = [split(v) for v in z]
    z_sq = [mm(z_parts[i], z_parts[i]) for i in n]
    m = [mm(x_parts[i], split(z_sq[i])) for i in n]
    q = two_steps(m, [split(v) for v in m], eye)
    return [mm(z_parts[i], split(q[i])) for i in n]


def pack_kernel(count_ref, anom_ref, innov_ref, prec_ref, pos_ref, out_ref):
    out_ref[0:K, :] = anom_ref[...].astype(F32).T.astype(BF16)
    slot = lax.broadcasted_iota(jnp.int32, (1, K), 1)
    live = jnp.where(slot < count_ref[0, 0], prec_ref[...].astype(F32), 0.0)
    meta = jnp.concatenate(
        [innov_ref[...].astype(F32), live, pos_ref[...].astype(F32), jnp.zeros((12, K), F32)], 0
    )
    out_ref[K:ROWS, :] = meta.astype(BF16)


def point_weights(meta, ox, oy, points):
    rows = (len(points) + 7) // 8 * 8
    at = lax.broadcasted_iota(jnp.int32, (rows, K), 0)
    px = jnp.zeros((rows, K), F32)
    py = px
    for i, (a, b) in enumerate(points):
        px = jnp.where(at == i, center(a), px)
        py = jnp.where(at == i, center(b), py)
    dx = (meta[2:3] + float(ox * CT)) - px
    dy = (meta[3:4] + float(oy * CT)) - py
    sq = dx * dx + dy * dy
    inside = sq < float(RLOC * RLOC)
    out = []
    for rate in (2.0, 4.5):
        out.append(jnp.where(inside, jnp.exp(-sq * (rate / (RLOC * RLOC))), 0.0) * meta[1:2])
    return out


def points_kernel(points, batch, *refs):
    x_refs, y_refs = refs[0:5], refs[5:9]
    out_ref, sw_ref, wp_ref, s_ref, g_ref, pull_ref = refs[9:]

    def block(t):
        ox, oy = t
        if oy == 0:
            return x_refs[ox + 2]
        wide = abs(oy) == 1
        ref = y_refs[{-1: 0, 1: 1, -2: 2, 2: 3}[oy]]
        return ref.at[ox + 2 if wide else ox + 1]

    seen = sorted({t for p in points for t in tiles_of(p)})
    place = {t: i for i, t in enumerate(seen)}
    rows = (len(points) + 7) // 8 * 8
    for t in seen:
        meta = block(t)[K:ROWS, :].astype(F32)
        w = point_weights(meta, t[0], t[1], points)
        lanes = slice(place[t] * K, place[t] * K + K)
        for g in range(2):
            sw_ref[place[t], g * rows : g * rows + rows, :] = jnp.sqrt(w[g])
        hi, lo = split(jnp.concatenate(w, 0) * meta[0:1])
        wp_ref[0 : 2 * rows, lanes] = hi
        wp_ref[2 * rows : 4 * rows, lanes] = lo
    anom_seen = jnp.concatenate([block(t)[0:K, :] for t in seen], 1)
    pull = lax.dot_general(
        anom_seen, wp_ref[:, 0 : len(seen) * K], NT, preferred_element_type=F32
    )
    pull_ref[...] = pull[:, 0 : 2 * rows] + pull[:, 2 * rows : 4 * rows]

    for i, p in enumerate(points):
        own = tiles_of(p)
        for j, t in enumerate(own):
            anom = block(t)[0:K, :].astype(F32)
            for g in range(2):
                scale = sw_ref[place[t], g * rows + i : g * rows + i + 1, :]
                s_ref[i % 2, g, :, j * K : j * K + K] = (anom * scale).astype(BF16)
        width = len(own) * K
        for g in range(2):
            s = s_ref[i % 2, g, :, 0:width]
            g_ref[2 * i + g] = lax.dot_general(s, s, NT, preferred_element_type=F32)

    row = lax.broadcasted_iota(jnp.int32, (K, K), 0)
    col = lax.broadcasted_iota(jnp.int32, (K, K), 1)
    eye = jnp.where(row == col, 1.0, 0.0).astype(F32)
    total = 2 * len(points)
    for first in range(0, total, batch):
        ids = range(first, min(first + batch, total))
        xs, norms = [], []
        for i in ids:
            system = eye + g_ref[i] * (1.0 / (K - 1.0))
            sq = jnp.sum(jnp.sum(system * system, 0, keepdims=True), 1, keepdims=True)
            norm = jnp.sqrt(sq)
            norms.append(norm)
            xs.append(system * (1.0 / norm))
        zs = four_steps(xs, eye)
        for i, z, norm in zip(ids, zs, norms):
            lane = (i % 2) * rows + i // 2
            inner = jnp.sum(z * pull_ref[:, lane : lane + 1], 0, keepdims=True)
            shift = jnp.sum(z * inner, 1, keepdims=True) * (1.0 / (norm * (K - 1.0)))
            out_ref[i // 2, i % 2] = (z * (1.0 / jnp.sqrt(norm)) + shift).astype(BF16)


def transforms(points, x_blocks, y_blocks, batch, name):
    rows = (len(points) + 7) // 8 * 8
    seen = len({t for p in points for t in tiles_of(p)})
    most = max(len(tiles_of(p)) for p in points)
    n = len(points)
    return pl.pallas_call(
        functools.partial(points_kernel, points, batch),
        out_shape=jax.ShapeDtypeStruct((n, 2, K, K), BF16),
        scratch_shapes=[
            pltpu.VMEM((seen, 2 * rows, K), F32),
            pltpu.VMEM((4 * rows, seen * K), BF16),
            pltpu.VMEM((2, 2, K, most * K), BF16),
            pltpu.VMEM((2 * n, K, K), F32),
            pltpu.VMEM((K, 2 * rows), F32),
        ],
        compiler_params=pltpu.CompilerParams(vmem_limit_bytes=VMEM),
        cost_estimate=pl.CostEstimate(
            flops=n * 1_400_000_000 // 2, bytes_accessed=4_000_000, transcendentals=0
        ),
        name=name,
    )(*x_blocks, *y_blocks)


def apply_kernel(edge_ref, ens_ref, own_ref, low_ref, high_ref, out_ref, rim_ref):
    for side, (src, own) in enumerate(((low_ref, 0), (high_ref, APX - 1))):

        @pl.when(edge_ref[side] != 0)
        def _():
            rim_ref[side] = own_ref[own]

        @pl.when(edge_ref[side] == 0)
        def _():
            rim_ref[side] = src[...]

    def transform(x, y, g):
        if y == 0:
            return rim_ref[0, x, g]
        if y == APX + 1:
            return rim_ref[1, x, g]
        return own_ref[y - 1, x, g]

    ones = jnp.ones((K, K), BF16)
    frac = [(s + 0.5) / SPACING for s in range(SPACING)]
    corner = [[1.0 - f for f in frac], frac]
    for q in range(APX + 1):
        for p in range(APX + 1):
            cells = [
                (s, t)
                for s in range(2)
                for t in range(2)
                if 0 <= 2 * q - 1 + s < CT and 0 <= 2 * p - 1 + t < CT
            ]
            ens = jnp.concatenate([ens_ref[2 * q - 1 + s, 2 * p - 1 + t] for s, t in cells], 0)
            mean = lax.dot_general(ens, ones, NN, preferred_element_type=F32) * (1.0 / K)
            anom = (ens.astype(F32) - mean).astype(BF16)
            for g in range(2):
                spans = [slice(c * 2 * NHALF + g * NHALF, c * 2 * NHALF + (g + 1) * NHALF) for c in range(len(cells))]
                left = jnp.concatenate([anom[sp] for sp in spans], 0)
                sums = [mean[sp] for sp in spans]
                adds = [None] * len(cells)
                for cx in range(2):
                    for cy in range(2):
                        prod = lax.dot_general(
                            left, transform(q + cx, p + cy, g), NN, preferred_element_type=F32
                        )
                        for c, (s, t) in enumerate(cells):
                            term = prod[c * NHALF : (c + 1) * NHALF] * (corner[cx][s] * corner[cy][t])
                            adds[c] = term if adds[c] is None else adds[c] + term
                for c, (s, t) in enumerate(cells):
                    out_ref[2 * q - 1 + s, 2 * p - 1 + t, g * NHALF : (g + 1) * NHALF, :] = (
                        sums[c] + adds[c]
                    ).astype(BF16)


def apply(edges, ensemble, own, low, high):
    return pl.pallas_call(
        apply_kernel,
        out_shape=jax.ShapeDtypeStruct(ensemble.shape, BF16),
        in_specs=[pl.BlockSpec(memory_space=pltpu.SMEM)] + [pl.BlockSpec(memory_space=pltpu.VMEM)] * 4,
        scratch_shapes=[pltpu.VMEM((2, APX + 2, 2, K, K), BF16)],
        compiler_params=pltpu.CompilerParams(vmem_limit_bytes=VMEM),
        name="apply_transforms",
    )(edges, ensemble, own, low, high)


def shifted(block, axis, distance, closed):
    n = lax.axis_size(axis)
    pairs = [((i + distance) % n, i) for i in range(n) if closed or 0 <= i + distance < n]
    return lax.ppermute(block, axis, pairs)


def shards(ensemble, obs_anom, obs_innov, obs_prec, obs_pos, obs_count):
    own = pl.pallas_call(
        pack_kernel,
        out_shape=jax.ShapeDtypeStruct((ROWS, K), BF16),
        in_specs=[pl.BlockSpec(memory_space=pltpu.SMEM)] + [pl.BlockSpec(memory_space=pltpu.VMEM)] * 4,
        name="pack_slots",
    )(
        obs_count,
        obs_anom.reshape(K, K),
        obs_innov.reshape(1, K),
        obs_prec.reshape(1, K),
        obs_pos.reshape(2, K),
    )
    x_blocks = {0: own}
    for d in (-2, -1, 1, 2):
        x_blocks[d] = shifted(own, "gx", d, True)
    x_list = [x_blocks[d] for d in range(-2, 3)]
    wide = jnp.stack(x_list)
    near = jnp.stack(x_list[1:4])
    y_blocks = [shifted(wide if abs(d) == 1 else near, "gy", d, False) for d in (-1, 1, -2, 2)]
    across = range(-1, APX + 1)
    outer = transforms([(a, b) for b in (0, APX - 1) for a in across], x_list, y_blocks, 12, "outer_points")
    inner = transforms([(a, b) for b in (1, 2) for a in across], x_list, y_blocks, 12, "inner_points")
    outer = outer.reshape(2, APX + 2, 2, K, K)
    inner = inner.reshape(2, APX + 2, 2, K, K)
    low = shifted(outer[1], "gy", -1, False)
    high = shifted(outer[0], "gy", 1, False)
    mats = jnp.concatenate([outer[0:1], inner, outer[1:2]], 0)
    row = lax.axis_index("gy")
    edges = jnp.stack([row == 0, row == lax.axis_size("gy") - 1]).astype(jnp.int32)
    return apply(edges, ensemble, mats, low, high)


def solution(mesh):
    placed = (
        P("gx", "gy", None, None),
        P("gx", "gy", None, None),
        P("gx", "gy", None),
        P("gx", "gy", None),
        P("gx", "gy", None, None),
        P("gx", "gy"),
    )
    return jax.shard_map(
        shards, mesh=mesh, in_specs=placed, out_specs=P("gx", "gy", None, None), check_vma=False
    )
```

profile of v0, /device:TPU:95, one launch (start us, length us, event | category | flops | bytes accessed | tf_op | source)
XLA Modules:
  0.0 83.4 jit_solution(1382992556443312956)
XLA Ops:
  0.7 1.5 %pack_slots.1.refs_2_ = bf16[144,128]{1,0:T(8,128)(2,1)} custom-call(s32[1,1]{1,0:T(1,128)S(6)} %copy.11.count_ref, bf16[128,128]{1,0:T(8,128)(2,1)} %bitcast.25, bf16[1,128]{1,0:T(2,128)(2,1)} %bitcast.27, bf16[1,128]{1,0:T(2,128)(2,1)} %bitcast.28, s32[2,128]{1,0:T(2,128)} %bitcast.26), custom_call_target="tpu_custom_call" | custom-call | tf_op jit(solution)/shard_map/pack_slots/pallas_call | solution.py:261
  2.1 0.0 collective-permute-start
  2.2 1.6 %collective-permute-start.1 = (bf16[144,128]{1,0:T(8,128)(2,1)}, bf16[144,128]{1,0:T(8,128)(2,1)S(1)}, u32[]{:S(2)}, u32[]{:S(2)}) collective-permute-start(bf16[144,128]{1,0:T(8,128)(2,1)} %pack_slots.1.refs_2_), channel_id=1, source_target_pairs={{240,0},{0,16},{16,32},{32,48},{48,64},{64,80},{80,96},{96,112},{1... | collective-permute-start | bytes 110600 | tf_op jit(solution)/shard_map/ppermute | solution.py:257
  3.8 1.2 %collective-permute-start.2 = (bf16[144,128]{1,0:T(8,128)(2,1)}, bf16[144,128]{1,0:T(8,128)(2,1)S(1)}, u32[]{:S(2)}, u32[]{:S(2)}) collective-permute-start(bf16[144,128]{1,0:T(8,128)(2,1)} %pack_slots.1.refs_2_), channel_id=1, source_target_pairs={{16,0},{32,16},{48,32},{64,48},{80,64},{96,80},{112,96},{128,112},... | collective-permute-start | bytes 110600 | tf_op jit(solution)/shard_map/ppermute | solution.py:257
  5.0 3.7 %collective-permute-start.3 = (bf16[144,128]{1,0:T(8,128)(2,1)}, bf16[144,128]{1,0:T(8,128)(2,1)S(1)}, u32[]{:S(2)}, u32[]{:S(2)}) collective-permute-start(bf16[144,128]{1,0:T(8,128)(2,1)} %pack_slots.1.refs_2_), channel_id=1, source_target_pairs={{32,0},{48,16},{64,32},{80,48},{96,64},{112,80},{128,96},{144,112}... | collective-permute-start | bytes 110600 | tf_op jit(solution)/shard_map/ppermute | solution.py:257
  8.7 0.0 collective-permute-done.refs_0_
  8.7 0.0 collective-permute-done.1.refs_1_
  8.7 0.8 constant_dynamic-update-slice_fusion.1
  9.5 0.0 collective-permute-done.2.refs_3_
  9.5 2.2 %collective-permute-done.3.refs_4_ = bf16[144,128]{1,0:T(8,128)(2,1)S(1)} collective-permute-done((bf16[144,128]{1,0:T(8,128)(2,1)}, bf16[144,128]{1,0:T(8,128)(2,1)S(1)}, u32[]{:S(2)}, u32[]{:S(2)}) %collective-permute-start.3) | collective-permute-done | bytes 36896 | tf_op jit(solution)/shard_map/ppermute | solution.py:257
  11.8 8.9 %collective-permute-start.4 = (bf16[5,144,128]{2,1,0:T(8,128)(2,1)S(1)}, bf16[5,144,128]{2,1,0:T(8,128)(2,1)S(1)}, u32[]{:S(2)}, u32[]{:S(2)}) collective-permute-start(bf16[5,144,128]{2,1,0:T(8,128)(2,1)S(1)} %bitcast_dynamic-update-slice_fusion), channel_id=1, source_target_pairs={{0,1},{1,2},{2,3},{3,4},{4,5},{5,6},{6,7},{7,8},{8,9},{9,10},{10,1... | collective-permute-start | bytes 552968 | tf_op jit(solution)/shard_map/ppermute | solution.py:257
  20.7 1.9 %collective-permute-start.5 = (bf16[5,144,128]{2,1,0:T(8,128)(2,1)S(1)}, bf16[5,144,128]{2,1,0:T(8,128)(2,1)S(1)}, u32[]{:S(2)}, u32[]{:S(2)}) collective-permute-start(bf16[5,144,128]{2,1,0:T(8,128)(2,1)S(1)} %bitcast_dynamic-update-slice_fusion), channel_id=1, source_target_pairs={{1,0},{2,1},{3,2},{4,3},{5,4},{6,5},{7,6},{8,7},{9,8},{10,9},{11,1... | collective-permute-start | bytes 552968 | tf_op jit(solution)/shard_map/ppermute | solution.py:257
  22.6 0.8 pad_maximum_fusion.1
  23.4 3.2 %collective-permute-start.6 = (bf16[3,144,128]{2,1,0:T(8,128)(2,1)S(1)}, bf16[3,144,128]{2,1,0:T(8,128)(2,1)S(1)}, u32[]{:S(2)}, u32[]{:S(2)}) collective-permute-start(bf16[3,144,128]{2,1,0:T(8,128)(2,1)S(1)} %pad_maximum_fusion.1), channel_id=1, source_target_pairs={{0,2},{1,3},{2,4},{3,5},{4,6},{5,7},{6,8},{7,9},{8,10},{9,11},{10,... | collective-permute-start | bytes 331784 | tf_op jit(solution)/shard_map/ppermute | solution.py:257
  26.6 2.1 %collective-permute-start.7 = (bf16[3,144,128]{2,1,0:T(8,128)(2,1)S(1)}, bf16[3,144,128]{2,1,0:T(8,128)(2,1)S(1)}, u32[]{:S(2)}, u32[]{:S(2)}) collective-permute-start(bf16[3,144,128]{2,1,0:T(8,128)(2,1)S(1)} %pad_maximum_fusion.1), channel_id=1, source_target_pairs={{2,0},{3,1},{4,2},{5,3},{6,4},{7,5},{8,6},{9,7},{10,8},{11,9},{12,... | collective-permute-start | bytes 331784 | tf_op jit(solution)/shard_map/ppermute | solution.py:257
  28.7 0.1 add_convert_fusion.edge_ref
  28.8 0.7 collective-permute-done.6.refs_7_
  29.5 9.8 %collective-permute-done.7.refs_8_ = bf16[3,144,128]{2,1,0:T(8,128)(2,1)S(1)} collective-permute-done((bf16[3,144,128]{2,1,0:T(8,128)(2,1)S(1)}, bf16[3,144,128]{2,1,0:T(8,128)(2,1)S(1)}, u32[]{:S(2)}, u32[]{:S(2)}) %collective-permute-start.7) | collective-permute-done | bytes 110624 | tf_op jit(solution)/shard_map/ppermute | solution.py:257
  39.3 0.0 collective-permute-done.4.refs_5_
  39.3 0.0 collective-permute-done.5.refs_6_
  39.3 0.8 copy-done.1
  40.1 8.1 %outer_points.1 = bf16[12,2,128,128]{3,2,1,0:T(8,128)(2,1)S(1)} custom-call(bf16[144,128]{1,0:T(8,128)(2,1)S(1)} %collective-permute-done.refs_0_, bf16[144,128]{1,0:T(8,128)(2,1)S(1)} %collective-permute-done.1.refs_1_, bf16[144,128]{1,0:T(8,128)(2,1)S(1)} %copy-done.1, bf16[144,128]{1,0:T(8,128)(2,1)S(1)} %collective-permute-done.2.refs_3_, ...), custom_call_target="tpu_custom_call" | custom-call | flops 8400000000 | bytes 4000000 | tf_op jit(solution)/shard_map/outer_points/pallas_call | solution.py:174
  48.2 0.0 copy-start.2
  48.3 0.4 fusion
  48.6 9.1 %collective-permute-start.8 = (bf16[6,2,128,128]{3,2,1,0:T(8,128)(2,1)S(1)}, bf16[6,2,128,128]{3,2,1,0:T(8,128)(2,1)S(1)}, u32[]{:S(2)}, u32[]{:S(2)}) collective-permute-start(bf16[6,2,128,128]{3,2,1,0:T(8,128)(2,1)S(1)} %get-tuple-element.8), channel_id=1, source_target_pairs={{0,1},{1,2},{2,3},{3,4},{4,5},{5,6},{6,7},{7,8},{8,9},{9,10},{10,1... | collective-permute-start | bytes 1179656 | tf_op jit(solution)/shard_map/ppermute | solution.py:257
  57.7 2.9 %collective-permute-start.9 = (bf16[6,2,128,128]{3,2,1,0:T(8,128)(2,1)S(1)}, bf16[6,2,128,128]{3,2,1,0:T(8,128)(2,1)S(1)}, u32[]{:S(2)}, u32[]{:S(2)}) collective-permute-start(bf16[6,2,128,128]{3,2,1,0:T(8,128)(2,1)S(1)} %get-tuple-element.5), channel_id=1, source_target_pairs={{1,0},{2,1},{3,2},{4,3},{5,4},{6,5},{7,6},{8,7},{9,8},{10,9},{11,1... | collective-permute-start | bytes 1179656 | tf_op jit(solution)/shard_map/ppermute | solution.py:257
  60.7 8.1 %inner_points.1 = bf16[12,2,128,128]{3,2,1,0:T(8,128)(2,1)S(1)} custom-call(bf16[144,128]{1,0:T(8,128)(2,1)S(1)} %collective-permute-done.refs_0_, bf16[144,128]{1,0:T(8,128)(2,1)S(1)} %collective-permute-done.1.refs_1_, bf16[144,128]{1,0:T(8,128)(2,1)S(1)} %copy-done.2, bf16[144,128]{1,0:T(8,128)(2,1)S(1)} %collective-permute-done.2.refs_3_, ...), custom_call_target="tpu_custom_call" | custom-call | flops 8400000000 | bytes 4000000 | tf_op jit(solution)/shard_map/inner_points/pallas_call | solution.py:174
  68.8 0.0 copy-start
  68.8 0.2 pad_maximum_fusion.own_ref
  69.0 0.0 collective-permute-done.8.low_ref
  69.0 7.7 %collective-permute-done.9.high_ref = bf16[6,2,128,128]{3,2,1,0:T(8,128)(2,1)S(1)} collective-permute-done((bf16[6,2,128,128]{3,2,1,0:T(8,128)(2,1)S(1)}, bf16[6,2,128,128]{3,2,1,0:T(8,128)(2,1)S(1)}, u32[]{:S(2)}, u32[]{:S(2)}) %collective-permute-start.9) | collective-permute-done | bytes 393248 | tf_op jit(solution)/shard_map/ppermute | solution.py:257
  76.7 6.7 %apply_transforms.1 = bf16[8,8,64,128]{3,2,1,0:T(8,128)(2,1)} custom-call(s32[2]{0:T(128)S(1)} %add_convert_fusion.edge_ref, bf16[8,8,64,128]{3,2,1,0:T(8,128)(2,1)S(1)} %copy-done, bf16[4,6,2,128,128]{4,3,2,1,0:T(8,128)(2,1)S(1)} %pad_maximum_fusion.own_ref, bf16[6,2,128,128]{3,2,1,0:T(8,128)(2,1)S(1)} %collective-permute-done.8.low_ref, ...), custom_call_target="tpu_custom_call" | custom-call | tf_op jit(solution)/shard_map/apply_transforms/pallas_call | solution.py:244
  (7 shorter events, 0.0 us)
Async XLA Ops:
  2.1 6.5 %collective-permute-start = (bf16[144,128]{1,0:T(8,128)(2,1)}, bf16[144,128]{1,0:T(8,128)(2,1)S(1)}, u32[]{:S(2)}, u32[]{:S(2)}) collective-permute-start(bf16[144,128]{1,0:T(8,128)(2,1)} %pack_slots.1.refs_2_), channel_id=1, source_target_pairs={{224,0},{240,16},{0,32},{16,48},{32,64},{48,80},{64,96},{80,112},{... | collective-permute-start | bytes 110600 | tf_op jit(solution)/shard_map/ppermute | solution.py:257
  2.2 6.5 %collective-permute-start.1 = (bf16[144,128]{1,0:T(8,128)(2,1)}, bf16[144,128]{1,0:T(8,128)(2,1)S(1)}, u32[]{:S(2)}, u32[]{:S(2)}) collective-permute-start(bf16[144,128]{1,0:T(8,128)(2,1)} %pack_slots.1.refs_2_), channel_id=1, source_target_pairs={{240,0},{0,16},{16,32},{32,48},{48,64},{64,80},{80,96},{96,112},{1... | collective-permute-start | bytes 110600 | tf_op jit(solution)/shard_map/ppermute | solution.py:257
  3.8 5.7 %collective-permute-start.2 = (bf16[144,128]{1,0:T(8,128)(2,1)}, bf16[144,128]{1,0:T(8,128)(2,1)S(1)}, u32[]{:S(2)}, u32[]{:S(2)}) collective-permute-start(bf16[144,128]{1,0:T(8,128)(2,1)} %pack_slots.1.refs_2_), channel_id=1, source_target_pairs={{16,0},{32,16},{48,32},{64,48},{80,64},{96,80},{112,96},{128,112},... | collective-permute-start | bytes 110600 | tf_op jit(solution)/shard_map/ppermute | solution.py:257
  5.0 6.8 %collective-permute-start.3 = (bf16[144,128]{1,0:T(8,128)(2,1)}, bf16[144,128]{1,0:T(8,128)(2,1)S(1)}, u32[]{:S(2)}, u32[]{:S(2)}) collective-permute-start(bf16[144,128]{1,0:T(8,128)(2,1)} %pack_slots.1.refs_2_), channel_id=1, source_target_pairs={{32,0},{48,16},{64,32},{80,48},{96,64},{112,80},{128,96},{144,112}... | collective-permute-start | bytes 110600 | tf_op jit(solution)/shard_map/ppermute | solution.py:257
  11.8 27.6 %collective-permute-start.4 = (bf16[5,144,128]{2,1,0:T(8,128)(2,1)S(1)}, bf16[5,144,128]{2,1,0:T(8,128)(2,1)S(1)}, u32[]{:S(2)}, u32[]{:S(2)}) collective-permute-start(bf16[5,144,128]{2,1,0:T(8,128)(2,1)S(1)} %bitcast_dynamic-update-slice_fusion), channel_id=1, source_target_pairs={{0,1},{1,2},{2,3},{3,4},{4,5},{5,6},{6,7},{7,8},{8,9},{9,10},{10,1... | collective-permute-start | bytes 552968 | tf_op jit(solution)/shard_map/ppermute | solution.py:257
  20.7 18.6 %collective-permute-start.5 = (bf16[5,144,128]{2,1,0:T(8,128)(2,1)S(1)}, bf16[5,144,128]{2,1,0:T(8,128)(2,1)S(1)}, u32[]{:S(2)}, u32[]{:S(2)}) collective-permute-start(bf16[5,144,128]{2,1,0:T(8,128)(2,1)S(1)} %bitcast_dynamic-update-slice_fusion), channel_id=1, source_target_pairs={{1,0},{2,1},{3,2},{4,3},{5,4},{6,5},{7,6},{8,7},{9,8},{10,9},{11,1... | collective-permute-start | bytes 552968 | tf_op jit(solution)/shard_map/ppermute | solution.py:257
  23.4 6.1 %collective-permute-start.6 = (bf16[3,144,128]{2,1,0:T(8,128)(2,1)S(1)}, bf16[3,144,128]{2,1,0:T(8,128)(2,1)S(1)}, u32[]{:S(2)}, u32[]{:S(2)}) collective-permute-start(bf16[3,144,128]{2,1,0:T(8,128)(2,1)S(1)} %pad_maximum_fusion.1), channel_id=1, source_target_pairs={{0,2},{1,3},{2,4},{3,5},{4,6},{5,7},{6,8},{7,9},{8,10},{9,11},{10,... | collective-permute-start | bytes 331784 | tf_op jit(solution)/shard_map/ppermute | solution.py:257
  26.6 12.7 %collective-permute-start.7 = (bf16[3,144,128]{2,1,0:T(8,128)(2,1)S(1)}, bf16[3,144,128]{2,1,0:T(8,128)(2,1)S(1)}, u32[]{:S(2)}, u32[]{:S(2)}) collective-permute-start(bf16[3,144,128]{2,1,0:T(8,128)(2,1)S(1)} %pad_maximum_fusion.1), channel_id=1, source_target_pairs={{2,0},{3,1},{4,2},{5,3},{6,4},{7,5},{8,6},{9,7},{10,8},{11,9},{12,... | collective-permute-start | bytes 331784 | tf_op jit(solution)/shard_map/ppermute | solution.py:257
  39.3 0.8 copy-start.1
  48.2 12.4 %copy-start.2 = (bf16[144,128]{1,0:T(8,128)(2,1)S(1)}, bf16[144,128]{1,0:T(8,128)(2,1)}, u32[]{:S(2)}) copy-start(bf16[144,128]{1,0:T(8,128)(2,1)} %pack_slots.1.refs_2_) | copy-start | bytes 110596
  48.6 20.4 %collective-permute-start.8 = (bf16[6,2,128,128]{3,2,1,0:T(8,128)(2,1)S(1)}, bf16[6,2,128,128]{3,2,1,0:T(8,128)(2,1)S(1)}, u32[]{:S(2)}, u32[]{:S(2)}) collective-permute-start(bf16[6,2,128,128]{3,2,1,0:T(8,128)(2,1)S(1)} %get-tuple-element.8), channel_id=1, source_target_pairs={{0,1},{1,2},{2,3},{3,4},{4,5},{5,6},{6,7},{7,8},{8,9},{9,10},{10,1... | collective-permute-start | bytes 1179656 | tf_op jit(solution)/shard_map/ppermute | solution.py:257
  57.7 19.0 %collective-permute-start.9 = (bf16[6,2,128,128]{3,2,1,0:T(8,128)(2,1)S(1)}, bf16[6,2,128,128]{3,2,1,0:T(8,128)(2,1)S(1)}, u32[]{:S(2)}, u32[]{:S(2)}) collective-permute-start(bf16[6,2,128,128]{3,2,1,0:T(8,128)(2,1)S(1)} %get-tuple-element.5), channel_id=1, source_target_pairs={{1,0},{2,1},{3,2},{4,3},{5,4},{6,5},{7,6},{8,7},{9,8},{10,9},{11,1... | collective-permute-start | bytes 1179656 | tf_op jit(solution)/shard_map/ppermute | solution.py:257
  68.8 7.9 %copy-start = (bf16[8,8,64,128]{3,2,1,0:T(8,128)(2,1)S(1)}, bf16[8,8,64,128]{3,2,1,0:T(8,128)(2,1)}, u32[]{:S(2)}) copy-start(bf16[8,8,64,128]{3,2,1,0:T(8,128)(2,1)} %ens_ref.1) | copy-start | bytes 3145732
where the time goes:
time: 84 us; the launch traced here: 83.4 us
  starting transfers between devices  34.7 us (41%)
  Pallas kernels  24.4 us (29%)
  waiting for transfers between devices  20.5 us (24%)
  local copies, waits for them, and re-layouts  1.96 us (2%)
  other arithmetic  1.04 us (1%)
    ppermute x10, starting transfers between devices, shifted(): return lax.ppermute(block, axis, pairs)  34.7 us
    ppermute x10, waiting for transfers between devices, shifted(): return lax.ppermute(block, axis, pairs)  20.5 us
    pallas_call x2, Pallas kernels, transforms(): pl.pallas_call(functools.partial(points_kernel, points, batch), out_shape...  16.3 us
    pallas_call x1, Pallas kernels, apply(): pl.pallas_call(apply_kernel, out_shape=jax.ShapeDtypeStruct(ensemble.shap...  6.67 us
  transfers between devices with their start and end apart: 10, of which 4 were waited for; matrix products, arithmetic and copies ran while one was open for 2% of the time, Pallas kernels for 10%

commit v1 on v0

v1 whole, which is shorter than its diff:
```python
import functools

import jax
import jax.numpy as jnp
from jax import lax
from jax.experimental import pallas as pl
from jax.experimental.pallas import tpu as pltpu
from jax.sharding import PartitionSpec as P

K = 128
APX = 4
CT = 8
SPACING = 2
RLOC = 12
NHALF = 32
ROWS = K + 16
VMEM = 50 << 20

NT = (((1,), (1,)), ((), ()))
NN = (((1,), (0,)), ((), ()))
F32 = jnp.float32
BF16 = jnp.bfloat16

POINTS = [(a, b) for b in range(APX) for a in range(-1, APX + 1)]
FIRST = APX + 2


def center(a):
    return SPACING * a + (SPACING - 1) / 2.0


def least_distance(offset, point):
    return min(abs(offset * CT + s - center(point)) for s in range(CT))


def tiles_of(point, rows):
    a, b = point
    return [
        (ox, oy)
        for oy in rows
        for ox in range(-2, 3)
        if least_distance(ox, a) ** 2 + least_distance(oy, b) ** 2 < RLOC * RLOC
    ]


def split(x):
    hi = x.astype(BF16)
    lo = (x - hi.astype(F32)).astype(BF16)
    return hi, lo


def mm(a, b):
    left = jnp.concatenate([a[0], a[1]], 1)
    right = jnp.concatenate([b[0], b[1]], 1)
    right = jnp.concatenate([right, right], 0)
    out = lax.dot_general(left, right, NN, preferred_element_type=F32)
    return out[:, :K] + out[:, K:]


C0, C1, C2, C3, C4 = 2.25, -2.4375, 1.6875, -0.5625, 0.0625


def two_steps(xs, parts, eye):
    n = range(len(xs))
    sq = [mm(parts[i], parts[i]) for i in n]
    high = [mm(split(sq[i]), split(C3 * xs[i] + C4 * sq[i])) for i in n]
    return [C0 * eye + C1 * xs[i] + C2 * sq[i] + high[i] for i in n]


def four_steps(xs, eye):
    n = range(len(xs))
    x_parts = [split(x) for x in xs]
    z = two_steps(xs, x_parts, eye)
    z_parts = [split(v) for v in z]
    z_sq = [mm(z_parts[i], z_parts[i]) for i in n]
    m = [mm(x_parts[i], split(z_sq[i])) for i in n]
    q = two_steps(m, [split(v) for v in m], eye)
    return [mm(z_parts[i], split(q[i])) for i in n]


def pack_kernel(count_ref, anom_ref, innov_ref, prec_ref, pos_ref, out_ref):
    out_ref[0:K, :] = anom_ref[...].astype(F32).T.astype(BF16)
    slot = lax.broadcasted_iota(jnp.int32, (1, K), 1)
    live = jnp.where(slot < count_ref[0, 0], prec_ref[...].astype(F32), 0.0)
    meta = jnp.concatenate(
        [innov_ref[...].astype(F32), live, pos_ref[...].astype(F32), jnp.zeros((12, K), F32)], 0
    )
    out_ref[K:ROWS, :] = meta.astype(BF16)


def padded(n):
    return (n + 7) // 8 * 8


def point_weights(meta, frame_ref, ox, oy, points):
    rows = padded(len(points))
    at = lax.broadcasted_iota(jnp.int32, (rows, K), 0)
    px = jnp.zeros((rows, K), F32)
    py = px
    for i, (a, b) in enumerate(points):
        px = jnp.where(at == i, center(a), px)
        py = jnp.where(at == i, center(b), py)
    rx = frame_ref[0].astype(F32)
    ry = frame_ref[1].astype(F32)
    x = meta[2:3] * (1.0 - 2.0 * rx) + (CT - 1.0) * rx
    y = meta[3:4] * (1.0 - 2.0 * ry) + (CT - 1.0) * ry
    dx = (x + float(ox * CT)) - px
    dy = (y + float(oy * CT)) - py
    sq = dx * dx + dy * dy
    inside = sq < float(RLOC * RLOC)
    out = []
    for rate in (2.0, 4.5):
        out.append(jnp.where(inside, jnp.exp(-sq * (rate / (RLOC * RLOC))), 0.0) * meta[1:2])
    return out


def add_up(points, rows, block, frame_ref, sw_ref, wp_ref, s_ref, put_gram, put_pull):
    seen = sorted({t for p in points for t in tiles_of(p, rows)})
    place = {t: i for i, t in enumerate(seen)}
    n = padded(len(points))
    for t in seen:
        meta = block(t)[K:ROWS, :].astype(F32)
        w = point_weights(meta, frame_ref, t[0], t[1], points)
        lanes = slice(place[t] * K, place[t] * K + K)
        for g in range(2):
            sw_ref[place[t], g * n : g * n + n, :] = jnp.sqrt(w[g])
        hi, lo = split(jnp.concatenate(w, 0) * meta[0:1])
        wp_ref[0 : 2 * n, lanes] = hi
        wp_ref[2 * n : 4 * n, lanes] = lo
    anom_seen = jnp.concatenate([block(t)[0:K, :] for t in seen], 1)
    pull = lax.dot_general(anom_seen, wp_ref[...], NT, preferred_element_type=F32)
    put_pull(pull[:, 0 : 2 * n] + pull[:, 2 * n : 4 * n])
    for i, p in enumerate(points):
        own = tiles_of(p, rows)
        for j, t in enumerate(own):
            anom = block(t)[0:K, :].astype(F32)
            for g in range(2):
                scale = sw_ref[place[t], g * n + i : g * n + i + 1, :]
                s_ref[i % 2, g, :, j * K : j * K + K] = (anom * scale).astype(BF16)
        for g in range(2):
            s = s_ref[i % 2, g, :, 0 : len(own) * K]
            put_gram(i, g, lax.dot_general(s, s, NT, preferred_element_type=F32))


def sum_scratch(points, rows):
    n = padded(len(points))
    seen = len({t for p in points for t in tiles_of(p, rows)})
    most = max(len(tiles_of(p, rows)) for p in points)
    return [
        pltpu.VMEM((seen, 2 * n, K), F32),
        pltpu.VMEM((4 * n, seen * K), BF16),
        pltpu.VMEM((2, 2, K, most * K), BF16),
    ]


def near_kernel(frame_ref, pair_ref, a_ref, b_ref, ta_ref, tb_ref, first_ref, rest_ref, pull_ref, *scratch):
    def block(t):
        ox, oy = t
        if ox <= 0:
            return (pair_ref, ta_ref, tb_ref)[-ox].at[oy if ox == 0 else 1 - oy]
        return (a_ref, b_ref)[ox - 1].at[oy]

    def put_gram(i, g, value):
        if i < FIRST:
            first_ref[2 * i + g] = value
        else:
            rest_ref[2 * (i - FIRST) + g] = value

    def put_pull(value):
        pull_ref[...] = value

    add_up(POINTS, (0, 1), block, frame_ref, *scratch, put_gram, put_pull)


def points_kernel(points, rows, batch, frame_ref, y_ref, z_ref, gram_ref, pull_in_ref, out_ref, sw, wp, s, g_ref, pull_ref):
    n = padded(len(points))
    skip = POINTS.index(points[0])

    def block(t):
        ox, oy = t
        if oy == -1:
            return y_ref.at[2 - ox]
        if oy == -2:
            return y_ref.at[6 - ox]
        return z_ref.at[2 + ox]

    def put_gram(i, g, value):
        g_ref[2 * i + g] = value

    def put_pull(value):
        pull_ref[...] = value

    add_up(points, rows, block, frame_ref, sw, wp, s, put_gram, put_pull)
    row = lax.broadcasted_iota(jnp.int32, (K, K), 0)
    col = lax.broadcasted_iota(jnp.int32, (K, K), 1)
    eye = jnp.where(row == col, 1.0, 0.0).astype(F32)
    total = 2 * len(points)
    for start in range(0, total, batch):
        ids = range(start, min(start + batch, total))
        xs, norms = [], []
        for i in ids:
            system = eye + (gram_ref[i] + g_ref[i]) * (1.0 / (K - 1.0))
            sq = jnp.sum(jnp.sum(system * system, 0, keepdims=True), 1, keepdims=True)
            norm = jnp.sqrt(sq)
            norms.append(norm)
            xs.append(system * (1.0 / norm))
        zs = four_steps(xs, eye)
        for i, z, norm in zip(ids, zs, norms):
            p, g = i // 2, i % 2
            near = g * len(POINTS) + skip + p
            far = g * n + p
            pull = pull_in_ref[:, near : near + 1] + pull_ref[:, far : far + 1]
            inner = jnp.sum(z * pull, 0, keepdims=True)
            shift = jnp.sum(z * inner, 1, keepdims=True) * (1.0 / (norm * (K - 1.0)))
            out_ref[p, g] = (z * (1.0 / jnp.sqrt(norm)) + shift).astype(BF16)


def specs(n):
    return [pl.BlockSpec(memory_space=pltpu.SMEM)] + [pl.BlockSpec(memory_space=pltpu.VMEM)] * n


def near_sums(frame, *blocks):
    n = len(POINTS)
    return pl.pallas_call(
        near_kernel,
        out_shape=[
            jax.ShapeDtypeStruct((2 * FIRST, K, K), F32),
            jax.ShapeDtypeStruct((2 * (n - FIRST), K, K), F32),
            jax.ShapeDtypeStruct((K, 2 * n), F32),
        ],
        in_specs=specs(len(blocks)),
        scratch_shapes=sum_scratch(POINTS, (0, 1)),
        compiler_params=pltpu.CompilerParams(vmem_limit_bytes=VMEM),
        cost_estimate=pl.CostEstimate(flops=6_000_000_000, bytes_accessed=5_000_000, transcendentals=0),
        name="near_sums",
    )(frame, *blocks)


def transforms(points, rows, batch, frame, y, z, gram, pull, name):
    n = len(points)
    return pl.pallas_call(
        functools.partial(points_kernel, points, rows, batch),
        out_shape=jax.ShapeDtypeStruct((n, 2, K, K), BF16),
        in_specs=specs(4),
        scratch_shapes=sum_scratch(points, rows)
        + [pltpu.VMEM((2 * n, K, K), F32), pltpu.VMEM((K, 2 * padded(n)), F32)],
        compiler_params=pltpu.CompilerParams(vmem_limit_bytes=VMEM),
        cost_estimate=pl.CostEstimate(flops=n * 700_000_000, bytes_accessed=4_000_000, transcendentals=0),
        name=name,
    )(frame, y, z, gram, pull)


def apply_kernel(frame_ref, ens_ref, first_ref, rest_ref, low_ref, high_ref, out_ref, rim_ref):
    side = APX + 2
    rx, ry = frame_ref[0], frame_ref[1]

    @pl.when(frame_ref[2] != 0)
    def _():
        for x in range(side):
            rim_ref[x] = first_ref[x]

    @pl.when(frame_ref[2] == 0)
    def _():
        for x in range(side):
            rim_ref[x] = low_ref[side - 1 - x]

    def transform(x, y, g):
        if y == 0:
            return rim_ref[x, g]
        if y == 1:
            return first_ref[x, g]
        if y == APX + 1:
            return high_ref[side - 1 - x, g]
        return rest_ref[(y - 2) * side + x, g]

    ones = jnp.ones((K, K), BF16)
    frac = [(s + 0.5) / SPACING for s in range(SPACING)]
    corner = [[1.0 - f for f in frac], frac]
    for q in range(APX + 1):
        for p in range(APX + 1):
            cells = [
                (s, t)
                for s in range(2)
                for t in range(2)
                if 0 <= 2 * q - 1 + s < CT and 0 <= 2 * p - 1 + t < CT
            ]
            at = []
            for s, t in cells:
                i, j = 2 * q - 1 + s, 2 * p - 1 + t
                at.append((i + rx * (CT - 1 - 2 * i), j + ry * (CT - 1 - 2 * j)))
            ens = jnp.concatenate([ens_ref[i, j] for i, j in at], 0)
            mean = lax.dot_general(ens, ones, NN, preferred_element_type=F32) * (1.0 / K)
            anom = (ens.astype(F32) - mean).astype(BF16)
            for g in range(2):
                spans = [
                    slice(c * 2 * NHALF + g * NHALF, c * 2 * NHALF + (g + 1) * NHALF)
                    for c in range(len(cells))
                ]
                left = jnp.concatenate([anom[sp] for sp in spans], 0)
                adds = [None] * len(cells)
                for cx in range(2):
                    for cy in range(2):
                        prod = lax.dot_general(
                            left, transform(q + cx, p + cy, g), NN, preferred_element_type=F32
                        )
                        for c, (s, t) in enumerate(cells):
                            term = prod[c * NHALF : (c + 1) * NHALF] * (corner[cx][s] * corner[cy][t])
                            adds[c] = term if adds[c] is None else adds[c] + term
                for c, (i, j) in enumerate(at):
                    out_ref[i, j, g * NHALF : (g + 1) * NHALF, :] = (mean[spans[c]] + adds[c]).astype(BF16)


def apply(frame, ensemble, first, rest, low, high):
    return pl.pallas_call(
        apply_kernel,
        out_shape=jax.ShapeDtypeStruct(ensemble.shape, BF16),
        in_specs=specs(5),
        scratch_shapes=[pltpu.VMEM((APX + 2, 2, K, K), BF16)],
        compiler_params=pltpu.CompilerParams(vmem_limit_bytes=VMEM),
        name="apply_transforms",
    )(frame, ensemble, first, rest, low, high)


def moved(block, source, sizes):
    nx, ny = sizes
    pairs = []
    for x in range(nx):
        for y in range(ny):
            at = source(x, y)
            if at is not None:
                pairs.append((at[0] % nx * ny + at[1], x * ny + y))
    return lax.ppermute(block, ("gx", "gy"), pairs)


def shards(ensemble, obs_anom, obs_innov, obs_prec, obs_pos, obs_count):
    sizes = (lax.axis_size("gx"), lax.axis_size("gy"))

    def core(x, y):
        return x, y ^ 1

    def side(distance):
        return lambda x, y: (x + distance * (1 - 2 * ((x ^ y) & 1)), y)

    def beyond(x, y):
        at = y + 2 * (y & 1) - 1
        return (x, at) if 0 <= at < sizes[1] else None

    own = pl.pallas_call(
        pack_kernel,
        out_shape=jax.ShapeDtypeStruct((ROWS, K), BF16),
        in_specs=specs(4),
        name="pack_slots",
    )(
        obs_count,
        obs_anom.reshape(K, K),
        obs_innov.reshape(1, K),
        obs_prec.reshape(1, K),
        obs_pos.reshape(2, K),
    )
    col, row = lax.axis_index("gx"), lax.axis_index("gy")
    ry = row & 1
    rx = (col ^ row) & 1
    edge = jnp.where((row == 0) | (row == sizes[1] - 1), 1, 0)
    frame = jnp.stack([rx, ry, edge]).astype(jnp.int32)

    pair = jnp.stack([own, moved(own, core, sizes)])
    a = moved(pair, side(1), sizes)
    b = moved(pair, side(2), sizes)
    ta = moved(a, core, sizes)
    tb = moved(b, core, sizes)
    wide = jnp.stack([tb[1], ta[1], pair[0], a[0], b[0], ta[0], pair[1], a[1]])
    y = moved(wide, beyond, sizes)
    gram_first, gram_rest, pull = near_sums(frame, pair, a, b, ta, tb)
    first = transforms(POINTS[:FIRST], (-2, -1), 12, frame, y, y, gram_first, pull, "first_points")
    low = moved(first, beyond, sizes)
    z = moved(y, core, sizes)
    rest = transforms(POINTS[FIRST:], (-2, -1, 2), 12, frame, y, z, gram_rest, pull, "rest_points")
    high = moved(rest[-FIRST:], core, sizes)
    return apply(frame, ensemble, first, rest, low, high)


def solution(mesh):
    placed = (
        P("gx", "gy", None, None),
        P("gx", "gy", None, None),
        P("gx", "gy", None),
        P("gx", "gy", None),
        P("gx", "gy", None, None),
        P("gx", "gy"),
    )
    return jax.shard_map(
        shards, mesh=mesh, in_specs=placed, out_specs=P("gx", "gy", None, None), check_vma=False
    )
```

time: 84 us -> 64.3 us (0.77)
  the two profiles are of different devices: /device:TPU:95 before, /device:TPU:57 now
where the time goes in v1:
time: 64.3 us; the launch traced here: 64 us
  Pallas kernels  27.6 us (43%)
  starting transfers between devices  21.7 us (34%)
  waiting for transfers between devices  10.8 us (17%)
  local copies, waits for them, and re-layouts  2.28 us (4%)
  other arithmetic  0.85 us (1%)
  between operations  0.76 us (1%)
    ppermute x9, starting transfers between devices, moved(): return lax.ppermute(block, ('gx', 'gy'), pairs)  21.7 us
    pallas_call x2, Pallas kernels, transforms(): pl.pallas_call(functools.partial(points_kernel, points, rows, batch), out...  14.6 us
    ppermute x9, waiting for transfers between devices, moved(): return lax.ppermute(block, ('gx', 'gy'), pairs)  10.8 us
    pallas_call x1, Pallas kernels, apply(): pl.pallas_call(apply_kernel, out_shape=jax.ShapeDtypeStruct(ensemble.shap...  6.86 us
    pallas_call x1, Pallas kernels, near_sums(): pl.pallas_call(near_kernel, out_shape=[jax.ShapeDtypeStruct((2 * FIRST, K...  4.63 us
    unnamed x11, local copies, waits for them, and re-layouts  2.24 us
    pallas_call x1, Pallas kernels, shards(): pl.pallas_call(pack_kernel, out_shape=jax.ShapeDtypeStruct((ROWS, K), BF1...  1.5 us
  transfers between devices with their start and end apart: 9, of which 6 were waited for; matrix products, arithmetic and copies ran while one was open for 0% of the time, Pallas kernels for 30%

profile of v1, /device:TPU:57, one launch (start us, length us, event | category | flops | bytes accessed | tf_op | source)
XLA Modules:
  0.0 64.0 jit_solution(485179444861158113)
XLA Ops:
  0.7 1.5 %pack_slots.1 = bf16[144,128]{1,0:T(8,128)(2,1)} custom-call(s32[1,1]{1,0:T(1,128)S(6)} %copy.14.count_ref, bf16[128,128]{1,0:T(8,128)(2,1)} %bitcast.13, bf16[1,128]{1,0:T(2,128)(2,1)} %bitcast.15, bf16[1,128]{1,0:T(2,128)(2,1)} %bitcast.16, s32[2,128]{1,0:T(2,128)} %bitcast.14), custom_call_target="tpu_custom_call" | custom-call | tf_op jit(solution)/shard_map/pack_slots/pallas_call | solution.py:348
  2.1 0.7 %collective-permute-start = (bf16[144,128]{1,0:T(8,128)(2,1)}, bf16[144,128]{1,0:T(8,128)(2,1)S(1)}, u32[]{:S(2)}, u32[]{:S(2)}) collective-permute-start(bf16[144,128]{1,0:T(8,128)(2,1)} %pack_slots.1), channel_id=1, source_target_pairs={{1,0},{0,1},{3,2},{2,3},{5,4},{4,5},{7,6},{6,7},{9,8},{8,9},{11,10... | collective-permute-start | bytes 110600 | tf_op jit(solution)/shard_map/ppermute | solution.py:332
  2.8 1.1 %collective-permute-done = bf16[144,128]{1,0:T(8,128)(2,1)S(1)} collective-permute-done((bf16[144,128]{1,0:T(8,128)(2,1)}, bf16[144,128]{1,0:T(8,128)(2,1)S(1)}, u32[]{:S(2)}, u32[]{:S(2)}) %collective-permute-start) | collective-permute-done | bytes 36896 | tf_op jit(solution)/shard_map/ppermute | solution.py:332
  3.9 0.8 %pad_maximum_fusion.pair_ref = bf16[2,144,128]{2,1,0:T(8,128)(2,1)S(1)} fusion(bf16[1,144,128]{2,1,0:T(8,128)(2,1)S(1)} %bitcast.12, bf16[1,144,128]{2,1,0:T(8,128)(2,1)} %bitcast.11), kind=kLoop, calls=%fused_computation | loop fusion | flops 36864 | bytes 147456 | tf_op jit(solution)/shard_map/stack | solution.py:366
  4.7 5.2 %collective-permute-start.1 = (bf16[2,144,128]{2,1,0:T(8,128)(2,1)S(1)}, bf16[2,144,128]{2,1,0:T(8,128)(2,1)S(1)}, u32[]{:S(2)}, u32[]{:S(2)}) collective-permute-start(bf16[2,144,128]{2,1,0:T(8,128)(2,1)S(1)} %pad_maximum_fusion.pair_ref), channel_id=1, source_target_pairs={{32,0},{225,1},{34,2},{227,3},{36,4},{229,5},{38,6},{231,7},{40,8}... | collective-permute-start | bytes 221192 | tf_op jit(solution)/shard_map/ppermute | solution.py:332
  9.9 0.0 collective-permute-start.3
  9.9 2.5 %collective-permute-done.1.b_ref = bf16[2,144,128]{2,1,0:T(8,128)(2,1)S(1)} collective-permute-done((bf16[2,144,128]{2,1,0:T(8,128)(2,1)S(1)}, bf16[2,144,128]{2,1,0:T(8,128)(2,1)S(1)}, u32[]{:S(2)}, u32[]{:S(2)}) %collective-permute-start.1) | collective-permute-done | bytes 73760 | tf_op jit(solution)/shard_map/ppermute | solution.py:332
  12.4 0.8 %collective-permute-start.2 = (bf16[2,144,128]{2,1,0:T(8,128)(2,1)S(1)}, bf16[2,144,128]{2,1,0:T(8,128)(2,1)S(1)}, u32[]{:S(2)}, u32[]{:S(2)}) collective-permute-start(bf16[2,144,128]{2,1,0:T(8,128)(2,1)S(1)} %collective-permute-done.1.b_ref), channel_id=1, source_target_pairs={{1,0},{0,1},{3,2},{2,3},{5,4},{4,5},{7,6},{6,7},{9,8},{8,9},{11,10... | collective-permute-start | bytes 221192 | tf_op jit(solution)/shard_map/ppermute | solution.py:332
  13.2 0.1 pad_add_fusion.frame_ref
  13.3 0.3 collective-permute-done.3.a_ref
  13.5 1.0 %collective-permute-start.4 = (bf16[2,144,128]{2,1,0:T(8,128)(2,1)S(1)}, bf16[2,144,128]{2,1,0:T(8,128)(2,1)S(1)}, u32[]{:S(2)}, u32[]{:S(2)}) collective-permute-start(bf16[2,144,128]{2,1,0:T(8,128)(2,1)S(1)} %collective-permute-done.3.a_ref), channel_id=1, source_target_pairs={{1,0},{0,1},{3,2},{2,3},{5,4},{4,5},{7,6},{6,7},{9,8},{8,9},{11,10... | collective-permute-start | bytes 221192 | tf_op jit(solution)/shard_map/ppermute | solution.py:332
  14.6 0.0 collective-permute-done.2.tb_ref
  14.6 0.9 %collective-permute-done.4.ta_ref = bf16[2,144,128]{2,1,0:T(8,128)(2,1)S(1)} collective-permute-done((bf16[2,144,128]{2,1,0:T(8,128)(2,1)S(1)}, bf16[2,144,128]{2,1,0:T(8,128)(2,1)S(1)}, u32[]{:S(2)}, u32[]{:S(2)}) %collective-permute-start.4) | collective-permute-done | bytes 73760 | tf_op jit(solution)/shard_map/ppermute | solution.py:332
  15.5 0.8 %constant_dynamic-update-slice_fusion.1 = bf16[8,144,128]{2,1,0:T(8,128)(2,1)S(1)} fusion(bf16[8,144,128]{2,1,0:T(8,128)(2,1)S(1)} %slice_dynamic-update-slice_fusion.4, bf16[144,128]{1,0:T(8,128)(2,1)} %pack_slots.1), kind=kLoop, calls=%fused_computation.8 | loop fusion | bytes 73728
  16.3 6.9 %collective-permute-start.5 = (bf16[8,144,128]{2,1,0:T(8,128)(2,1)S(1)}, bf16[8,144,128]{2,1,0:T(8,128)(2,1)S(1)}, u32[]{:S(2)}, u32[]{:S(2)}) collective-permute-start(bf16[8,144,128]{2,1,0:T(8,128)(2,1)S(1)} %slice_dynamic-update-slice_fusion), channel_id=1, source_target_pairs={{2,1},{1,2},{4,3},{3,4},{6,5},{5,6},{8,7},{7,8},{10,9},{9,10},{12,... | collective-permute-start | bytes 884744 | tf_op jit(solution)/shard_map/ppermute | solution.py:332
  23.2 4.6 %near_sums.1 = (f32[12,128,128]{2,1,0:T(8,128)S(1)}, f32[36,128,128]{2,1,0:T(8,128)S(1)}, f32[128,48]{1,0:T(8,128)S(1)}) custom-call(s32[3]{0:T(128)S(1)} %pad_add_fusion.frame_ref, bf16[2,144,128]{2,1,0:T(8,128)(2,1)S(1)} %pad_maximum_fusion.pair_ref, bf16[2,144,128]{2,1,0:T(8,128)(2,1)S(1)} %collective-permute-done.3.a_ref, ...), custom_call_target="tpu_custom_call" | custom-call | flops 6000000000 | bytes 5000000 | tf_op jit(solution)/shard_map/near_sums/pallas_call | solution.py:224
  27.8 0.0 copy-start.1
  27.9 1.4 %copy-done.1 = f32[36,128,128]{2,1,0:T(8,128)} copy-done((f32[36,128,128]{2,1,0:T(8,128)}, f32[36,128,128]{2,1,0:T(8,128)S(1)}, u32[]{:S(2)}) %copy-start.1) | copy-done | bytes 2359320
  29.3 4.3 %collective-permute-done.5.y_ref.z_ref = bf16[8,144,128]{2,1,0:T(8,128)(2,1)S(1)} collective-permute-done((bf16[8,144,128]{2,1,0:T(8,128)(2,1)S(1)}, bf16[8,144,128]{2,1,0:T(8,128)(2,1)S(1)}, u32[]{:S(2)}, u32[]{:S(2)}) %collective-permute-start.5) | collective-permute-done | bytes 294944 | tf_op jit(solution)/shard_map/ppermute | solution.py:332
  33.5 0.0 collective-permute-start.6
  33.6 3.8 %first_points.1.first_ref = bf16[6,2,128,128]{3,2,1,0:T(8,128)(2,1)S(1)} custom-call(s32[3]{0:T(128)S(1)} %pad_add_fusion.frame_ref, bf16[8,144,128]{2,1,0:T(8,128)(2,1)S(1)} %collective-permute-done.5.y_ref.z_ref, bf16[8,144,128]{2,1,0:T(8,128)(2,1)S(1)} %collective-permute-done.5.y_ref.z_ref, f32[12,128,128]{2,1,0:T(8,128)S(1)} %get-tuple-element.8.gram_ref, ...), custom_call_target="tpu_custom_call" | custom-call | flops 4200000000 | bytes 4000000 | tf_op jit(solution)/shard_map/first_points/pallas_call | solution.py:241
  37.4 7.0 %collective-permute-start.7 = (bf16[6,2,128,128]{3,2,1,0:T(8,128)(2,1)S(1)}, bf16[6,2,128,128]{3,2,1,0:T(8,128)(2,1)S(1)}, u32[]{:S(2)}, u32[]{:S(2)}) collective-permute-start(bf16[6,2,128,128]{3,2,1,0:T(8,128)(2,1)S(1)} %first_points.1.first_ref), channel_id=1, source_target_pairs={{2,1},{1,2},{4,3},{3,4},{6,5},{5,6},{8,7},{7,8},{10,9},{9,10},{12,... | collective-permute-start | bytes 1179656 | tf_op jit(solution)/shard_map/ppermute | solution.py:332
  44.4 0.0 collective-permute-done.6.z_ref
  44.5 0.0 copy-start
  44.5 10.8 %rest_points.1.rest_ref = bf16[18,2,128,128]{3,2,1,0:T(8,128)(2,1)S(1)} custom-call(s32[3]{0:T(128)S(1)} %pad_add_fusion.frame_ref, bf16[8,144,128]{2,1,0:T(8,128)(2,1)S(1)} %collective-permute-done.5.y_ref.z_ref, bf16[8,144,128]{2,1,0:T(8,128)(2,1)S(1)} %collective-permute-done.6.z_ref, f32[36,128,128]{2,1,0:T(8,128)} %copy-done.1, ...), custom_call_target="tpu_custom_call" | custom-call | flops 12600000512 | bytes 4000000 | tf_op jit(solution)/shard_map/rest_points/pallas_call | solution.py:241
  55.3 0.1 collective-permute-start.8
  55.4 0.0 collective-permute-done.7.low_ref
  55.4 1.7 %collective-permute-done.8.high_ref = bf16[6,2,128,128]{3,2,1,0:T(8,128)(2,1)S(1)} collective-permute-done((bf16[6,2,128,128]{3,2,1,0:T(8,128)(2,1)S(1)}, bf16[6,2,128,128]{3,2,1,0:T(8,128)(2,1)S(1)}, u32[]{:S(2)}, u32[]{:S(2)}) %collective-permute-start.8) | collective-permute-done | bytes 393248 | tf_op jit(solution)/shard_map/ppermute | solution.py:332
  57.1 0.0 copy-done
  57.1 6.9 %apply_transforms.1 = bf16[8,8,64,128]{3,2,1,0:T(8,128)(2,1)} custom-call(s32[3]{0:T(128)S(1)} %pad_add_fusion.frame_ref, bf16[8,8,64,128]{3,2,1,0:T(8,128)(2,1)S(1)} %copy-done, bf16[6,2,128,128]{3,2,1,0:T(8,128)(2,1)S(1)} %first_points.1.first_ref, bf16[18,2,128,128]{3,2,1,0:T(8,128)(2,1)S(1)} %rest_points.1.rest_ref, ...), custom_call_target="tpu_custom_call" | custom-call | tf_op jit(solution)/shard_map/apply_transforms/pallas_call | solution.py:314
  (8 shorter events, 0.1 us)
Async XLA Ops:
  2.1 1.8 %collective-permute-start = (bf16[144,128]{1,0:T(8,128)(2,1)}, bf16[144,128]{1,0:T(8,128)(2,1)S(1)}, u32[]{:S(2)}, u32[]{:S(2)}) collective-permute-start(bf16[144,128]{1,0:T(8,128)(2,1)} %pack_slots.1), channel_id=1, source_target_pairs={{1,0},{0,1},{3,2},{2,3},{5,4},{4,5},{7,6},{6,7},{9,8},{8,9},{11,10... | collective-permute-start | bytes 110600 | tf_op jit(solution)/shard_map/ppermute | solution.py:332
  4.7 7.7 %collective-permute-start.1 = (bf16[2,144,128]{2,1,0:T(8,128)(2,1)S(1)}, bf16[2,144,128]{2,1,0:T(8,128)(2,1)S(1)}, u32[]{:S(2)}, u32[]{:S(2)}) collective-permute-start(bf16[2,144,128]{2,1,0:T(8,128)(2,1)S(1)} %pad_maximum_fusion.pair_ref), channel_id=1, source_target_pairs={{32,0},{225,1},{34,2},{227,3},{36,4},{229,5},{38,6},{231,7},{40,8}... | collective-permute-start | bytes 221192 | tf_op jit(solution)/shard_map/ppermute | solution.py:332
  9.9 3.7 %collective-permute-start.3 = (bf16[2,144,128]{2,1,0:T(8,128)(2,1)S(1)}, bf16[2,144,128]{2,1,0:T(8,128)(2,1)S(1)}, u32[]{:S(2)}, u32[]{:S(2)}) collective-permute-start(bf16[2,144,128]{2,1,0:T(8,128)(2,1)S(1)} %pad_maximum_fusion.pair_ref), channel_id=1, source_target_pairs={{16,0},{241,1},{18,2},{243,3},{20,4},{245,5},{22,6},{247,7},{24,8}... | collective-permute-start | bytes 221192 | tf_op jit(solution)/shard_map/ppermute | solution.py:332
  12.4 2.2 %collective-permute-start.2 = (bf16[2,144,128]{2,1,0:T(8,128)(2,1)S(1)}, bf16[2,144,128]{2,1,0:T(8,128)(2,1)S(1)}, u32[]{:S(2)}, u32[]{:S(2)}) collective-permute-start(bf16[2,144,128]{2,1,0:T(8,128)(2,1)S(1)} %collective-permute-done.1.b_ref), channel_id=1, source_target_pairs={{1,0},{0,1},{3,2},{2,3},{5,4},{4,5},{7,6},{6,7},{9,8},{8,9},{11,10... | collective-permute-start | bytes 221192 | tf_op jit(solution)/shard_map/ppermute | solution.py:332
  13.5 1.9 %collective-permute-start.4 = (bf16[2,144,128]{2,1,0:T(8,128)(2,1)S(1)}, bf16[2,144,128]{2,1,0:T(8,128)(2,1)S(1)}, u32[]{:S(2)}, u32[]{:S(2)}) collective-permute-start(bf16[2,144,128]{2,1,0:T(8,128)(2,1)S(1)} %collective-permute-done.3.a_ref), channel_id=1, source_target_pairs={{1,0},{0,1},{3,2},{2,3},{5,4},{4,5},{7,6},{6,7},{9,8},{8,9},{11,10... | collective-permute-start | bytes 221192 | tf_op jit(solution)/shard_map/ppermute | solution.py:332
  16.3 17.2 %collective-permute-start.5 = (bf16[8,144,128]{2,1,0:T(8,128)(2,1)S(1)}, bf16[8,144,128]{2,1,0:T(8,128)(2,1)S(1)}, u32[]{:S(2)}, u32[]{:S(2)}) collective-permute-start(bf16[8,144,128]{2,1,0:T(8,128)(2,1)S(1)} %slice_dynamic-update-slice_fusion), channel_id=1, source_target_pairs={{2,1},{1,2},{4,3},{3,4},{6,5},{5,6},{8,7},{7,8},{10,9},{9,10},{12,... | collective-permute-start | bytes 884744 | tf_op jit(solution)/shard_map/ppermute | solution.py:332
  27.8 1.4 %copy-start.1 = (f32[36,128,128]{2,1,0:T(8,128)}, f32[36,128,128]{2,1,0:T(8,128)S(1)}, u32[]{:S(2)}) copy-start(f32[36,128,128]{2,1,0:T(8,128)S(1)} %get-tuple-element.10.gram_ref) | copy-start | bytes 7077892
  33.5 10.9 %collective-permute-start.6 = (bf16[8,144,128]{2,1,0:T(8,128)(2,1)S(1)}, bf16[8,144,128]{2,1,0:T(8,128)(2,1)S(1)}, u32[]{:S(2)}, u32[]{:S(2)}) collective-permute-start(bf16[8,144,128]{2,1,0:T(8,128)(2,1)S(1)} %collective-permute-done.5.y_ref.z_ref), channel_id=1, source_target_pairs={{1,0},{0,1},{3,2},{2,3},{5,4},{4,5},{7,6},{6,7},{9,8},{8,9},{11,10... | collective-permute-start | bytes 884744 | tf_op jit(solution)/shard_map/ppermute | solution.py:332
  37.4 18.0 %collective-permute-start.7 = (bf16[6,2,128,128]{3,2,1,0:T(8,128)(2,1)S(1)}, bf16[6,2,128,128]{3,2,1,0:T(8,128)(2,1)S(1)}, u32[]{:S(2)}, u32[]{:S(2)}) collective-permute-start(bf16[6,2,128,128]{3,2,1,0:T(8,128)(2,1)S(1)} %first_points.1.first_ref), channel_id=1, source_target_pairs={{2,1},{1,2},{4,3},{3,4},{6,5},{5,6},{8,7},{7,8},{10,9},{9,10},{12,... | collective-permute-start | bytes 1179656 | tf_op jit(solution)/shard_map/ppermute | solution.py:332
  44.5 12.7 %copy-start = (bf16[8,8,64,128]{3,2,1,0:T(8,128)(2,1)S(1)}, bf16[8,8,64,128]{3,2,1,0:T(8,128)(2,1)}, u32[]{:S(2)}) copy-start(bf16[8,8,64,128]{3,2,1,0:T(8,128)(2,1)} %ens_ref.1) | copy-start | bytes 3145732
  55.3 1.8 %collective-permute-start.8 = (bf16[6,2,128,128]{3,2,1,0:T(8,128)(2,1)S(1)}, bf16[6,2,128,128]{3,2,1,0:T(8,128)(2,1)S(1)}, u32[]{:S(2)}, u32[]{:S(2)}) collective-permute-start(bf16[6,2,128,128]{3,2,1,0:T(8,128)(2,1)S(1)} %slice.34), channel_id=1, source_target_pairs={{1,0},{0,1},{3,2},{2,3},{5,4},{4,5},{7,6},{6,7},{9,8},{8,9},{11,10... | collective-permute-start | bytes 1179656 | tf_op jit(solution)/shard_map/ppermute | solution.py:332

commit v2 on v1

v2 whole, which is shorter than its diff:
```python
import functools

import jax
import jax.numpy as jnp
from jax import lax
from jax.experimental import pallas as pl
from jax.experimental.pallas import tpu as pltpu
from jax.sharding import PartitionSpec as P

K = 128
APX = 4
CT = 8
SPACING = 2
RLOC = 12
NHALF = 32
META = 4
ROWS = K + 16
PAIR = 2 * K + 16
WIDE = 10 * K + 48

NT = (((1,), (1,)), ((), ()))
NN = (((1,), (0,)), ((), ()))
F32 = jnp.float32
BF16 = jnp.bfloat16

SIDE = APX + 2
POINTS = [(a, b) for b in range(-1, APX) for a in range(-1, APX + 1)]
FIRST = 3 * SIDE


def center(a):
    return SPACING * a + (SPACING - 1) / 2.0


def least_distance(offset, point):
    return min(abs(offset * CT + s - center(point)) for s in range(CT))


def tiles_of(point, rows):
    a, b = point
    return [
        (ox, oy)
        for oy in rows
        for ox in range(-2, 3)
        if least_distance(ox, a) ** 2 + least_distance(oy, b) ** 2 < RLOC * RLOC
    ]


def split(x):
    hi = x.astype(BF16)
    lo = (x - hi.astype(F32)).astype(BF16)
    return hi, lo


def mm(a, b):
    left = jnp.concatenate([a[0], a[1]], 1)
    right = jnp.concatenate([b[0], b[1]], 1)
    right = jnp.concatenate([right, right], 0)
    out = lax.dot_general(left, right, NN, preferred_element_type=F32)
    return out[:, :K] + out[:, K:]


C0, C1, C2, C3, C4 = 2.25, -2.4375, 1.6875, -0.5625, 0.0625


def two_steps(xs, parts, eye):
    n = range(len(xs))
    sq = [mm(parts[i], parts[i]) for i in n]
    high = [mm(split(sq[i]), split(C3 * xs[i] + C4 * sq[i])) for i in n]
    return [C0 * eye + C1 * xs[i] + C2 * sq[i] + high[i] for i in n]


def four_steps(xs, eye):
    n = range(len(xs))
    x_parts = [split(x) for x in xs]
    z = two_steps(xs, x_parts, eye)
    z_parts = [split(v) for v in z]
    z_sq = [mm(z_parts[i], z_parts[i]) for i in n]
    m = [mm(x_parts[i], split(z_sq[i])) for i in n]
    q = two_steps(m, [split(v) for v in m], eye)
    return [mm(z_parts[i], split(q[i])) for i in n]


def pack_kernel(count_ref, anom_ref, innov_ref, prec_ref, pos_ref, out_ref):
    out_ref[0:K, :] = anom_ref[...].astype(F32).T.astype(BF16)
    slot = lax.broadcasted_iota(jnp.int32, (1, K), 1)
    live = jnp.where(slot < count_ref[0, 0], prec_ref[...].astype(F32), 0.0)
    meta = jnp.concatenate(
        [innov_ref[...].astype(F32), live, pos_ref[...].astype(F32), jnp.zeros((12, K), F32)], 0
    )
    out_ref[K:ROWS, :] = meta.astype(BF16)


def pair_kernel(own_ref, other_ref, out_ref):
    out_ref[0:K, :] = own_ref[0:K, :]
    out_ref[K : 2 * K, :] = other_ref[0:K, :]
    meta = [ref[K:ROWS, :].astype(F32)[0:META] for ref in (own_ref, other_ref)]
    out_ref[2 * K : PAIR, :] = jnp.concatenate(meta + [jnp.zeros((8, K), F32)], 0).astype(BF16)


def wide_kernel(pair_ref, a_ref, b_ref, ta_ref, tb_ref, out_ref):
    parts = [(tb_ref, 1), (ta_ref, 1), (pair_ref, 0), (a_ref, 0), (b_ref, 0)]
    parts += [(tb_ref, 0), (ta_ref, 0), (pair_ref, 1), (a_ref, 1), (b_ref, 1)]
    meta = []
    for k, (ref, row) in enumerate(parts):
        out_ref[k * K : k * K + K, :] = ref[row * K : row * K + K, :]
        meta.append(ref[2 * K : PAIR, :].astype(F32)[row * META : row * META + META])
    meta.append(jnp.zeros((8, K), F32))
    out_ref[10 * K : WIDE, :] = jnp.concatenate(meta, 0).astype(BF16)


def padded(n):
    return (n + 7) // 8 * 8


def point_weights(meta, frame_ref, ox, oy, points):
    rows = padded(len(points))
    at = lax.broadcasted_iota(jnp.int32, (rows, K), 0)
    px = jnp.zeros((rows, K), F32)
    py = px
    for i, (a, b) in enumerate(points):
        px = jnp.where(at == i, center(a), px)
        py = jnp.where(at == i, center(b), py)
    rx = frame_ref[0].astype(F32)
    ry = frame_ref[1].astype(F32)
    x = meta[2:3] * (1.0 - 2.0 * rx) + (CT - 1.0) * rx
    y = meta[3:4] * (1.0 - 2.0 * ry) + (CT - 1.0) * ry
    dx = (x + float(ox * CT)) - px
    dy = (y + float(oy * CT)) - py
    sq = dx * dx + dy * dy
    inside = sq < float(RLOC * RLOC)
    out = []
    for rate in (2.0, 4.5):
        out.append(jnp.where(inside, jnp.exp(-sq * (rate / (RLOC * RLOC))), 0.0) * meta[1:2])
    return out


def add_up(points, rows, block, frame_ref, sw_ref, wp_ref, s_ref, put_gram, put_pull):
    seen = sorted({t for p in points for t in tiles_of(p, rows)})
    place = {t: i for i, t in enumerate(seen)}
    n = padded(len(points))

    def anom(t):
        ref, k = block(t)
        return ref[k * K : k * K + K, :]

    metas = {}
    for t in seen:
        ref, k = block(t)
        if id(ref) not in metas:
            metas[id(ref)] = ref[10 * K : WIDE, :].astype(F32)
        meta = metas[id(ref)][k * META : k * META + META]
        w = point_weights(meta, frame_ref, t[0], t[1], points)
        lanes = slice(place[t] * K, place[t] * K + K)
        for g in range(2):
            sw_ref[place[t], g * n : g * n + n, :] = jnp.sqrt(w[g])
        hi, lo = split(jnp.concatenate(w, 0) * meta[0:1])
        wp_ref[0 : 2 * n, lanes] = hi
        wp_ref[2 * n : 4 * n, lanes] = lo
    anom_seen = jnp.concatenate([anom(t) for t in seen], 1)
    pull = lax.dot_general(anom_seen, wp_ref[...], NT, preferred_element_type=F32)
    put_pull(pull[:, 0 : 2 * n] + pull[:, 2 * n : 4 * n])
    for i, p in enumerate(points):
        own = tiles_of(p, rows)
        for j, t in enumerate(own):
            rows_in = anom(t).astype(F32)
            for g in range(2):
                scale = sw_ref[place[t], g * n + i : g * n + i + 1, :]
                s_ref[i % 2, g, :, j * K : j * K + K] = (rows_in * scale).astype(BF16)
        for g in range(2):
            s = s_ref[i % 2, g, :, 0 : len(own) * K]
            put_gram(i, g, lax.dot_general(s, s, NT, preferred_element_type=F32))


def sum_scratch(points, rows):
    n = padded(len(points))
    seen = len({t for p in points for t in tiles_of(p, rows)})
    most = max(len(tiles_of(p, rows)) for p in points)
    return [
        pltpu.VMEM((seen, 2 * n, K), F32),
        pltpu.VMEM((4 * n, seen * K), BF16),
        pltpu.VMEM((2, 2, K, most * K), BF16),
    ]


def near_kernel(frame_ref, wide_ref, first_ref, rest_ref, pull_ref, *scratch):
    def block(t):
        return wide_ref, 5 * t[1] + 2 + t[0]

    def put_gram(i, g, value):
        if i < FIRST:
            first_ref[2 * i + g] = value
        else:
            rest_ref[2 * (i - FIRST) + g] = value

    def put_pull(value):
        pull_ref[...] = value

    add_up(POINTS, (0, 1), block, frame_ref, *scratch, put_gram, put_pull)


def points_kernel(points, rows, batch, *refs):
    frame_ref, y_ref = refs[0:2]
    z_ref = refs[2] if 2 in rows else None
    gram_ref, pull_in_ref, out_ref, sw, wp, s, g_ref, pull_ref = refs[-8:]
    n = padded(len(points))
    skip = POINTS.index(points[0])

    def block(t):
        ox, oy = t
        if oy == 2:
            return z_ref, 2 + ox
        return y_ref, (2 if oy == -1 else 7) - ox

    def put_gram(i, g, value):
        g_ref[2 * i + g] = gram_ref[2 * i + g] + value

    def put_pull(value):
        pull_ref[...] = value

    add_up(points, rows, block, frame_ref, sw, wp, s, put_gram, put_pull)
    row = lax.broadcasted_iota(jnp.int32, (K, K), 0)
    col = lax.broadcasted_iota(jnp.int32, (K, K), 1)
    eye = jnp.where(row == col, 1.0, 0.0).astype(F32)
    total = 2 * len(points)
    for start in range(0, total, batch):
        ids = range(start, min(start + batch, total))
        xs, norms = [], []
        for i in ids:
            system = eye + g_ref[i] * (1.0 / (K - 1.0))
            sq = jnp.sum(jnp.sum(system * system, 0, keepdims=True), 1, keepdims=True)
            norm = jnp.sqrt(sq)
            norms.append(norm)
            xs.append(system * (1.0 / norm))
        zs = four_steps(xs, eye)
        for i, z, norm in zip(ids, zs, norms):
            p, g = i // 2, i % 2
            near = g * padded(len(POINTS)) + skip + p
            far = g * n + p
            pull = pull_in_ref[:, near : near + 1] + pull_ref[:, far : far + 1]
            inner = jnp.sum(z * pull, 0, keepdims=True)
            shift = jnp.sum(z * inner, 1, keepdims=True) * (1.0 / (norm * (K - 1.0)))
            out_ref[p, g] = (z * (1.0 / jnp.sqrt(norm)) + shift).astype(BF16)


def specs(n, scalars=1):
    return [pl.BlockSpec(memory_space=pltpu.SMEM)] * scalars + [pl.BlockSpec(memory_space=pltpu.VMEM)] * n


def joined(kernel, rows, name, *blocks):
    return pl.pallas_call(
        kernel,
        out_shape=jax.ShapeDtypeStruct((rows, K), BF16),
        in_specs=specs(len(blocks), 0),
        name=name,
    )(*blocks)


def near_sums(frame, wide):
    n = len(POINTS)
    return pl.pallas_call(
        near_kernel,
        out_shape=[
            jax.ShapeDtypeStruct((2 * FIRST, K, K), F32),
            jax.ShapeDtypeStruct((2 * (n - FIRST), K, K), F32),
            jax.ShapeDtypeStruct((K, 2 * padded(n)), F32),
        ],
        in_specs=specs(1),
        scratch_shapes=sum_scratch(POINTS, (0, 1)),
        compiler_params=pltpu.CompilerParams(vmem_limit_bytes=16 << 20),
        cost_estimate=pl.CostEstimate(flops=6_000_000_000, bytes_accessed=5_000_000, transcendentals=0),
        name="near_sums",
    )(frame, wide)


def transforms(points, rows, batch, name, frame, *arrays):
    n = len(points)
    return pl.pallas_call(
        functools.partial(points_kernel, points, rows, batch),
        out_shape=jax.ShapeDtypeStruct((n, 2, K, K), BF16),
        in_specs=specs(len(arrays)),
        scratch_shapes=sum_scratch(points, rows)
        + [pltpu.VMEM((2 * n, K, K), F32), pltpu.VMEM((K, 2 * padded(n)), F32)],
        compiler_params=pltpu.CompilerParams(vmem_limit_bytes=28 << 20),
        cost_estimate=pl.CostEstimate(flops=n * 500_000_000, bytes_accessed=4_000_000, transcendentals=0),
        name=name,
    )(frame, *arrays)


def anomalies_kernel(ens_ref, anom_ref, mean_ref):
    ones = jnp.ones((K, K), BF16)
    rows = CT * 2 * NHALF
    for i in range(CT):
        ens = ens_ref[i].reshape(rows, K)
        mean = lax.dot_general(ens, ones, NN, preferred_element_type=F32) * (1.0 / K)
        anom_ref[i] = (ens.astype(F32) - mean).astype(BF16).reshape(CT, 2 * NHALF, K)
        mean_ref[i] = mean.reshape(CT, 2 * NHALF, K)


def anomalies(ensemble):
    return pl.pallas_call(
        anomalies_kernel,
        out_shape=[
            jax.ShapeDtypeStruct(ensemble.shape, BF16),
            jax.ShapeDtypeStruct(ensemble.shape, F32),
        ],
        in_specs=specs(1, 0),
        compiler_params=pltpu.CompilerParams(vmem_limit_bytes=12 << 20),
        cost_estimate=pl.CostEstimate(flops=1_000_000_000, bytes_accessed=4_000_000, transcendentals=0),
        name="anomalies",
    )(ensemble)


def apply_kernel(frame_ref, anom_ref, mean_ref, first_ref, rest_ref, high_ref, out_ref):
    rx, ry, edge = frame_ref[0], frame_ref[1], frame_ref[2]

    def transform(x, y, g):
        if y == 0:
            return first_ref[x + edge * SIDE, g]
        if y < 3:
            return first_ref[y * SIDE + x, g]
        if y <= APX:
            return rest_ref[(y - 3) * SIDE + x, g]
        return high_ref[SIDE - 1 - x, g]

    frac = [(s + 0.5) / SPACING for s in range(SPACING)]
    corner = [[1.0 - f for f in frac], frac]
    for p in range(APX + 1):
        for q in range(APX + 1):
            cells = []
            for s in range(2):
                for t in range(2):
                    i, j = 2 * q - 1 + s, 2 * p - 1 + t
                    if 0 <= i < CT and 0 <= j < CT:
                        cells.append((s, t, i + rx * (CT - 1 - 2 * i), j + ry * (CT - 1 - 2 * j)))
            for g in range(2):
                span = slice(g * NHALF, (g + 1) * NHALF)
                left = jnp.concatenate([anom_ref[i, j, span, :] for _, _, i, j in cells], 0)
                sums = [mean_ref[i, j, span, :] for _, _, i, j in cells]
                for cx in range(2):
                    both = jnp.concatenate([transform(q + cx, p + cy, g) for cy in range(2)], 1)
                    prod = lax.dot_general(left, both, NN, preferred_element_type=F32)
                    for cy in range(2):
                        for c, (s, t, _, _) in enumerate(cells):
                            part = prod[c * NHALF : (c + 1) * NHALF, cy * K : (cy + 1) * K]
                            sums[c] = sums[c] + part * (corner[cx][s] * corner[cy][t])
                for total, (_, _, i, j) in zip(sums, cells):
                    out_ref[i, j, span, :] = total.astype(BF16)


def apply(frame, anom, mean, first, rest, high):
    return pl.pallas_call(
        apply_kernel,
        out_shape=jax.ShapeDtypeStruct(anom.shape, BF16),
        in_specs=specs(5),
        compiler_params=pltpu.CompilerParams(vmem_limit_bytes=16 << 20),
        name="apply_transforms",
    )(frame, anom, mean, first, rest, high)


def moved(block, source, sizes):
    nx, ny = sizes
    pairs = []
    for x in range(nx):
        for y in range(ny):
            at = source(x, y)
            if at is not None:
                pairs.append((at[0] % nx * ny + at[1], x * ny + y))
    return lax.ppermute(block, ("gx", "gy"), pairs)


def shards(ensemble, obs_anom, obs_innov, obs_prec, obs_pos, obs_count):
    sizes = (lax.axis_size("gx"), lax.axis_size("gy"))

    def core(x, y):
        return x, y ^ 1

    def side(distance):
        return lambda x, y: (x + distance * (1 - 2 * ((x ^ y) & 1)), y)

    def beyond(x, y):
        at = y + 2 * (y & 1) - 1
        return (x, at) if 0 <= at < sizes[1] else None

    own = pl.pallas_call(
        pack_kernel,
        out_shape=jax.ShapeDtypeStruct((ROWS, K), BF16),
        in_specs=specs(4),
        name="pack_slots",
    )(
        obs_count,
        obs_anom.reshape(K, K),
        obs_innov.reshape(1, K),
        obs_prec.reshape(1, K),
        obs_pos.reshape(2, K),
    )
    col, row = lax.axis_index("gx"), lax.axis_index("gy")
    edge = jnp.where((row == 0) | (row == sizes[1] - 1), 1, 0)
    frame = jnp.stack([(col ^ row) & 1, row & 1, edge]).astype(jnp.int32)

    pair = joined(pair_kernel, PAIR, "pair_tiles", own, moved(own, core, sizes))
    a = moved(pair, side(1), sizes)
    b = moved(pair, side(2), sizes)
    ta = moved(a, core, sizes)
    tb = moved(b, core, sizes)
    wide = joined(wide_kernel, WIDE, "two_rows", pair, a, b, ta, tb)
    y = moved(wide, beyond, sizes)
    anom, mean = anomalies(ensemble)
    gram_first, gram_rest, pull = near_sums(frame, wide)
    y, pull = lax.optimization_barrier((y, pull))
    z = moved(y, core, sizes)
    first = transforms(POINTS[:FIRST], (-2, -1), 12, "first_points", frame, y, gram_first, pull)
    rest = transforms(POINTS[FIRST:], (-1, 2), 12, "rest_points", frame, y, z, gram_rest, pull)
    high = moved(rest[-SIDE:], core, sizes)
    return apply(frame, anom, mean, first, rest, high)


def solution(mesh):
    placed = (
        P("gx", "gy", None, None),
        P("gx", "gy", None, None),
        P("gx", "gy", None),
        P("gx", "gy", None),
        P("gx", "gy", None, None),
        P("gx", "gy"),
    )
    return jax.shard_map(
        shards, mesh=mesh, in_specs=placed, out_specs=P("gx", "gy", None, None), check_vma=False
    )
```

time: 64.3 us -> 59.1 us (0.919)
  the two profiles are of different devices: /device:TPU:57 before, /device:TPU:25 now
where the time goes in v2:
time: 59.1 us; the launch traced here: 58.5 us
  Pallas kernels  29.6 us (50%)
  starting transfers between devices  14 us (24%)
  waiting for transfers between devices  11.8 us (20%)
  local copies, waits for them, and re-layouts  2.26 us (4%)
  between operations  0.73 us (1%)
    pallas_call x2, Pallas kernels, transforms(): pl.pallas_call(functools.partial(points_kernel, points, rows, batch), out...  16.1 us
    ppermute x8, starting transfers between devices, moved(): return lax.ppermute(block, ('gx', 'gy'), pairs)  14 us
    ppermute x8, waiting for transfers between devices, moved(): return lax.ppermute(block, ('gx', 'gy'), pairs)  11.8 us
    pallas_call x1, Pallas kernels, near_sums(): pl.pallas_call(near_kernel, out_shape=[jax.ShapeDtypeStruct((2 * FIRST, K...  5.52 us
    pallas_call x2, Pallas kernels, joined(): pl.pallas_call(kernel, out_shape=jax.ShapeDtypeStruct((rows, K), BF16), i...  3.2 us
    pallas_call x1, Pallas kernels, apply(): pl.pallas_call(apply_kernel, out_shape=jax.ShapeDtypeStruct(anom.shape, B...  2.87 us
    unnamed x14, local copies, waits for them, and re-layouts  2.23 us
    pallas_call x1, Pallas kernels, shards(): pl.pallas_call(pack_kernel, out_shape=jax.ShapeDtypeStruct((ROWS, K), BF1...  1.5 us
  transfers between devices with their start and end apart: 8, of which 6 were waited for; matrix products, arithmetic and copies ran while one was open for 0% of the time, Pallas kernels for 26%

profile of v2, /device:TPU:25, one launch (start us, length us, event | category | flops | bytes accessed | tf_op | source)
XLA Modules:
  0.0 58.5 jit_solution(16106038470982585239)
XLA Ops:
  0.7 1.5 %pack_slots.1.own_ref = bf16[144,128]{1,0:T(8,128)(2,1)} custom-call(s32[1,1]{1,0:T(1,128)S(6)} %copy.7.count_ref, bf16[128,128]{1,0:T(8,128)(2,1)} %bitcast.7, bf16[1,128]{1,0:T(2,128)(2,1)} %bitcast.9, bf16[1,128]{1,0:T(2,128)(2,1)} %bitcast.10, s32[2,128]{1,0:T(2,128)} %bitcast.8), custom_call_target="tpu_custom_call" | custom-call | tf_op jit(solution)/shard_map/pack_slots/pallas_call | solution.py:385
  2.1 0.7 %collective-permute-start = (bf16[144,128]{1,0:T(8,128)(2,1)}, bf16[144,128]{1,0:T(8,128)(2,1)S(1)}, u32[]{:S(2)}, u32[]{:S(2)}) collective-permute-start(bf16[144,128]{1,0:T(8,128)(2,1)} %pack_slots.1.own_ref), channel_id=1, source_target_pairs={{1,0},{0,1},{3,2},{2,3},{5,4},{4,5},{7,6},{6,7},{9,8},{8,9},{11,10... | collective-permute-start | bytes 110600 | tf_op jit(solution)/shard_map/ppermute | solution.py:369
  2.8 1.1 %collective-permute-done.other_ref = bf16[144,128]{1,0:T(8,128)(2,1)S(1)} collective-permute-done((bf16[144,128]{1,0:T(8,128)(2,1)}, bf16[144,128]{1,0:T(8,128)(2,1)S(1)}, u32[]{:S(2)}, u32[]{:S(2)}) %collective-permute-start) | collective-permute-done | bytes 36896 | tf_op jit(solution)/shard_map/ppermute | solution.py:369
  3.9 0.6 %copy-done.6 = bf16[144,128]{1,0:T(8,128)(2,1)} copy-done((bf16[144,128]{1,0:T(8,128)(2,1)}, bf16[144,128]{1,0:T(8,128)(2,1)S(1)}, u32[]{:S(2)}) %copy-start.6) | copy-done | bytes 36888
  4.5 1.4 %pair_tiles.1.pair_ref = bf16[272,128]{1,0:T(8,128)(2,1)} custom-call(bf16[144,128]{1,0:T(8,128)(2,1)} %pack_slots.1.own_ref, bf16[144,128]{1,0:T(8,128)(2,1)} %copy-done.6), custom_call_target="tpu_custom_call" | custom-call | tf_op jit(solution)/shard_map/pair_tiles/pallas_call | solution.py:251
  5.9 6.5 %collective-permute-start.1 = (bf16[272,128]{1,0:T(8,128)(2,1)}, bf16[272,128]{1,0:T(8,128)(2,1)S(1)}, u32[]{:S(2)}, u32[]{:S(2)}) collective-permute-start(bf16[272,128]{1,0:T(8,128)(2,1)} %pair_tiles.1.pair_ref), channel_id=1, source_target_pairs={{16,0},{241,1},{18,2},{243,3},{20,4},{245,5},{22,6},{247,7},{24,8}... | collective-permute-start | bytes 208904 | tf_op jit(solution)/shard_map/ppermute | solution.py:369
  12.5 0.0 collective-permute-start.2
  12.5 2.1 %collective-permute-done.1.a_ref = bf16[272,128]{1,0:T(8,128)(2,1)S(1)} collective-permute-done((bf16[272,128]{1,0:T(8,128)(2,1)}, bf16[272,128]{1,0:T(8,128)(2,1)S(1)}, u32[]{:S(2)}, u32[]{:S(2)}) %collective-permute-start.1) | collective-permute-done | bytes 69664 | tf_op jit(solution)/shard_map/ppermute | solution.py:369
  14.6 0.0 collective-permute-start.3
  14.6 4.3 %collective-permute-done.2.b_ref = bf16[272,128]{1,0:T(8,128)(2,1)S(1)} collective-permute-done((bf16[272,128]{1,0:T(8,128)(2,1)}, bf16[272,128]{1,0:T(8,128)(2,1)S(1)}, u32[]{:S(2)}, u32[]{:S(2)}) %collective-permute-start.2) | collective-permute-done | bytes 69664 | tf_op jit(solution)/shard_map/ppermute | solution.py:369
  18.9 0.0 collective-permute-start.4
  18.9 0.1 pad_add_fusion.frame_ref.refs_0_
  18.9 0.0 collective-permute-done.3.ta_ref
  18.9 1.2 %collective-permute-done.4.tb_ref = bf16[272,128]{1,0:T(8,128)(2,1)S(1)} collective-permute-done((bf16[272,128]{1,0:T(8,128)(2,1)S(1)}, bf16[272,128]{1,0:T(8,128)(2,1)S(1)}, u32[]{:S(2)}, u32[]{:S(2)}) %collective-permute-start.4) | collective-permute-done | bytes 69664 | tf_op jit(solution)/shard_map/ppermute | solution.py:369
  20.1 0.0 copy-done.2
  20.1 0.0 copy-done.3
  20.1 0.0 copy-done.4
  20.1 0.6 %copy-done.5 = bf16[272,128]{1,0:T(8,128)(2,1)} copy-done((bf16[272,128]{1,0:T(8,128)(2,1)}, bf16[272,128]{1,0:T(8,128)(2,1)S(1)}, u32[]{:S(2)}) %copy-start.5) | copy-done | bytes 69656
  20.8 1.8 %two_rows.1.wide_ref = bf16[1328,128]{1,0:T(8,128)(2,1)} custom-call(bf16[272,128]{1,0:T(8,128)(2,1)} %pair_tiles.1.pair_ref, bf16[272,128]{1,0:T(8,128)(2,1)} %copy-done.2, bf16[272,128]{1,0:T(8,128)(2,1)} %copy-done.3, bf16[272,128]{1,0:T(8,128)(2,1)} %copy-done.4, bf16[272,128]{1,0:T(8,128)(2,1)} %copy-done.5), custom_call_target="tpu_custom_call" | custom-call | tf_op jit(solution)/shard_map/two_rows/pallas_call | solution.py:251
  22.5 6.4 %collective-permute-start.5 = (bf16[1328,128]{1,0:T(8,128)(2,1)}, bf16[1328,128]{1,0:T(8,128)(2,1)S(1)}, u32[]{:S(2)}, u32[]{:S(2)}) collective-permute-start(bf16[1328,128]{1,0:T(8,128)(2,1)} %two_rows.1.wide_ref), channel_id=1, source_target_pairs={{2,1},{1,2},{4,3},{3,4},{6,5},{5,6},{8,7},{7,8},{10,9},{9,10},{12,... | collective-permute-start | bytes 1019912 | tf_op jit(solution)/shard_map/ppermute | solution.py:369
  28.9 0.0 copy-start
  28.9 1.0 %copy-done = bf16[1328,128]{1,0:T(8,128)(2,1)S(1)} copy-done((bf16[1328,128]{1,0:T(8,128)(2,1)S(1)}, bf16[1328,128]{1,0:T(8,128)(2,1)}, u32[]{:S(2)}) %copy-start) | copy-done | bytes 339992
  29.9 5.5 %near_sums.1 = (f32[36,128,128]{2,1,0:T(8,128)S(1)}, f32[24,128,128]{2,1,0:T(8,128)S(1)}, f32[128,64]{1,0:T(8,128)S(1)}) custom-call(s32[3]{0:T(128)S(1)} %pad_add_fusion.frame_ref.refs_0_, bf16[1328,128]{1,0:T(8,128)(2,1)S(1)} %copy-done), custom_call_target="tpu_custom_call" | custom-call | flops 6000000000 | bytes 5000000 | tf_op jit(solution)/shard_map/near_sums/pallas_call | solution.py:261
  35.4 2.0 %collective-permute-done.5.refs_1_ = bf16[1328,128]{1,0:T(8,128)(2,1)S(1)} collective-permute-done((bf16[1328,128]{1,0:T(8,128)(2,1)}, bf16[1328,128]{1,0:T(8,128)(2,1)S(1)}, u32[]{:S(2)}, u32[]{:S(2)}) %collective-permute-start.5) | collective-permute-done | bytes 340000 | tf_op jit(solution)/shard_map/ppermute | solution.py:369
  37.4 0.0 collective-permute-start.6
  37.4 0.4 anomalies.1
  37.8 1.2 %collective-permute-done.6.refs_2_ = bf16[1328,128]{1,0:T(8,128)(2,1)S(1)} collective-permute-done((bf16[1328,128]{1,0:T(8,128)(2,1)S(1)}, bf16[1328,128]{1,0:T(8,128)(2,1)S(1)}, u32[]{:S(2)}, u32[]{:S(2)}) %collective-permute-start.6) | collective-permute-done | bytes 340000 | tf_op jit(solution)/shard_map/ppermute | solution.py:369
  39.0 6.5 %rest_points.1.rest_ref = bf16[12,2,128,128]{3,2,1,0:T(8,128)(2,1)S(1)} custom-call(s32[3]{0:T(128)S(1)} %pad_add_fusion.frame_ref.refs_0_, bf16[1328,128]{1,0:T(8,128)(2,1)S(1)} %collective-permute-done.5.refs_1_, bf16[1328,128]{1,0:T(8,128)(2,1)S(1)} %collective-permute-done.6.refs_2_, f32[24,128,128]{2,1,0:T(8,128)S(1)} %get-tuple-element.18.refs_3_, ...), custom_call_target="tpu_custom_call" | custom-call | flops 6000000000 | bytes 4000000 | tf_op jit(solution)/shard_map/rest_points/pallas_call | solution.py:278
  45.6 0.4 collective-permute-start.7
  46.0 9.6 %first_points.1.first_ref = bf16[18,2,128,128]{3,2,1,0:T(8,128)(2,1)S(1)} custom-call(s32[3]{0:T(128)S(1)} %pad_add_fusion.frame_ref.refs_0_, bf16[1328,128]{1,0:T(8,128)(2,1)S(1)} %collective-permute-done.5.refs_1_, f32[36,128,128]{2,1,0:T(8,128)S(1)} %get-tuple-element.16.refs_2_, f32[128,64]{1,0:T(8,128)S(1)} %get-tuple-element.17.refs_3_.refs_4_), custom_call_target="tpu_custom_call" | custom-call | flops 8999999488 | bytes 4000000 | tf_op jit(solution)/shard_map/first_points/pallas_call | solution.py:278
  55.6 0.0 collective-permute-done.7.high_ref
  55.6 2.9 %apply_transforms.1 = bf16[8,8,64,128]{3,2,1,0:T(8,128)(2,1)} custom-call(s32[3]{0:T(128)S(1)} %pad_add_fusion.frame_ref.refs_0_, bf16[8,8,64,128]{3,2,1,0:T(8,128)(2,1)S(1)} %get-tuple-element.12.anom_ref, f32[8,8,64,128]{3,2,1,0:T(8,128)S(1)} %get-tuple-element.13.mean_ref, bf16[18,2,128,128]{3,2,1,0:T(8,128)(2,1)S(1)} %first_points.1.first_ref, ...), custom_call_target="tpu_custom_call" | custom-call | tf_op jit(solution)/shard_map/apply_transforms/pallas_call | solution.py:352
  (8 shorter events, 0.0 us)
Async XLA Ops:
  2.1 1.8 %collective-permute-start = (bf16[144,128]{1,0:T(8,128)(2,1)}, bf16[144,128]{1,0:T(8,128)(2,1)S(1)}, u32[]{:S(2)}, u32[]{:S(2)}) collective-permute-start(bf16[144,128]{1,0:T(8,128)(2,1)} %pack_slots.1.own_ref), channel_id=1, source_target_pairs={{1,0},{0,1},{3,2},{2,3},{5,4},{4,5},{7,6},{6,7},{9,8},{8,9},{11,10... | collective-permute-start | bytes 110600 | tf_op jit(solution)/shard_map/ppermute | solution.py:369
  3.9 0.6 %copy-start.6 = (bf16[144,128]{1,0:T(8,128)(2,1)}, bf16[144,128]{1,0:T(8,128)(2,1)S(1)}, u32[]{:S(2)}) copy-start(bf16[144,128]{1,0:T(8,128)(2,1)S(1)} %collective-permute-done.other_ref) | copy-start | bytes 110596
  5.9 8.6 %collective-permute-start.1 = (bf16[272,128]{1,0:T(8,128)(2,1)}, bf16[272,128]{1,0:T(8,128)(2,1)S(1)}, u32[]{:S(2)}, u32[]{:S(2)}) collective-permute-start(bf16[272,128]{1,0:T(8,128)(2,1)} %pair_tiles.1.pair_ref), channel_id=1, source_target_pairs={{16,0},{241,1},{18,2},{243,3},{20,4},{245,5},{22,6},{247,7},{24,8}... | collective-permute-start | bytes 208904 | tf_op jit(solution)/shard_map/ppermute | solution.py:369
  12.5 6.4 %collective-permute-start.2 = (bf16[272,128]{1,0:T(8,128)(2,1)}, bf16[272,128]{1,0:T(8,128)(2,1)S(1)}, u32[]{:S(2)}, u32[]{:S(2)}) collective-permute-start(bf16[272,128]{1,0:T(8,128)(2,1)} %pair_tiles.1.pair_ref), channel_id=1, source_target_pairs={{32,0},{225,1},{34,2},{227,3},{36,4},{229,5},{38,6},{231,7},{40,8}... | collective-permute-start | bytes 208904 | tf_op jit(solution)/shard_map/ppermute | solution.py:369
  14.6 5.6 %copy-start.2 = (bf16[272,128]{1,0:T(8,128)(2,1)}, bf16[272,128]{1,0:T(8,128)(2,1)S(1)}, u32[]{:S(2)}) copy-start(bf16[272,128]{1,0:T(8,128)(2,1)S(1)} %collective-permute-done.1.a_ref) | copy-start | bytes 208900
  14.6 4.4 %collective-permute-start.3 = (bf16[272,128]{1,0:T(8,128)(2,1)S(1)}, bf16[272,128]{1,0:T(8,128)(2,1)S(1)}, u32[]{:S(2)}, u32[]{:S(2)}) collective-permute-start(bf16[272,128]{1,0:T(8,128)(2,1)S(1)} %collective-permute-done.1.a_ref), channel_id=1, source_target_pairs={{1,0},{0,1},{3,2},{2,3},{5,4},{4,5},{7,6},{6,7},{9,8},{8,9},{11,10... | collective-permute-start | bytes 208904 | tf_op jit(solution)/shard_map/ppermute | solution.py:369
  18.9 1.3 %copy-start.3 = (bf16[272,128]{1,0:T(8,128)(2,1)}, bf16[272,128]{1,0:T(8,128)(2,1)S(1)}, u32[]{:S(2)}) copy-start(bf16[272,128]{1,0:T(8,128)(2,1)S(1)} %collective-permute-done.2.b_ref) | copy-start | bytes 208900
  18.9 1.3 %collective-permute-start.4 = (bf16[272,128]{1,0:T(8,128)(2,1)S(1)}, bf16[272,128]{1,0:T(8,128)(2,1)S(1)}, u32[]{:S(2)}, u32[]{:S(2)}) collective-permute-start(bf16[272,128]{1,0:T(8,128)(2,1)S(1)} %collective-permute-done.2.b_ref), channel_id=1, source_target_pairs={{1,0},{0,1},{3,2},{2,3},{5,4},{4,5},{7,6},{6,7},{9,8},{8,9},{11,10... | collective-permute-start | bytes 208904 | tf_op jit(solution)/shard_map/ppermute | solution.py:369
  18.9 1.2 %copy-start.4 = (bf16[272,128]{1,0:T(8,128)(2,1)}, bf16[272,128]{1,0:T(8,128)(2,1)S(1)}, u32[]{:S(2)}) copy-start(bf16[272,128]{1,0:T(8,128)(2,1)S(1)} %collective-permute-done.3.ta_ref) | copy-start | bytes 208900
  20.1 0.6 %copy-start.5 = (bf16[272,128]{1,0:T(8,128)(2,1)}, bf16[272,128]{1,0:T(8,128)(2,1)S(1)}, u32[]{:S(2)}) copy-start(bf16[272,128]{1,0:T(8,128)(2,1)S(1)} %collective-permute-done.4.tb_ref) | copy-start | bytes 208900
  22.5 14.8 %collective-permute-start.5 = (bf16[1328,128]{1,0:T(8,128)(2,1)}, bf16[1328,128]{1,0:T(8,128)(2,1)S(1)}, u32[]{:S(2)}, u32[]{:S(2)}) collective-permute-start(bf16[1328,128]{1,0:T(8,128)(2,1)} %two_rows.1.wide_ref), channel_id=1, source_target_pairs={{2,1},{1,2},{4,3},{3,4},{6,5},{5,6},{8,7},{7,8},{10,9},{9,10},{12,... | collective-permute-start | bytes 1019912 | tf_op jit(solution)/shard_map/ppermute | solution.py:369
  28.9 1.0 %copy-start = (bf16[1328,128]{1,0:T(8,128)(2,1)S(1)}, bf16[1328,128]{1,0:T(8,128)(2,1)}, u32[]{:S(2)}) copy-start(bf16[1328,128]{1,0:T(8,128)(2,1)} %two_rows.1.wide_ref) | copy-start | bytes 1019908
  29.9 7.5 %copy-start.1 = (bf16[8,8,64,128]{3,2,1,0:T(8,128)(2,1)S(1)}, bf16[8,8,64,128]{3,2,1,0:T(8,128)(2,1)}, u32[]{:S(2)}) copy-start(bf16[8,8,64,128]{3,2,1,0:T(8,128)(2,1)} %ens_ref.1) | copy-start | bytes 3145732
  37.4 1.6 %collective-permute-start.6 = (bf16[1328,128]{1,0:T(8,128)(2,1)S(1)}, bf16[1328,128]{1,0:T(8,128)(2,1)S(1)}, u32[]{:S(2)}, u32[]{:S(2)}) collective-permute-start(bf16[1328,128]{1,0:T(8,128)(2,1)S(1)} %collective-permute-done.5.refs_1_), channel_id=1, source_target_pairs={{1,0},{0,1},{3,2},{2,3},{5,4},{4,5},{7,6},{6,7},{9,8},{8,9},{11,10... | collective-permute-start | bytes 1019912 | tf_op jit(solution)/shard_map/ppermute | solution.py:369
  45.6 10.0 %collective-permute-start.7 = (bf16[6,2,128,128]{3,2,1,0:T(8,128)(2,1)S(1)}, bf16[6,2,128,128]{3,2,1,0:T(8,128)(2,1)S(1)}, u32[]{:S(2)}, u32[]{:S(2)}) collective-permute-start(bf16[6,2,128,128]{3,2,1,0:T(8,128)(2,1)S(1)} %slice.4), channel_id=1, source_target_pairs={{1,0},{0,1},{3,2},{2,3},{5,4},{4,5},{7,6},{6,7},{9,8},{8,9},{11,10... | collective-permute-start | bytes 1179656 | tf_op jit(solution)/shard_map/ppermute | solution.py:369

commit v3 on v2

--- a/solution.py
+++ b/solution.py
@@ -16,7 +16,9 @@
 META = 4
 ROWS = K + 16
 PAIR = 2 * K + 16
-WIDE = 10 * K + 48
+WIDE = 5 * K + 32
+SLOTS = 2
+LAG = 10
 
 NT = (((1,), (1,)), ((), ()))
 NN = (((1,), (0,)), ((), ()))
@@ -60,25 +62,15 @@
     return out[:, :K] + out[:, K:]
 
 
+def rounded(x):
+    return (x.astype(BF16),)
+
+
+def mm_high(a, b):
+    return lax.dot_general(a[0], b[0], NN, preferred_element_type=F32)
+
+
 C0, C1, C2, C3, C4 = 2.25, -2.4375, 1.6875, -0.5625, 0.0625
-
-
-def two_steps(xs, parts, eye):
-    n = range(len(xs))
-    sq = [mm(parts[i], parts[i]) for i in n]
-    high = [mm(split(sq[i]), split(C3 * xs[i] + C4 * sq[i])) for i in n]
-    return [C0 * eye + C1 * xs[i] + C2 * sq[i] + high[i] for i in n]
-
-
-def four_steps(xs, eye):
-    n = range(len(xs))
-    x_parts = [split(x) for x in xs]
-    z = two_steps(xs, x_parts, eye)
-    z_parts = [split(v) for v in z]
-    z_sq = [mm(z_parts[i], z_parts[i]) for i in n]
-    m = [mm(x_parts[i], split(z_sq[i])) for i in n]
-    q = two_steps(m, [split(v) for v in m], eye)
-    return [mm(z_parts[i], split(q[i])) for i in n]
 
 
 def pack_kernel(count_ref, anom_ref, innov_ref, prec_ref, pos_ref, out_ref):
@@ -98,15 +90,15 @@
     out_ref[2 * K : PAIR, :] = jnp.concatenate(meta + [jnp.zeros((8, K), F32)], 0).astype(BF16)
 
 
-def wide_kernel(pair_ref, a_ref, b_ref, ta_ref, tb_ref, out_ref):
-    parts = [(tb_ref, 1), (ta_ref, 1), (pair_ref, 0), (a_ref, 0), (b_ref, 0)]
-    parts += [(tb_ref, 0), (ta_ref, 0), (pair_ref, 1), (a_ref, 1), (b_ref, 1)]
-    meta = []
-    for k, (ref, row) in enumerate(parts):
-        out_ref[k * K : k * K + K, :] = ref[row * K : row * K + K, :]
-        meta.append(ref[2 * K : PAIR, :].astype(F32)[row * META : row * META + META])
-    meta.append(jnp.zeros((8, K), F32))
-    out_ref[10 * K : WIDE, :] = jnp.concatenate(meta, 0).astype(BF16)
+def rows_kernel(pair_ref, a_ref, b_ref, ta_ref, tb_ref, *out_refs):
+    for row, out_ref in enumerate(out_refs):
+        parts = [(tb_ref, 1 - row), (ta_ref, 1 - row), (pair_ref, row), (a_ref, row), (b_ref, row)]
+        meta = []
+        for k, (ref, at) in enumerate(parts):
+            out_ref[k * K : k * K + K, :] = ref[at * K : at * K + K, :]
+            meta.append(ref[2 * K : PAIR, :].astype(F32)[at * META : at * META + META])
+        meta.append(jnp.zeros((12, K), F32))
+        out_ref[5 * K : WIDE, :] = jnp.concatenate(meta, 0).astype(BF16)
 
 
 def padded(n):
@@ -148,7 +140,7 @@
     for t in seen:
         ref, k = block(t)
         if id(ref) not in metas:
-            metas[id(ref)] = ref[10 * K : WIDE, :].astype(F32)
+            metas[id(ref)] = ref[5 * K : WIDE, :].astype(F32)
         meta = metas[id(ref)][k * META : k * META + META]
         w = point_weights(meta, frame_ref, t[0], t[1], points)
         lanes = slice(place[t] * K, place[t] * K + K)
@@ -158,18 +150,21 @@
         wp_ref[0 : 2 * n, lanes] = hi
         wp_ref[2 * n : 4 * n, lanes] = lo
     anom_seen = jnp.concatenate([anom(t) for t in seen], 1)
-    pull = lax.dot_general(anom_seen, wp_ref[...], NT, preferred_element_type=F32)
-    put_pull(pull[:, 0 : 2 * n] + pull[:, 2 * n : 4 * n])
-    for i, p in enumerate(points):
-        own = tiles_of(p, rows)
+    pull = lax.dot_general(wp_ref[...], anom_seen, NT, preferred_element_type=F32)
+    put_pull(pull[0 : 2 * n] + pull[2 * n : 4 * n])
+
+    def add_point(i):
+        own = tiles_of(points[i], rows)
         for j, t in enumerate(own):
             rows_in = anom(t).astype(F32)
             for g in range(2):
                 scale = sw_ref[place[t], g * n + i : g * n + i + 1, :]
-                s_ref[i % 2, g, :, j * K : j * K + K] = (rows_in * scale).astype(BF16)
+                s_ref[i % SLOTS, g, :, j * K : j * K + K] = (rows_in * scale).astype(BF16)
         for g in range(2):
-            s = s_ref[i % 2, g, :, 0 : len(own) * K]
+            s = s_ref[i % SLOTS, g, :, 0 : len(own) * K]
             put_gram(i, g, lax.dot_general(s, s, NT, preferred_element_type=F32))
+
+    return add_point
 
 
 def sum_scratch(points, rows):
@@ -179,13 +174,13 @@
     return [
         pltpu.VMEM((seen, 2 * n, K), F32),
         pltpu.VMEM((4 * n, seen * K), BF16),
-        pltpu.VMEM((2, 2, K, most * K), BF16),
+        pltpu.VMEM((SLOTS, 2, K, most * K), BF16),
     ]
 
 
-def near_kernel(frame_ref, wide_ref, first_ref, rest_ref, pull_ref, *scratch):
+def near_kernel(frame_ref, own_ref, other_ref, first_ref, rest_ref, pull_ref, *scratch):
     def block(t):
-        return wide_ref, 5 * t[1] + 2 + t[0]
+        return (own_ref, other_ref)[t[1]], 2 + t[0]
 
     def put_gram(i, g, value):
         if i < FIRST:
@@ -196,21 +191,21 @@
     def put_pull(value):
         pull_ref[...] = value
 
-    add_up(POINTS, (0, 1), block, frame_ref, *scratch, put_gram, put_pull)
+    add_point = add_up(POINTS, (0, 1), block, frame_ref, *scratch, put_gram, put_pull)
+    for i in range(len(POINTS)):
+        add_point(i)
 
 
 def points_kernel(points, rows, batch, *refs):
-    frame_ref, y_ref = refs[0:2]
-    z_ref = refs[2] if 2 in rows else None
+    frame_ref = refs[0]
+    row_refs = dict(zip(rows, refs[1:]))
     gram_ref, pull_in_ref, out_ref, sw, wp, s, g_ref, pull_ref = refs[-8:]
     n = padded(len(points))
     skip = POINTS.index(points[0])
 
     def block(t):
         ox, oy = t
-        if oy == 2:
-            return z_ref, 2 + ox
-        return y_ref, (2 if oy == -1 else 7) - ox
+        return row_refs[oy], 2 + (ox if oy == 2 else -ox)
 
     def put_gram(i, g, value):
         g_ref[2 * i + g] = gram_ref[2 * i + g] + value
@@ -218,29 +213,78 @@
     def put_pull(value):
         pull_ref[...] = value
 
-    add_up(points, rows, block, frame_ref, sw, wp, s, put_gram, put_pull)
+    add_point = add_up(points, rows, block, frame_ref, sw, wp, s, put_gram, put_pull)
     row = lax.broadcasted_iota(jnp.int32, (K, K), 0)
     col = lax.broadcasted_iota(jnp.int32, (K, K), 1)
     eye = jnp.where(row == col, 1.0, 0.0).astype(F32)
-    total = 2 * len(points)
-    for start in range(0, total, batch):
-        ids = range(start, min(start + batch, total))
-        xs, norms = [], []
-        for i in ids:
-            system = eye + g_ref[i] * (1.0 / (K - 1.0))
-            sq = jnp.sum(jnp.sum(system * system, 0, keepdims=True), 1, keepdims=True)
-            norm = jnp.sqrt(sq)
-            norms.append(norm)
-            xs.append(system * (1.0 / norm))
-        zs = four_steps(xs, eye)
-        for i, z, norm in zip(ids, zs, norms):
-            p, g = i // 2, i % 2
-            near = g * padded(len(POINTS)) + skip + p
-            far = g * n + p
-            pull = pull_in_ref[:, near : near + 1] + pull_ref[:, far : far + 1]
-            inner = jnp.sum(z * pull, 0, keepdims=True)
-            shift = jnp.sum(z * inner, 1, keepdims=True) * (1.0 / (norm * (K - 1.0)))
-            out_ref[p, g] = (z * (1.0 / jnp.sqrt(norm)) + shift).astype(BF16)
+
+    def steps(first):
+        ids = [(p, g) for p in range(first, min(first + batch, len(points))) for g in range(2)]
+        now = {}
+
+        def gram():
+            for p, g in ids[::2]:
+                add_point(p)
+
+        def scale():
+            now["x"], now["norm"] = [], []
+            for p, g in ids:
+                system = eye + g_ref[2 * p + g] * (1.0 / (K - 1.0))
+                sq = jnp.sum(jnp.sum(system * system, 0, keepdims=True), 1, keepdims=True)
+                norm = jnp.sqrt(sq)
+                now["norm"].append(norm)
+                now["x"].append(system * (1.0 / norm))
+            now["xs"] = [split(x) for x in now["x"]]
+
+        def square(parts, out, times):
+            def run():
+                now[out] = [times(v, v) for v in now[parts]]
+
+            return run
+
+        def polynomial(x, sq, out, parts, times):
+            def run():
+                high = [times(parts(q), parts(C3 * v + C4 * q)) for v, q in zip(now[x], now[sq])]
+                now[out] = [
+                    split(C0 * eye + C1 * v + C2 * q + h) for v, q, h in zip(now[x], now[sq], high)
+                ]
+
+            return run
+
+        def second():
+            now["m"] = [mm(a, split(b)) for a, b in zip(now["xs"], now["w"])]
+            now["ms"] = [split(v) for v in now["m"]]
+
+        def inverse():
+            now["i"] = [mm(a, b) for a, b in zip(now["z"], now["q"])]
+
+        def write():
+            for (p, g), z, norm in zip(ids, now["i"], now["norm"]):
+                near = g * padded(len(POINTS)) + skip + p
+                far = g * n + p
+                pull = pull_in_ref[near : near + 1, :] + pull_ref[far : far + 1, :]
+                inner = jnp.sum(z * pull, 1, keepdims=True)
+                shift = jnp.sum(z * inner, 0, keepdims=True) * (1.0 / (norm * (K - 1.0)))
+                out_ref[p, g] = (z * (1.0 / jnp.sqrt(norm)) + shift).astype(BF16)
+
+        return [
+            gram,
+            scale,
+            square("xs", "b", mm_high),
+            polynomial("x", "b", "z", rounded, mm_high),
+            square("z", "w", mm),
+            second,
+            square("ms", "c", mm),
+            polynomial("m", "c", "q", split, mm),
+            inverse,
+            write,
+        ]
+
+    order = []
+    for k, first in enumerate(range(0, len(points), batch)):
+        order += [(k * LAG + j, k, step) for j, step in enumerate(steps(first))]
+    for _, _, step in sorted(order, key=lambda e: e[:2]):
+        step()
 
 
 def specs(n, scalars=1):
@@ -250,27 +294,28 @@
 def joined(kernel, rows, name, *blocks):
     return pl.pallas_call(
         kernel,
-        out_shape=jax.ShapeDtypeStruct((rows, K), BF16),
+        out_shape=[jax.ShapeDtypeStruct((n, K), BF16) for n in rows],
         in_specs=specs(len(blocks), 0),
+        compiler_params=pltpu.CompilerParams(vmem_limit_bytes=2 << 20),
         name=name,
     )(*blocks)
 
 
-def near_sums(frame, wide):
+def near_sums(frame, own, other):
     n = len(POINTS)
     return pl.pallas_call(
         near_kernel,
         out_shape=[
             jax.ShapeDtypeStruct((2 * FIRST, K, K), F32),
             jax.ShapeDtypeStruct((2 * (n - FIRST), K, K), F32),
-            jax.ShapeDtypeStruct((K, 2 * padded(n)), F32),
+            jax.ShapeDtypeStruct((2 * padded(n), K), F32),
         ],
-        in_specs=specs(1),
+        in_specs=specs(2),
         scratch_shapes=sum_scratch(POINTS, (0, 1)),
         compiler_params=pltpu.CompilerParams(vmem_limit_bytes=16 << 20),
         cost_estimate=pl.CostEstimate(flops=6_000_000_000, bytes_accessed=5_000_000, transcendentals=0),
         name="near_sums",
-    )(frame, wide)
+    )(frame, own, other)
 
 
 def transforms(points, rows, batch, name, frame, *arrays):
@@ -280,7 +325,7 @@
         out_shape=jax.ShapeDtypeStruct((n, 2, K, K), BF16),
         in_specs=specs(len(arrays)),
         scratch_shapes=sum_scratch(points, rows)
-        + [pltpu.VMEM((2 * n, K, K), F32), pltpu.VMEM((K, 2 * padded(n)), F32)],
+        + [pltpu.VMEM((2 * n, K, K), F32), pltpu.VMEM((2 * padded(n), K), F32)],
         compiler_params=pltpu.CompilerParams(vmem_limit_bytes=28 << 20),
         cost_estimate=pl.CostEstimate(flops=n * 500_000_000, bytes_accessed=4_000_000, transcendentals=0),
         name=name,
@@ -338,8 +383,8 @@
                 left = jnp.concatenate([anom_ref[i, j, span, :] for _, _, i, j in cells], 0)
                 sums = [mean_ref[i, j, span, :] for _, _, i, j in cells]
                 for cx in range(2):
-                    both = jnp.concatenate([transform(q + cx, p + cy, g) for cy in range(2)], 1)
-                    prod = lax.dot_general(left, both, NN, preferred_element_type=F32)
+                    both = jnp.concatenate([transform(q + cx, p + cy, g) for cy in range(2)], 0)
+                    prod = lax.dot_general(left, both, NT, preferred_element_type=F32)
                     for cy in range(2):
                         for c, (s, t, _, _) in enumerate(cells):
                             part = prod[c * NHALF : (c + 1) * NHALF, cy * K : (cy + 1) * K]
@@ -386,6 +431,7 @@
         pack_kernel,
         out_shape=jax.ShapeDtypeStruct((ROWS, K), BF16),
         in_specs=specs(4),
+        compiler_params=pltpu.CompilerParams(vmem_limit_bytes=2 << 20),
         name="pack_slots",
     )(
         obs_count,
@@ -398,19 +444,19 @@
     edge = jnp.where((row == 0) | (row == sizes[1] - 1), 1, 0)
     frame = jnp.stack([(col ^ row) & 1, row & 1, edge]).astype(jnp.int32)
 
-    pair = joined(pair_kernel, PAIR, "pair_tiles", own, moved(own, core, sizes))
+    (pair,) = joined(pair_kernel, [PAIR], "pair_tiles", own, moved(own, core, sizes))
     a = moved(pair, side(1), sizes)
     b = moved(pair, side(2), sizes)
     ta = moved(a, core, sizes)
     tb = moved(b, core, sizes)
-    wide = joined(wide_kernel, WIDE, "two_rows", pair, a, b, ta, tb)
-    y = moved(wide, beyond, sizes)
+    near, next_row = joined(rows_kernel, [WIDE, WIDE], "two_rows", pair, a, b, ta, tb)
+    y1 = moved(near, beyond, sizes)
     anom, mean = anomalies(ensemble)
-    gram_first, gram_rest, pull = near_sums(frame, wide)
-    y, pull = lax.optimization_barrier((y, pull))
-    z = moved(y, core, sizes)
-    first = transforms(POINTS[:FIRST], (-2, -1), 12, "first_points", frame, y, gram_first, pull)
-    rest = transforms(POINTS[FIRST:], (-1, 2), 12, "rest_points", frame, y, z, gram_rest, pull)
+    gram_first, gram_rest, pull = near_sums(frame, near, next_row)
+    y2 = moved(lax.optimization_barrier((next_row, pull))[0], beyond, sizes)
+    z = moved(lax.optimization_barrier((y1, pull))[0], core, sizes)
+    rest = transforms(POINTS[FIRST:], (-1, 2), 12, "rest_points", frame, y1, z, gram_rest, pull)
+    first = transforms(POINTS[:FIRST], (-2, -1), 9, "first_points", frame, y2, y1, gram_first, pull)
     high = moved(rest[-SIDE:], core, sizes)
     return apply(frame, anom, mean, first, rest, high)
 

time: 59.1 us -> 58.2 us (0.985)
  starting transfers between devices: 14 us -> 20.6 us
  Pallas kernels: 29.6 us -> 24.7 us
  waiting for transfers between devices: 11.8 us -> 9.02 us
    ppermute x8 -> x9, starting transfers between devices: 14 us -> 20.6 us  [moved(): return lax.ppermute(block, ('gx', 'gy'), pairs)]
    pallas_call x2, Pallas kernels: 3.2 us -> 0.04 us  [joined(): pl.pallas_call(kernel, out_shape=[jax.ShapeDtypeStruct((n, K), BF16) for...]
    ppermute x8 -> x9, waiting for transfers between devices: 11.8 us -> 9.02 us  [moved(): return lax.ppermute(block, ('gx', 'gy'), pairs)]
    pallas_call x1, Pallas kernels: 1.5 us -> 0.09 us  [shards(): pl.pallas_call(pack_kernel, out_shape=jax.ShapeDtypeStruct((ROWS, K), BF1...]
    pallas_call x2, Pallas kernels: 16.1 us -> 14.9 us  [transforms(): pl.pallas_call(functools.partial(points_kernel, points, rows, batch), out...]
    pallas_call x1, Pallas kernels: 2.87 us -> 3.71 us  [apply(): pl.pallas_call(apply_kernel, out_shape=jax.ShapeDtypeStruct(anom.shape, B...]
    unnamed x14 -> x10, local copies, waits for them, and re-layouts: 2.23 us -> 2.75 us
  transfers between devices with their start and end apart: 8 -> 9, of which waited for: 6 -> 5; matrix products, arithmetic and copies ran while one was open for 0% -> 0% of each run, Pallas kernels for 26% -> 36%
where the time goes in v3:
time: 58.2 us; the launch traced here: 58 us
  Pallas kernels  24.7 us (42%)
  starting transfers between devices  20.6 us (35%)
  waiting for transfers between devices  9.02 us (15%)
  local copies, waits for them, and re-layouts  2.77 us (5%)
  between operations  0.77 us (1%)
    ppermute x9, starting transfers between devices, moved(): return lax.ppermute(block, ('gx', 'gy'), pairs)  20.6 us
    pallas_call x2, Pallas kernels, transforms(): pl.pallas_call(functools.partial(points_kernel, points, rows, batch), out...  14.9 us
    ppermute x9, waiting for transfers between devices, moved(): return lax.ppermute(block, ('gx', 'gy'), pairs)  9.02 us
    pallas_call x1, Pallas kernels, near_sums(): pl.pallas_call(near_kernel, out_shape=[jax.ShapeDtypeStruct((2 * FIRST, K...  5.55 us
    pallas_call x1, Pallas kernels, apply(): pl.pallas_call(apply_kernel, out_shape=jax.ShapeDtypeStruct(anom.shape, B...  3.71 us
    unnamed x10, local copies, waits for them, and re-layouts  2.75 us
  transfers between devices with their start and end apart: 9, of which 5 were waited for; matrix products, arithmetic and copies ran while one was open for 0% of the time, Pallas kernels for 36%

profile of v3, /device:TPU:25, one launch (start us, length us, event | category | flops | bytes accessed | tf_op | source)
XLA Modules:
  0.0 58.0 jit_solution(12031817901416471055)
XLA Ops:
  0.7 0.0 copy-start
  0.7 0.7 %copy-done = bf16[1,1,128,128]{3,2,1,0:T(8,128)(2,1)S(1)} copy-done((bf16[1,1,128,128]{3,2,1,0:T(8,128)(2,1)S(1)}, bf16[1,1,128,128]{3,2,1,0:T(8,128)(2,1)}, u32[]{:S(2)}) %copy-start) | copy-done | bytes 32792
  1.4 0.7 %copy-done.1 = s32[1,1,2,128]{3,2,1,0:T(2,128)S(1)} copy-done((s32[1,1,2,128]{3,2,1,0:T(2,128)S(1)}, s32[1,1,2,128]{3,2,1,0:T(2,128)}, u32[]{:S(2)}) %copy-start.1) | copy-done | bytes 1048
  2.1 0.7 %copy-done.2 = bf16[1,1,128]{2,1,0:T(2,128)(2,1)S(1)} copy-done((bf16[1,1,128]{2,1,0:T(2,128)(2,1)S(1)}, bf16[1,1,128]{2,1,0:T(2,128)(2,1)}, u32[]{:S(2)}) %copy-start.2) | copy-done | bytes 280
  2.7 0.7 %copy-done.3 = bf16[1,1,128]{2,1,0:T(2,128)(2,1)S(1)} copy-done((bf16[1,1,128]{2,1,0:T(2,128)(2,1)S(1)}, bf16[1,1,128]{2,1,0:T(2,128)(2,1)}, u32[]{:S(2)}) %copy-start.3) | copy-done | bytes 280
  3.4 0.1 pack_slots.1.own_ref
  3.5 0.8 %collective-permute-start = (bf16[144,128]{1,0:T(8,128)(2,1)S(1)}, bf16[144,128]{1,0:T(8,128)(2,1)S(1)}, u32[]{:S(2)}, u32[]{:S(2)}) collective-permute-start(bf16[144,128]{1,0:T(8,128)(2,1)S(1)} %pack_slots.1.own_ref), channel_id=1, source_target_pairs={{1,0},{0,1},{3,2},{2,3},{5,4},{4,5},{7,6},{6,7},{9,8},{8,9},{11,10... | collective-permute-start | bytes 110600 | tf_op jit(solution)/shard_map/ppermute | solution.py:414
  4.3 0.9 %collective-permute-done.other_ref = bf16[144,128]{1,0:T(8,128)(2,1)S(1)} collective-permute-done((bf16[144,128]{1,0:T(8,128)(2,1)S(1)}, bf16[144,128]{1,0:T(8,128)(2,1)S(1)}, u32[]{:S(2)}, u32[]{:S(2)}) %collective-permute-start) | collective-permute-done | bytes 36896 | tf_op jit(solution)/shard_map/ppermute | solution.py:414
  5.1 6.6 %collective-permute-start.1 = (bf16[272,128]{1,0:T(8,128)(2,1)S(1)}, bf16[272,128]{1,0:T(8,128)(2,1)S(1)}, u32[]{:S(2)}, u32[]{:S(2)}) collective-permute-start(bf16[272,128]{1,0:T(8,128)(2,1)S(1)} %pair_tiles.1.pair_ref), channel_id=1, source_target_pairs={{16,0},{241,1},{18,2},{243,3},{20,4},{245,5},{22,6},{247,7},{24,8}... | collective-permute-start | bytes 208904 | tf_op jit(solution)/shard_map/ppermute | solution.py:414
  11.8 0.0 collective-permute-start.2
  11.8 1.9 %collective-permute-done.1.a_ref = bf16[272,128]{1,0:T(8,128)(2,1)S(1)} collective-permute-done((bf16[272,128]{1,0:T(8,128)(2,1)S(1)}, bf16[272,128]{1,0:T(8,128)(2,1)S(1)}, u32[]{:S(2)}, u32[]{:S(2)}) %collective-permute-start.1) | collective-permute-done | bytes 69664 | tf_op jit(solution)/shard_map/ppermute | solution.py:414
  13.6 0.0 collective-permute-start.3
  13.6 4.3 %collective-permute-done.2.b_ref = bf16[272,128]{1,0:T(8,128)(2,1)S(1)} collective-permute-done((bf16[272,128]{1,0:T(8,128)(2,1)S(1)}, bf16[272,128]{1,0:T(8,128)(2,1)S(1)}, u32[]{:S(2)}, u32[]{:S(2)}) %collective-permute-start.2) | collective-permute-done | bytes 69664 | tf_op jit(solution)/shard_map/ppermute | solution.py:414
  17.9 0.0 collective-permute-start.4
  17.9 0.1 pad_add_fusion.frame_ref.refs_0_
  18.0 0.0 collective-permute-done.3.ta_ref
  18.0 1.2 %collective-permute-done.4.tb_ref = bf16[272,128]{1,0:T(8,128)(2,1)S(1)} collective-permute-done((bf16[272,128]{1,0:T(8,128)(2,1)S(1)}, bf16[272,128]{1,0:T(8,128)(2,1)S(1)}, u32[]{:S(2)}, u32[]{:S(2)}) %collective-permute-start.4) | collective-permute-done | bytes 69664 | tf_op jit(solution)/shard_map/ppermute | solution.py:414
  19.2 6.4 %collective-permute-start.6 = (bf16[672,128]{1,0:T(8,128)(2,1)S(1)}, bf16[672,128]{1,0:T(8,128)(2,1)S(1)}, u32[]{:S(2)}, u32[]{:S(2)}) collective-permute-start(bf16[672,128]{1,0:T(8,128)(2,1)S(1)} %get-tuple-element.17.own_ref), channel_id=1, source_target_pairs={{2,1},{1,2},{4,3},{3,4},{6,5},{5,6},{8,7},{7,8},{10,9},{9,10},{12,... | collective-permute-start | bytes 516104 | tf_op jit(solution)/shard_map/ppermute | solution.py:414
  25.6 0.0 copy-start.4
  25.6 5.5 %near_sums.1 = (f32[36,128,128]{2,1,0:T(8,128)S(1)}, f32[24,128,128]{2,1,0:T(8,128)S(1)}, f32[64,128]{1,0:T(8,128)S(1)}) custom-call(s32[3]{0:T(128)S(1)} %pad_add_fusion.frame_ref.refs_0_, bf16[672,128]{1,0:T(8,128)(2,1)S(1)} %get-tuple-element.17.own_ref, bf16[672,128]{1,0:T(8,128)(2,1)S(1)} %get-tuple-element.19.other_ref), custom_call_target="tpu_custom_call" | custom-call | flops 6000000000 | bytes 5000000 | tf_op jit(solution)/shard_map/near_sums/pallas_call | solution.py:306
  31.2 0.8 %collective-permute-done.6.refs_2_.refs_1_ = bf16[672,128]{1,0:T(8,128)(2,1)S(1)} collective-permute-done((bf16[672,128]{1,0:T(8,128)(2,1)S(1)}, bf16[672,128]{1,0:T(8,128)(2,1)S(1)}, u32[]{:S(2)}, u32[]{:S(2)}) %collective-permute-start.6) | collective-permute-done | bytes 172064 | tf_op jit(solution)/shard_map/ppermute | solution.py:414
  32.0 0.0 collective-permute-start.7
  32.0 0.0 copy-done.4
  32.0 0.4 anomalies.1
  32.4 6.5 %collective-permute-start.5 = (bf16[672,128]{1,0:T(8,128)(2,1)S(1)}, bf16[672,128]{1,0:T(8,128)(2,1)S(1)}, u32[]{:S(2)}, u32[]{:S(2)}) collective-permute-start(bf16[672,128]{1,0:T(8,128)(2,1)S(1)} %get-tuple-element.19.other_ref), channel_id=1, source_target_pairs={{2,1},{1,2},{4,3},{3,4},{6,5},{5,6},{8,7},{7,8},{10,9},{9,10},{12,... | collective-permute-start | bytes 516104 | tf_op jit(solution)/shard_map/ppermute | solution.py:414
  39.0 0.0 collective-permute-done.7.refs_2_
  39.0 6.0 %rest_points.1.rest_ref = bf16[12,2,128,128]{3,2,1,0:T(8,128)(2,1)S(1)} custom-call(s32[3]{0:T(128)S(1)} %pad_add_fusion.frame_ref.refs_0_, bf16[672,128]{1,0:T(8,128)(2,1)S(1)} %collective-permute-done.6.refs_2_.refs_1_, bf16[672,128]{1,0:T(8,128)(2,1)S(1)} %collective-permute-done.7.refs_2_, f32[24,128,128]{2,1,0:T(8,128)S(1)} %get-tuple-element.22.refs_3_, ...), custom_call_target="tpu_custom_call" | custom-call | flops 6000000000 | bytes 4000000 | tf_op jit(solution)/shard_map/rest_points/pallas_call | solution.py:323
  45.0 0.3 collective-permute-start.8
  45.3 0.0 collective-permute-done.5.refs_1_
  45.3 9.0 %first_points.1.first_ref = bf16[18,2,128,128]{3,2,1,0:T(8,128)(2,1)S(1)} custom-call(s32[3]{0:T(128)S(1)} %pad_add_fusion.frame_ref.refs_0_, bf16[672,128]{1,0:T(8,128)(2,1)S(1)} %collective-permute-done.5.refs_1_, bf16[672,128]{1,0:T(8,128)(2,1)S(1)} %collective-permute-done.6.refs_2_.refs_1_, f32[36,128,128]{2,1,0:T(8,128)S(1)} %get-tuple-element.20.refs_3_, ...), custom_call_target="tpu_custom_call" | custom-call | flops 8999999488 | bytes 4000000 | tf_op jit(solution)/shard_map/first_points/pallas_call | solution.py:323
  54.3 0.0 collective-permute-done.8.high_ref
  54.3 3.7 %apply_transforms.1 = bf16[8,8,64,128]{3,2,1,0:T(8,128)(2,1)} custom-call(s32[3]{0:T(128)S(1)} %pad_add_fusion.frame_ref.refs_0_, bf16[8,8,64,128]{3,2,1,0:T(8,128)(2,1)S(1)} %get-tuple-element.14.anom_ref, f32[8,8,64,128]{3,2,1,0:T(8,128)S(1)} %get-tuple-element.15.mean_ref, bf16[18,2,128,128]{3,2,1,0:T(8,128)(2,1)S(1)} %first_points.1.first_ref, ...), custom_call_target="tpu_custom_call" | custom-call | tf_op jit(solution)/shard_map/apply_transforms/pallas_call | solution.py:397
  (6 shorter events, 0.1 us)
Async XLA Ops:
  0.7 0.8 %copy-start = (bf16[1,1,128,128]{3,2,1,0:T(8,128)(2,1)S(1)}, bf16[1,1,128,128]{3,2,1,0:T(8,128)(2,1)}, u32[]{:S(2)}) copy-start(bf16[1,1,128,128]{3,2,1,0:T(8,128)(2,1)} %param.7) | copy-start | bytes 98308
  1.4 0.7 %copy-start.1 = (s32[1,1,2,128]{3,2,1,0:T(2,128)S(1)}, s32[1,1,2,128]{3,2,1,0:T(2,128)}, u32[]{:S(2)}) copy-start(s32[1,1,2,128]{3,2,1,0:T(2,128)} %param.10) | copy-start | bytes 3076
  2.1 0.7 %copy-start.2 = (bf16[1,1,128]{2,1,0:T(2,128)(2,1)S(1)}, bf16[1,1,128]{2,1,0:T(2,128)(2,1)}, u32[]{:S(2)}) copy-start(bf16[1,1,128]{2,1,0:T(2,128)(2,1)} %param.8) | copy-start | bytes 772
  2.7 0.7 %copy-start.3 = (bf16[1,1,128]{2,1,0:T(2,128)(2,1)S(1)}, bf16[1,1,128]{2,1,0:T(2,128)(2,1)}, u32[]{:S(2)}) copy-start(bf16[1,1,128]{2,1,0:T(2,128)(2,1)} %param.9) | copy-start | bytes 772
  3.5 1.6 %collective-permute-start = (bf16[144,128]{1,0:T(8,128)(2,1)S(1)}, bf16[144,128]{1,0:T(8,128)(2,1)S(1)}, u32[]{:S(2)}, u32[]{:S(2)}) collective-permute-start(bf16[144,128]{1,0:T(8,128)(2,1)S(1)} %pack_slots.1.own_ref), channel_id=1, source_target_pairs={{1,0},{0,1},{3,2},{2,3},{5,4},{4,5},{7,6},{6,7},{9,8},{8,9},{11,10... | collective-permute-start | bytes 110600 | tf_op jit(solution)/shard_map/ppermute | solution.py:414
  5.1 8.5 %collective-permute-start.1 = (bf16[272,128]{1,0:T(8,128)(2,1)S(1)}, bf16[272,128]{1,0:T(8,128)(2,1)S(1)}, u32[]{:S(2)}, u32[]{:S(2)}) collective-permute-start(bf16[272,128]{1,0:T(8,128)(2,1)S(1)} %pair_tiles.1.pair_ref), channel_id=1, source_target_pairs={{16,0},{241,1},{18,2},{243,3},{20,4},{245,5},{22,6},{247,7},{24,8}... | collective-permute-start | bytes 208904 | tf_op jit(solution)/shard_map/ppermute | solution.py:414
  11.8 6.2 %collective-permute-start.2 = (bf16[272,128]{1,0:T(8,128)(2,1)S(1)}, bf16[272,128]{1,0:T(8,128)(2,1)S(1)}, u32[]{:S(2)}, u32[]{:S(2)}) collective-permute-start(bf16[272,128]{1,0:T(8,128)(2,1)S(1)} %pair_tiles.1.pair_ref), channel_id=1, source_target_pairs={{32,0},{225,1},{34,2},{227,3},{36,4},{229,5},{38,6},{231,7},{40,8}... | collective-permute-start | bytes 208904 | tf_op jit(solution)/shard_map/ppermute | solution.py:414
  13.6 4.4 %collective-permute-start.3 = (bf16[272,128]{1,0:T(8,128)(2,1)S(1)}, bf16[272,128]{1,0:T(8,128)(2,1)S(1)}, u32[]{:S(2)}, u32[]{:S(2)}) collective-permute-start(bf16[272,128]{1,0:T(8,128)(2,1)S(1)} %collective-permute-done.1.a_ref), channel_id=1, source_target_pairs={{1,0},{0,1},{3,2},{2,3},{5,4},{4,5},{7,6},{6,7},{9,8},{8,9},{11,10... | collective-permute-start | bytes 208904 | tf_op jit(solution)/shard_map/ppermute | solution.py:414
  17.9 1.3 %collective-permute-start.4 = (bf16[272,128]{1,0:T(8,128)(2,1)S(1)}, bf16[272,128]{1,0:T(8,128)(2,1)S(1)}, u32[]{:S(2)}, u32[]{:S(2)}) collective-permute-start(bf16[272,128]{1,0:T(8,128)(2,1)S(1)} %collective-permute-done.2.b_ref), channel_id=1, source_target_pairs={{1,0},{0,1},{3,2},{2,3},{5,4},{4,5},{7,6},{6,7},{9,8},{8,9},{11,10... | collective-permute-start | bytes 208904 | tf_op jit(solution)/shard_map/ppermute | solution.py:414
  19.2 12.7 %collective-permute-start.6 = (bf16[672,128]{1,0:T(8,128)(2,1)S(1)}, bf16[672,128]{1,0:T(8,128)(2,1)S(1)}, u32[]{:S(2)}, u32[]{:S(2)}) collective-permute-start(bf16[672,128]{1,0:T(8,128)(2,1)S(1)} %get-tuple-element.17.own_ref), channel_id=1, source_target_pairs={{2,1},{1,2},{4,3},{3,4},{6,5},{5,6},{8,7},{7,8},{10,9},{9,10},{12,... | collective-permute-start | bytes 516104 | tf_op jit(solution)/shard_map/ppermute | solution.py:414
  25.6 6.4 %copy-start.4 = (bf16[8,8,64,128]{3,2,1,0:T(8,128)(2,1)S(1)}, bf16[8,8,64,128]{3,2,1,0:T(8,128)(2,1)}, u32[]{:S(2)}) copy-start(bf16[8,8,64,128]{3,2,1,0:T(8,128)(2,1)} %ens_ref.1) | copy-start | bytes 3145732
  32.0 7.0 %collective-permute-start.7 = (bf16[672,128]{1,0:T(8,128)(2,1)S(1)}, bf16[672,128]{1,0:T(8,128)(2,1)S(1)}, u32[]{:S(2)}, u32[]{:S(2)}) collective-permute-start(bf16[672,128]{1,0:T(8,128)(2,1)S(1)} %collective-permute-done.6.refs_2_.refs_1_), channel_id=1, source_target_pairs={{1,0},{0,1},{3,2},{2,3},{5,4},{4,5},{7,6},{6,7},{9,8},{8,9},{11,10... | collective-permute-start | bytes 516104 | tf_op jit(solution)/shard_map/ppermute | solution.py:414
  32.4 12.9 %collective-permute-start.5 = (bf16[672,128]{1,0:T(8,128)(2,1)S(1)}, bf16[672,128]{1,0:T(8,128)(2,1)S(1)}, u32[]{:S(2)}, u32[]{:S(2)}) collective-permute-start(bf16[672,128]{1,0:T(8,128)(2,1)S(1)} %get-tuple-element.19.other_ref), channel_id=1, source_target_pairs={{2,1},{1,2},{4,3},{3,4},{6,5},{5,6},{8,7},{7,8},{10,9},{9,10},{12,... | collective-permute-start | bytes 516104 | tf_op jit(solution)/shard_map/ppermute | solution.py:414
  45.0 9.3 %collective-permute-start.8 = (bf16[6,2,128,128]{3,2,1,0:T(8,128)(2,1)S(1)}, bf16[6,2,128,128]{3,2,1,0:T(8,128)(2,1)S(1)}, u32[]{:S(2)}, u32[]{:S(2)}) collective-permute-start(bf16[6,2,128,128]{3,2,1,0:T(8,128)(2,1)S(1)} %slice.4), channel_id=1, source_target_pairs={{1,0},{0,1},{3,2},{2,3},{5,4},{4,5},{7,6},{6,7},{9,8},{8,9},{11,10... | collective-permute-start | bytes 1179656 | tf_op jit(solution)/shard_map/ppermute | solution.py:414

commit v4 on v3

--- a/solution.py
+++ b/solution.py
@@ -18,6 +18,7 @@
 PAIR = 2 * K + 16
 WIDE = 5 * K + 32
 SLOTS = 2
+FLOPS = 500_000_000
 LAG = 10
 
 NT = (((1,), (1,)), ((), ()))
@@ -327,7 +328,7 @@
         scratch_shapes=sum_scratch(points, rows)
         + [pltpu.VMEM((2 * n, K, K), F32), pltpu.VMEM((2 * padded(n), K), F32)],
         compiler_params=pltpu.CompilerParams(vmem_limit_bytes=28 << 20),
-        cost_estimate=pl.CostEstimate(flops=n * 500_000_000, bytes_accessed=4_000_000, transcendentals=0),
+        cost_estimate=pl.CostEstimate(flops=n * FLOPS, bytes_accessed=4_000_000, transcendentals=0),
         name=name,
     )(frame, *arrays)
 
@@ -356,7 +357,7 @@
     )(ensemble)
 
 
-def apply_kernel(frame_ref, anom_ref, mean_ref, first_ref, rest_ref, high_ref, out_ref):
+def apply_kernel(frame_ref, anom_ref, mean_ref, first_ref, rest_ref, high_ref, out_ref, sum_ref):
     rx, ry, edge = frame_ref[0], frame_ref[1], frame_ref[2]
 
     def transform(x, y, g):
@@ -369,28 +370,30 @@
         return high_ref[SIDE - 1 - x, g]
 
     frac = [(s + 0.5) / SPACING for s in range(SPACING)]
-    corner = [[1.0 - f for f in frac], frac]
-    for p in range(APX + 1):
-        for q in range(APX + 1):
-            cells = []
-            for s in range(2):
-                for t in range(2):
-                    i, j = 2 * q - 1 + s, 2 * p - 1 + t
-                    if 0 <= i < CT and 0 <= j < CT:
-                        cells.append((s, t, i + rx * (CT - 1 - 2 * i), j + ry * (CT - 1 - 2 * j)))
+    factor = [[1.0 - f for f in frac], frac]
+
+    def columns(x):
+        at = [(i, x - (i + 1) // SPACING, (i + 1) % SPACING) for i in range(CT)]
+        return [(i, factor[c][s], c == 1) for i, c, s in at if c in (0, 1)]
+
+    def place(i, j):
+        return i + rx * (CT - 1 - 2 * i), j + ry * (CT - 1 - 2 * j)
+
+    for y in range(SIDE):
+        for x in range(SIDE):
+            cells = [(i, j, fi * fj, li and lj) for i, fi, li in columns(x) for j, fj, lj in columns(y)]
             for g in range(2):
                 span = slice(g * NHALF, (g + 1) * NHALF)
-                left = jnp.concatenate([anom_ref[i, j, span, :] for _, _, i, j in cells], 0)
-                sums = [mean_ref[i, j, span, :] for _, _, i, j in cells]
-                for cx in range(2):
-                    both = jnp.concatenate([transform(q + cx, p + cy, g) for cy in range(2)], 0)
-                    prod = lax.dot_general(left, both, NT, preferred_element_type=F32)
-                    for cy in range(2):
-                        for c, (s, t, _, _) in enumerate(cells):
-                            part = prod[c * NHALF : (c + 1) * NHALF, cy * K : (cy + 1) * K]
-                            sums[c] = sums[c] + part * (corner[cx][s] * corner[cy][t])
-                for total, (_, _, i, j) in zip(sums, cells):
-                    out_ref[i, j, span, :] = total.astype(BF16)
+                left = jnp.concatenate([anom_ref[(*place(i, j), span)] for i, j, _, _ in cells], 0)
+                prod = lax.dot_general(left, transform(x, y, g), NT, preferred_element_type=F32)
+                for c, (i, j, share, last) in enumerate(cells):
+                    fresh = x == (i + 1) // SPACING and y == (j + 1) // SPACING
+                    total = mean_ref[(*place(i, j), span)] if fresh else sum_ref[i, j, span]
+                    total = total + prod[c * NHALF : (c + 1) * NHALF] * share
+                    if last:
+                        out_ref[(*place(i, j), span)] = total.astype(BF16)
+                    else:
+                        sum_ref[i, j, span] = total
 
 
 def apply(frame, anom, mean, first, rest, high):
@@ -398,6 +401,7 @@
         apply_kernel,
         out_shape=jax.ShapeDtypeStruct(anom.shape, BF16),
         in_specs=specs(5),
+        scratch_shapes=[pltpu.VMEM(anom.shape, F32)],
         compiler_params=pltpu.CompilerParams(vmem_limit_bytes=16 << 20),
         name="apply_transforms",
     )(frame, anom, mean, first, rest, high)
@@ -431,7 +435,6 @@
         pack_kernel,
         out_shape=jax.ShapeDtypeStruct((ROWS, K), BF16),
         in_specs=specs(4),
-        compiler_params=pltpu.CompilerParams(vmem_limit_bytes=2 << 20),
         name="pack_slots",
     )(
         obs_count,

time: 58.2 us -> 57.5 us (0.988)
  local copies, waits for them, and re-layouts: 2.77 us -> 0.8 us
  Pallas kernels: 24.7 us -> 25.9 us
    unnamed x10 -> x4, local copies, waits for them, and re-layouts: 2.75 us -> 0.77 us
    pallas_call x1, Pallas kernels: 0.09 us -> 1.5 us  [shards(): pl.pallas_call(pack_kernel, out_shape=jax.ShapeDtypeStruct((ROWS, K), BF1...]
  transfers between devices with their start and end apart: 9 -> 9, of which waited for: 5 -> 5; matrix products, arithmetic and copies ran while one was open for 0% -> 0% of each run, Pallas kernels for 36% -> 37%
where the time goes in v4:
time: 57.5 us; the launch traced here: 57.3 us
  Pallas kernels  25.9 us (45%)
  starting transfers between devices  20.5 us (36%)
  waiting for transfers between devices  9.26 us (16%)
  local copies, waits for them, and re-layouts  0.8 us (1%)
  between operations  0.75 us (1%)
    ppermute x9, starting transfers between devices, moved(): return lax.ppermute(block, ('gx', 'gy'), pairs)  20.5 us
    pallas_call x2, Pallas kernels, transforms(): pl.pallas_call(functools.partial(points_kernel, points, rows, batch), out...  15 us
    ppermute x9, waiting for transfers between devices, moved(): return lax.ppermute(block, ('gx', 'gy'), pairs)  9.26 us
    pallas_call x1, Pallas kernels, near_sums(): pl.pallas_call(near_kernel, out_shape=[jax.ShapeDtypeStruct((2 * FIRST, K...  5.52 us
    pallas_call x1, Pallas kernels, apply(): pl.pallas_call(apply_kernel, out_shape=jax.ShapeDtypeStruct(anom.shape, B...  3.38 us
    pallas_call x1, Pallas kernels, shards(): pl.pallas_call(pack_kernel, out_shape=jax.ShapeDtypeStruct((ROWS, K), BF1...  1.5 us
  transfers between devices with their start and end apart: 9, of which 5 were waited for; matrix products, arithmetic and copies ran while one was open for 0% of the time, Pallas kernels for 37%

profile of v4, /device:TPU:25, one launch (start us, length us, event | category | flops | bytes accessed | tf_op | source)
XLA Modules:
  0.0 57.3 jit_solution(8763982316596201664)
XLA Ops:
  0.7 1.5 %pack_slots.1.own_ref = bf16[144,128]{1,0:T(8,128)(2,1)} custom-call(s32[1,1]{1,0:T(1,128)S(6)} %copy.7.count_ref, bf16[128,128]{1,0:T(8,128)(2,1)} %bitcast.7, bf16[1,128]{1,0:T(2,128)(2,1)} %bitcast.9, bf16[1,128]{1,0:T(2,128)(2,1)} %bitcast.10, s32[2,128]{1,0:T(2,128)} %bitcast.8), custom_call_target="tpu_custom_call" | custom-call | tf_op jit(solution)/shard_map/pack_slots/pallas_call | solution.py:434
  2.1 0.7 %collective-permute-start = (bf16[144,128]{1,0:T(8,128)(2,1)}, bf16[144,128]{1,0:T(8,128)(2,1)S(1)}, u32[]{:S(2)}, u32[]{:S(2)}) collective-permute-start(bf16[144,128]{1,0:T(8,128)(2,1)} %pack_slots.1.own_ref), channel_id=1, source_target_pairs={{1,0},{0,1},{3,2},{2,3},{5,4},{4,5},{7,6},{6,7},{9,8},{8,9},{11,10... | collective-permute-start | bytes 110600 | tf_op jit(solution)/shard_map/ppermute | solution.py:418
  2.8 1.1 %collective-permute-done.other_ref = bf16[144,128]{1,0:T(8,128)(2,1)S(1)} collective-permute-done((bf16[144,128]{1,0:T(8,128)(2,1)}, bf16[144,128]{1,0:T(8,128)(2,1)S(1)}, u32[]{:S(2)}, u32[]{:S(2)}) %collective-permute-start) | collective-permute-done | bytes 36896 | tf_op jit(solution)/shard_map/ppermute | solution.py:418
  3.9 0.0 copy-start
  3.9 0.8 %copy-done = bf16[144,128]{1,0:T(8,128)(2,1)S(1)} copy-done((bf16[144,128]{1,0:T(8,128)(2,1)S(1)}, bf16[144,128]{1,0:T(8,128)(2,1)}, u32[]{:S(2)}) %copy-start) | copy-done | bytes 36888
  4.7 6.6 %collective-permute-start.1 = (bf16[272,128]{1,0:T(8,128)(2,1)S(1)}, bf16[272,128]{1,0:T(8,128)(2,1)S(1)}, u32[]{:S(2)}, u32[]{:S(2)}) collective-permute-start(bf16[272,128]{1,0:T(8,128)(2,1)S(1)} %pair_tiles.1.pair_ref), channel_id=1, source_target_pairs={{16,0},{241,1},{18,2},{243,3},{20,4},{245,5},{22,6},{247,7},{24,8}... | collective-permute-start | bytes 208904 | tf_op jit(solution)/shard_map/ppermute | solution.py:418
  11.3 0.0 collective-permute-start.2
  11.3 1.9 %collective-permute-done.1.a_ref = bf16[272,128]{1,0:T(8,128)(2,1)S(1)} collective-permute-done((bf16[272,128]{1,0:T(8,128)(2,1)S(1)}, bf16[272,128]{1,0:T(8,128)(2,1)S(1)}, u32[]{:S(2)}, u32[]{:S(2)}) %collective-permute-start.1) | collective-permute-done | bytes 69664 | tf_op jit(solution)/shard_map/ppermute | solution.py:418
  13.2 0.0 collective-permute-start.3
  13.2 4.3 %collective-permute-done.2.b_ref = bf16[272,128]{1,0:T(8,128)(2,1)S(1)} collective-permute-done((bf16[272,128]{1,0:T(8,128)(2,1)S(1)}, bf16[272,128]{1,0:T(8,128)(2,1)S(1)}, u32[]{:S(2)}, u32[]{:S(2)}) %collective-permute-start.2) | collective-permute-done | bytes 69664 | tf_op jit(solution)/shard_map/ppermute | solution.py:418
  17.5 0.0 collective-permute-start.4
  17.5 0.1 pad_add_fusion.frame_ref.refs_0_
  17.6 0.0 collective-permute-done.3.ta_ref
  17.6 1.2 %collective-permute-done.4.tb_ref = bf16[272,128]{1,0:T(8,128)(2,1)S(1)} collective-permute-done((bf16[272,128]{1,0:T(8,128)(2,1)S(1)}, bf16[272,128]{1,0:T(8,128)(2,1)S(1)}, u32[]{:S(2)}, u32[]{:S(2)}) %collective-permute-start.4) | collective-permute-done | bytes 69664 | tf_op jit(solution)/shard_map/ppermute | solution.py:418
  18.8 6.4 %collective-permute-start.6 = (bf16[672,128]{1,0:T(8,128)(2,1)S(1)}, bf16[672,128]{1,0:T(8,128)(2,1)S(1)}, u32[]{:S(2)}, u32[]{:S(2)}) collective-permute-start(bf16[672,128]{1,0:T(8,128)(2,1)S(1)} %get-tuple-element.17.own_ref), channel_id=1, source_target_pairs={{2,1},{1,2},{4,3},{3,4},{6,5},{5,6},{8,7},{7,8},{10,9},{9,10},{12,... | collective-permute-start | bytes 516104 | tf_op jit(solution)/shard_map/ppermute | solution.py:418
  25.1 0.0 copy-start.1
  25.2 5.5 %near_sums.1 = (f32[36,128,128]{2,1,0:T(8,128)S(1)}, f32[24,128,128]{2,1,0:T(8,128)S(1)}, f32[64,128]{1,0:T(8,128)S(1)}) custom-call(s32[3]{0:T(128)S(1)} %pad_add_fusion.frame_ref.refs_0_, bf16[672,128]{1,0:T(8,128)(2,1)S(1)} %get-tuple-element.17.own_ref, bf16[672,128]{1,0:T(8,128)(2,1)S(1)} %get-tuple-element.19.other_ref), custom_call_target="tpu_custom_call" | custom-call | flops 6000000000 | bytes 5000000 | tf_op jit(solution)/shard_map/near_sums/pallas_call | solution.py:307
  30.7 0.8 %collective-permute-done.6.refs_2_.refs_1_ = bf16[672,128]{1,0:T(8,128)(2,1)S(1)} collective-permute-done((bf16[672,128]{1,0:T(8,128)(2,1)S(1)}, bf16[672,128]{1,0:T(8,128)(2,1)S(1)}, u32[]{:S(2)}, u32[]{:S(2)}) %collective-permute-start.6) | collective-permute-done | bytes 172064 | tf_op jit(solution)/shard_map/ppermute | solution.py:418
  31.5 0.0 collective-permute-start.7
  31.5 0.0 copy-done.1
  31.5 0.4 anomalies.1
  31.9 6.5 %collective-permute-start.5 = (bf16[672,128]{1,0:T(8,128)(2,1)S(1)}, bf16[672,128]{1,0:T(8,128)(2,1)S(1)}, u32[]{:S(2)}, u32[]{:S(2)}) collective-permute-start(bf16[672,128]{1,0:T(8,128)(2,1)S(1)} %get-tuple-element.19.other_ref), channel_id=1, source_target_pairs={{2,1},{1,2},{4,3},{3,4},{6,5},{5,6},{8,7},{7,8},{10,9},{9,10},{12,... | collective-permute-start | bytes 516104 | tf_op jit(solution)/shard_map/ppermute | solution.py:418
  38.5 0.0 collective-permute-done.7.refs_2_
  38.5 6.0 %rest_points.1.rest_ref = bf16[12,2,128,128]{3,2,1,0:T(8,128)(2,1)S(1)} custom-call(s32[3]{0:T(128)S(1)} %pad_add_fusion.frame_ref.refs_0_, bf16[672,128]{1,0:T(8,128)(2,1)S(1)} %collective-permute-done.6.refs_2_.refs_1_, bf16[672,128]{1,0:T(8,128)(2,1)S(1)} %collective-permute-done.7.refs_2_, f32[24,128,128]{2,1,0:T(8,128)S(1)} %get-tuple-element.22.refs_3_, ...), custom_call_target="tpu_custom_call" | custom-call | flops 6000000000 | bytes 4000000 | tf_op jit(solution)/shard_map/rest_points/pallas_call | solution.py:324
  44.6 0.3 collective-permute-start.8
  44.9 0.0 collective-permute-done.5.refs_1_
  44.9 9.0 %first_points.1.first_ref = bf16[18,2,128,128]{3,2,1,0:T(8,128)(2,1)S(1)} custom-call(s32[3]{0:T(128)S(1)} %pad_add_fusion.frame_ref.refs_0_, bf16[672,128]{1,0:T(8,128)(2,1)S(1)} %collective-permute-done.5.refs_1_, bf16[672,128]{1,0:T(8,128)(2,1)S(1)} %collective-permute-done.6.refs_2_.refs_1_, f32[36,128,128]{2,1,0:T(8,128)S(1)} %get-tuple-element.20.refs_3_, ...), custom_call_target="tpu_custom_call" | custom-call | flops 8999999488 | bytes 4000000 | tf_op jit(solution)/shard_map/first_points/pallas_call | solution.py:324
  53.9 0.0 collective-permute-done.8.high_ref
  53.9 3.4 %apply_transforms.1 = bf16[8,8,64,128]{3,2,1,0:T(8,128)(2,1)} custom-call(s32[3]{0:T(128)S(1)} %pad_add_fusion.frame_ref.refs_0_, bf16[8,8,64,128]{3,2,1,0:T(8,128)(2,1)S(1)} %get-tuple-element.14.anom_ref, f32[8,8,64,128]{3,2,1,0:T(8,128)S(1)} %get-tuple-element.15.mean_ref, bf16[18,2,128,128]{3,2,1,0:T(8,128)(2,1)S(1)} %first_points.1.first_ref, ...), custom_call_target="tpu_custom_call" | custom-call | tf_op jit(solution)/shard_map/apply_transforms/pallas_call | solution.py:400
  (3 shorter events, 0.1 us)
Async XLA Ops:
  2.1 1.8 %collective-permute-start = (bf16[144,128]{1,0:T(8,128)(2,1)}, bf16[144,128]{1,0:T(8,128)(2,1)S(1)}, u32[]{:S(2)}, u32[]{:S(2)}) collective-permute-start(bf16[144,128]{1,0:T(8,128)(2,1)} %pack_slots.1.own_ref), channel_id=1, source_target_pairs={{1,0},{0,1},{3,2},{2,3},{5,4},{4,5},{7,6},{6,7},{9,8},{8,9},{11,10... | collective-permute-start | bytes 110600 | tf_op jit(solution)/shard_map/ppermute | solution.py:418
  3.9 0.8 %copy-start = (bf16[144,128]{1,0:T(8,128)(2,1)S(1)}, bf16[144,128]{1,0:T(8,128)(2,1)}, u32[]{:S(2)}) copy-start(bf16[144,128]{1,0:T(8,128)(2,1)} %pack_slots.1.own_ref) | copy-start | bytes 110596
  4.7 8.5 %collective-permute-start.1 = (bf16[272,128]{1,0:T(8,128)(2,1)S(1)}, bf16[272,128]{1,0:T(8,128)(2,1)S(1)}, u32[]{:S(2)}, u32[]{:S(2)}) collective-permute-start(bf16[272,128]{1,0:T(8,128)(2,1)S(1)} %pair_tiles.1.pair_ref), channel_id=1, source_target_pairs={{16,0},{241,1},{18,2},{243,3},{20,4},{245,5},{22,6},{247,7},{24,8}... | collective-permute-start | bytes 208904 | tf_op jit(solution)/shard_map/ppermute | solution.py:418
  11.3 6.2 %collective-permute-start.2 = (bf16[272,128]{1,0:T(8,128)(2,1)S(1)}, bf16[272,128]{1,0:T(8,128)(2,1)S(1)}, u32[]{:S(2)}, u32[]{:S(2)}) collective-permute-start(bf16[272,128]{1,0:T(8,128)(2,1)S(1)} %pair_tiles.1.pair_ref), channel_id=1, source_target_pairs={{32,0},{225,1},{34,2},{227,3},{36,4},{229,5},{38,6},{231,7},{40,8}... | collective-permute-start | bytes 208904 | tf_op jit(solution)/shard_map/ppermute | solution.py:418
  13.2 4.4 %collective-permute-start.3 = (bf16[272,128]{1,0:T(8,128)(2,1)S(1)}, bf16[272,128]{1,0:T(8,128)(2,1)S(1)}, u32[]{:S(2)}, u32[]{:S(2)}) collective-permute-start(bf16[272,128]{1,0:T(8,128)(2,1)S(1)} %collective-permute-done.1.a_ref), channel_id=1, source_target_pairs={{1,0},{0,1},{3,2},{2,3},{5,4},{4,5},{7,6},{6,7},{9,8},{8,9},{11,10... | collective-permute-start | bytes 208904 | tf_op jit(solution)/shard_map/ppermute | solution.py:418
  17.5 1.3 %collective-permute-start.4 = (bf16[272,128]{1,0:T(8,128)(2,1)S(1)}, bf16[272,128]{1,0:T(8,128)(2,1)S(1)}, u32[]{:S(2)}, u32[]{:S(2)}) collective-permute-start(bf16[272,128]{1,0:T(8,128)(2,1)S(1)} %collective-permute-done.2.b_ref), channel_id=1, source_target_pairs={{1,0},{0,1},{3,2},{2,3},{5,4},{4,5},{7,6},{6,7},{9,8},{8,9},{11,10... | collective-permute-start | bytes 208904 | tf_op jit(solution)/shard_map/ppermute | solution.py:418
  18.8 12.7 %collective-permute-start.6 = (bf16[672,128]{1,0:T(8,128)(2,1)S(1)}, bf16[672,128]{1,0:T(8,128)(2,1)S(1)}, u32[]{:S(2)}, u32[]{:S(2)}) collective-permute-start(bf16[672,128]{1,0:T(8,128)(2,1)S(1)} %get-tuple-element.17.own_ref), channel_id=1, source_target_pairs={{2,1},{1,2},{4,3},{3,4},{6,5},{5,6},{8,7},{7,8},{10,9},{9,10},{12,... | collective-permute-start | bytes 516104 | tf_op jit(solution)/shard_map/ppermute | solution.py:418
  25.1 6.4 %copy-start.1 = (bf16[8,8,64,128]{3,2,1,0:T(8,128)(2,1)S(1)}, bf16[8,8,64,128]{3,2,1,0:T(8,128)(2,1)}, u32[]{:S(2)}) copy-start(bf16[8,8,64,128]{3,2,1,0:T(8,128)(2,1)} %ens_ref.1) | copy-start | bytes 3145732
  31.5 7.0 %collective-permute-start.7 = (bf16[672,128]{1,0:T(8,128)(2,1)S(1)}, bf16[672,128]{1,0:T(8,128)(2,1)S(1)}, u32[]{:S(2)}, u32[]{:S(2)}) collective-permute-start(bf16[672,128]{1,0:T(8,128)(2,1)S(1)} %collective-permute-done.6.refs_2_.refs_1_), channel_id=1, source_target_pairs={{1,0},{0,1},{3,2},{2,3},{5,4},{4,5},{7,6},{6,7},{9,8},{8,9},{11,10... | collective-permute-start | bytes 516104 | tf_op jit(solution)/shard_map/ppermute | solution.py:418
  31.9 13.0 %collective-permute-start.5 = (bf16[672,128]{1,0:T(8,128)(2,1)S(1)}, bf16[672,128]{1,0:T(8,128)(2,1)S(1)}, u32[]{:S(2)}, u32[]{:S(2)}) collective-permute-start(bf16[672,128]{1,0:T(8,128)(2,1)S(1)} %get-tuple-element.19.other_ref), channel_id=1, source_target_pairs={{2,1},{1,2},{4,3},{3,4},{6,5},{5,6},{8,7},{7,8},{10,9},{9,10},{12,... | collective-permute-start | bytes 516104 | tf_op jit(solution)/shard_map/ppermute | solution.py:418
  44.6 9.3 %collective-permute-start.8 = (bf16[6,2,128,128]{3,2,1,0:T(8,128)(2,1)S(1)}, bf16[6,2,128,128]{3,2,1,0:T(8,128)(2,1)S(1)}, u32[]{:S(2)}, u32[]{:S(2)}) collective-permute-start(bf16[6,2,128,128]{3,2,1,0:T(8,128)(2,1)S(1)} %slice.4), channel_id=1, source_target_pairs={{1,0},{0,1},{3,2},{2,3},{5,4},{4,5},{7,6},{6,7},{9,8},{8,9},{11,10... | collective-permute-start | bytes 1179656 | tf_op jit(solution)/shard_map/ppermute | solution.py:418

commit v5 on v4

--- a/solution.py
+++ b/solution.py
@@ -206,7 +206,7 @@
 
     def block(t):
         ox, oy = t
-        return row_refs[oy], 2 + (ox if oy == 2 else -ox)
+        return row_refs[oy], 2 + (-ox if oy == -1 else ox)
 
     def put_gram(i, g, value):
         g_ref[2 * i + g] = gram_ref[2 * i + g] + value
@@ -313,7 +313,7 @@
         ],
         in_specs=specs(2),
         scratch_shapes=sum_scratch(POINTS, (0, 1)),
-        compiler_params=pltpu.CompilerParams(vmem_limit_bytes=16 << 20),
+        compiler_params=pltpu.CompilerParams(vmem_limit_bytes=12 << 20),
         cost_estimate=pl.CostEstimate(flops=6_000_000_000, bytes_accessed=5_000_000, transcendentals=0),
         name="near_sums",
     )(frame, own, other)
@@ -327,7 +327,7 @@
         in_specs=specs(len(arrays)),
         scratch_shapes=sum_scratch(points, rows)
         + [pltpu.VMEM((2 * n, K, K), F32), pltpu.VMEM((2 * padded(n), K), F32)],
-        compiler_params=pltpu.CompilerParams(vmem_limit_bytes=28 << 20),
+        compiler_params=pltpu.CompilerParams(vmem_limit_bytes=16 << 20),
         cost_estimate=pl.CostEstimate(flops=n * FLOPS, bytes_accessed=4_000_000, transcendentals=0),
         name=name,
     )(frame, *arrays)
@@ -431,6 +431,10 @@
         at = y + 2 * (y & 1) - 1
         return (x, at) if 0 <= at < sizes[1] else None
 
+    def across(x, y):
+        at = y + 3 - 6 * (y & 1)
+        return (x, at) if 0 <= at < sizes[1] else None
+
     own = pl.pallas_call(
         pack_kernel,
         out_shape=jax.ShapeDtypeStruct((ROWS, K), BF16),
@@ -456,10 +460,12 @@
     y1 = moved(near, beyond, sizes)
     anom, mean = anomalies(ensemble)
     gram_first, gram_rest, pull = near_sums(frame, near, next_row)
-    y2 = moved(lax.optimization_barrier((next_row, pull))[0], beyond, sizes)
-    z = moved(lax.optimization_barrier((y1, pull))[0], core, sizes)
-    rest = transforms(POINTS[FIRST:], (-1, 2), 12, "rest_points", frame, y1, z, gram_rest, pull)
-    first = transforms(POINTS[:FIRST], (-2, -1), 9, "first_points", frame, y2, y1, gram_first, pull)
+    y2 = moved(near, across, sizes)
+    y1, pull = lax.optimization_barrier((y1, pull))
+    z1 = lax.cond(obs_count[0, 0] >= 0, lambda v: moved(v, core, sizes), lambda v: v, y1)
+    rest = transforms(POINTS[FIRST:], (-1, 2), 12, "rest_points", frame, y1, z1, gram_rest, pull)
+    z2 = moved(lax.optimization_barrier((y2, rest))[0], core, sizes)
+    first = transforms(POINTS[:FIRST], (-2, -1), 9, "first_points", frame, z2, y1, gram_first, pull)
     high = moved(rest[-SIDE:], core, sizes)
     return apply(frame, anom, mean, first, rest, high)
 

time: 57.5 us -> 58.6 us (1.019)
  local copies, waits for them, and re-layouts: 0.8 us -> 3.38 us
  starting transfers between devices: 20.5 us -> 18.2 us
    unnamed x4 -> x8, local copies, waits for them, and re-layouts: 0.77 us -> 3.35 us
    ppermute x9 -> x10, starting transfers between devices: 20.5 us -> 18.2 us  [moved(): return lax.ppermute(block, ('gx', 'gy'), pairs)]
    ppermute x9 -> x10, waiting for transfers between devices: 9.26 us -> 9.73 us  [moved(): return lax.ppermute(block, ('gx', 'gy'), pairs)]
  transfers between devices with their start and end apart: 9 -> 10, of which waited for: 5 -> 6; matrix products, arithmetic and copies ran while one was open for 0% -> 0% of each run, Pallas kernels for 37% -> 36%
where the time goes in v5:
time: 58.6 us; the launch traced here: 58.2 us
  Pallas kernels  26.1 us (45%)
  starting transfers between devices  18.2 us (31%)
  waiting for transfers between devices  9.73 us (17%)
  local copies, waits for them, and re-layouts  3.38 us (6%)
  between operations  0.74 us (1%)
    ppermute x10, starting transfers between devices, moved(): return lax.ppermute(block, ('gx', 'gy'), pairs)  18.2 us
    pallas_call x2, Pallas kernels, transforms(): pl.pallas_call(functools.partial(points_kernel, points, rows, batch), out...  15.4 us
    ppermute x10, waiting for transfers between devices, moved(): return lax.ppermute(block, ('gx', 'gy'), pairs)  9.73 us
    pallas_call x1, Pallas kernels, near_sums(): pl.pallas_call(near_kernel, out_shape=[jax.ShapeDtypeStruct((2 * FIRST, K...  5.44 us
    pallas_call x1, Pallas kernels, apply(): pl.pallas_call(apply_kernel, out_shape=jax.ShapeDtypeStruct(anom.shape, B...  3.37 us
    unnamed x8, local copies, waits for them, and re-layouts  3.35 us
    pallas_call x1, Pallas kernels, shards(): pl.pallas_call(pack_kernel, out_shape=jax.ShapeDtypeStruct((ROWS, K), BF1...  1.5 us
  transfers between devices with their start and end apart: 10, of which 6 were waited for; matrix products, arithmetic and copies ran while one was open for 0% of the time, Pallas kernels for 36%

profile of v5, /device:TPU:25, one launch (start us, length us, event | category | flops | bytes accessed | tf_op | source)
XLA Modules:
  0.0 58.2 jit_solution(13711152212496993088)
XLA Ops:
  0.7 1.5 %pack_slots.1.own_ref = bf16[144,128]{1,0:T(8,128)(2,1)} custom-call(s32[1,1]{1,0:T(1,128)S(6)} %copy.9.count_ref, bf16[128,128]{1,0:T(8,128)(2,1)} %bitcast.8, bf16[1,128]{1,0:T(2,128)(2,1)} %bitcast.10, bf16[1,128]{1,0:T(2,128)(2,1)} %bitcast.11, s32[2,128]{1,0:T(2,128)} %bitcast.9), custom_call_target="tpu_custom_call" | custom-call | tf_op jit(solution)/shard_map/pack_slots/pallas_call | solution.py:438
  2.1 0.7 %collective-permute-start.1 = (bf16[144,128]{1,0:T(8,128)(2,1)}, bf16[144,128]{1,0:T(8,128)(2,1)S(1)}, u32[]{:S(2)}, u32[]{:S(2)}) collective-permute-start(bf16[144,128]{1,0:T(8,128)(2,1)} %pack_slots.1.own_ref), channel_id=1, source_target_pairs={{1,0},{0,1},{3,2},{2,3},{5,4},{4,5},{7,6},{6,7},{9,8},{8,9},{11,10... | collective-permute-start | bytes 110600 | tf_op jit(solution)/shard_map/ppermute | solution.py:418
  2.8 1.1 %collective-permute-done.1.other_ref = bf16[144,128]{1,0:T(8,128)(2,1)S(1)} collective-permute-done((bf16[144,128]{1,0:T(8,128)(2,1)}, bf16[144,128]{1,0:T(8,128)(2,1)S(1)}, u32[]{:S(2)}, u32[]{:S(2)}) %collective-permute-start.1) | collective-permute-done | bytes 36896 | tf_op jit(solution)/shard_map/ppermute | solution.py:418
  3.9 0.8 %copy-done = bf16[144,128]{1,0:T(8,128)(2,1)S(1)} copy-done((bf16[144,128]{1,0:T(8,128)(2,1)S(1)}, bf16[144,128]{1,0:T(8,128)(2,1)}, u32[]{:S(2)}) %copy-start) | copy-done | bytes 36888
  4.7 6.6 %collective-permute-start.2 = (bf16[272,128]{1,0:T(8,128)(2,1)S(1)}, bf16[272,128]{1,0:T(8,128)(2,1)S(1)}, u32[]{:S(2)}, u32[]{:S(2)}) collective-permute-start(bf16[272,128]{1,0:T(8,128)(2,1)S(1)} %pair_tiles.1.pair_ref), channel_id=1, source_target_pairs={{16,0},{241,1},{18,2},{243,3},{20,4},{245,5},{22,6},{247,7},{24,8}... | collective-permute-start | bytes 208904 | tf_op jit(solution)/shard_map/ppermute | solution.py:418
  11.3 0.0 collective-permute-start.3
  11.3 1.9 %collective-permute-done.2.a_ref = bf16[272,128]{1,0:T(8,128)(2,1)S(1)} collective-permute-done((bf16[272,128]{1,0:T(8,128)(2,1)S(1)}, bf16[272,128]{1,0:T(8,128)(2,1)S(1)}, u32[]{:S(2)}, u32[]{:S(2)}) %collective-permute-start.2) | collective-permute-done | bytes 69664 | tf_op jit(solution)/shard_map/ppermute | solution.py:418
  13.2 0.0 collective-permute-start.4
  13.2 4.3 %collective-permute-done.3.b_ref = bf16[272,128]{1,0:T(8,128)(2,1)S(1)} collective-permute-done((bf16[272,128]{1,0:T(8,128)(2,1)S(1)}, bf16[272,128]{1,0:T(8,128)(2,1)S(1)}, u32[]{:S(2)}, u32[]{:S(2)}) %collective-permute-start.3) | collective-permute-done | bytes 69664 | tf_op jit(solution)/shard_map/ppermute | solution.py:418
  17.5 0.0 collective-permute-start.5
  17.5 0.1 pad_add_fusion.frame_ref.refs_0_
  17.6 0.0 collective-permute-done.4.ta_ref
  17.6 1.2 %collective-permute-done.5.tb_ref = bf16[272,128]{1,0:T(8,128)(2,1)S(1)} collective-permute-done((bf16[272,128]{1,0:T(8,128)(2,1)S(1)}, bf16[272,128]{1,0:T(8,128)(2,1)S(1)}, u32[]{:S(2)}, u32[]{:S(2)}) %collective-permute-start.5) | collective-permute-done | bytes 69664 | tf_op jit(solution)/shard_map/ppermute | solution.py:418
  18.8 6.4 %collective-permute-start.7 = (bf16[672,128]{1,0:T(8,128)(2,1)S(1)}, bf16[672,128]{1,0:T(8,128)(2,1)S(1)}, u32[]{:S(2)}, u32[]{:S(2)}) collective-permute-start(bf16[672,128]{1,0:T(8,128)(2,1)S(1)} %get-tuple-element.22.own_ref), channel_id=1, source_target_pairs={{2,1},{1,2},{4,3},{3,4},{6,5},{5,6},{8,7},{7,8},{10,9},{9,10},{12,... | collective-permute-start | bytes 516104 | tf_op jit(solution)/shard_map/ppermute | solution.py:418
  25.1 1.9 %collective-permute-start.6 = (bf16[672,128]{1,0:T(8,128)(2,1)S(1)}, bf16[672,128]{1,0:T(8,128)(2,1)S(1)}, u32[]{:S(2)}, u32[]{:S(2)}) collective-permute-start(bf16[672,128]{1,0:T(8,128)(2,1)S(1)} %get-tuple-element.22.own_ref), channel_id=1, source_target_pairs={{3,0},{5,2},{0,3},{7,4},{2,5},{9,6},{4,7},{11,8},{6,9},{13,10},{8,... | collective-permute-start | bytes 516104 | tf_op jit(solution)/shard_map/ppermute | solution.py:418
  27.1 5.4 %near_sums.1 = (f32[36,128,128]{2,1,0:T(8,128)S(1)}, f32[24,128,128]{2,1,0:T(8,128)S(1)}, f32[64,128]{1,0:T(8,128)S(1)}) custom-call(s32[3]{0:T(128)S(1)} %pad_add_fusion.frame_ref.refs_0_, bf16[672,128]{1,0:T(8,128)(2,1)S(1)} %get-tuple-element.22.own_ref, bf16[672,128]{1,0:T(8,128)(2,1)S(1)} %get-tuple-element.23.other_ref), custom_call_target="tpu_custom_call" | custom-call | flops 6000000000 | bytes 5000000 | tf_op jit(solution)/shard_map/near_sums/pallas_call | solution.py:307
  32.5 0.0 copy-start.2
  32.5 1.2 %copy-done.2 = f32[24,128,128]{2,1,0:T(8,128)} copy-done((f32[24,128,128]{2,1,0:T(8,128)}, f32[24,128,128]{2,1,0:T(8,128)S(1)}, u32[]{:S(2)}) %copy-start.2) | copy-done | bytes 1572888
  33.7 0.0 collective-permute-done.7.refs_1_.refs_2_
  33.7 2.8 %conditional.1 = (bf16[672,128]{1,0:T(8,128)(2,1)}) conditional(s32[]{:T(128)} %bitcast.7, bf16[672,128]{1,0:T(8,128)(2,1)S(1)} %collective-permute-done.7.refs_1_.refs_2_, bf16[672,128]{1,0:T(8,128)(2,1)S(1)} %collective-permute-done.7.refs_1_.refs_2_), branch_computations={%region_0.1_spmd, %region_1.2_spmd} | conditional | bytes 688176 | solution.py:465
  33.7 1.7 %collective-permute-start = (bf16[672,128]{1,0:T(8,128)(2,1)S(1)}, bf16[672,128]{1,0:T(8,128)(2,1)}, u32[]{:S(2)}, u32[]{:S(2)}) collective-permute-start(bf16[672,128]{1,0:T(8,128)(2,1)S(1)} %param.1), channel_id=1, source_target_pairs={{1,0},{0,1},{3,2},{2,3},{5,4},{4,5},{7,6},{6,7},{9,8},{8,9},{11,10... | collective-permute-start | bytes 516104 | tf_op jit(solution)/shard_map/cond/branch_1_fun/ppermute | solution.py:418
  35.4 1.2 %collective-permute-done = bf16[672,128]{1,0:T(8,128)(2,1)} collective-permute-done((bf16[672,128]{1,0:T(8,128)(2,1)S(1)}, bf16[672,128]{1,0:T(8,128)(2,1)}, u32[]{:S(2)}, u32[]{:S(2)}) %collective-permute-start) | collective-permute-done | bytes 172064 | tf_op jit(solution)/shard_map/cond/branch_1_fun/ppermute | solution.py:418
  36.6 1.4 %copy-done.3 = f32[24,128,128]{2,1,0:T(8,128)S(1)} copy-done((f32[24,128,128]{2,1,0:T(8,128)S(1)}, f32[24,128,128]{2,1,0:T(8,128)}, u32[]{:S(2)}) %copy-start.3) | copy-done | bytes 1572888
  38.0 6.4 %rest_points.1.rest_ref = bf16[12,2,128,128]{3,2,1,0:T(8,128)(2,1)S(1)} custom-call(s32[3]{0:T(128)S(1)} %pad_add_fusion.frame_ref.refs_0_, bf16[672,128]{1,0:T(8,128)(2,1)S(1)} %collective-permute-done.7.refs_1_.refs_2_, bf16[672,128]{1,0:T(8,128)(2,1)} %get-tuple-element.30.refs_2_, f32[24,128,128]{2,1,0:T(8,128)S(1)} %copy-done.3, ...), custom_call_target="tpu_custom_call" | custom-call | flops 6000000000 | bytes 4000000 | tf_op jit(solution)/shard_map/rest_points/pallas_call | solution.py:324
  44.4 0.0 collective-permute-done.6
  44.4 0.5 collective-permute-start.8
  44.8 0.4 anomalies.1
  45.3 0.4 collective-permute-start.9
  45.7 0.1 collective-permute-done.8.refs_1_
  45.9 9.0 %first_points.1.first_ref = bf16[18,2,128,128]{3,2,1,0:T(8,128)(2,1)S(1)} custom-call(s32[3]{0:T(128)S(1)} %pad_add_fusion.frame_ref.refs_0_, bf16[672,128]{1,0:T(8,128)(2,1)S(1)} %collective-permute-done.8.refs_1_, bf16[672,128]{1,0:T(8,128)(2,1)S(1)} %collective-permute-done.7.refs_1_.refs_2_, f32[36,128,128]{2,1,0:T(8,128)S(1)} %get-tuple-element.29.refs_3_, ...), custom_call_target="tpu_custom_call" | custom-call | flops 8999999488 | bytes 4000000 | tf_op jit(solution)/shard_map/first_points/pallas_call | solution.py:324
  54.9 0.0 collective-permute-done.9.high_ref
  54.9 3.4 %apply_transforms.1 = bf16[8,8,64,128]{3,2,1,0:T(8,128)(2,1)} custom-call(s32[3]{0:T(128)S(1)} %pad_add_fusion.frame_ref.refs_0_, bf16[8,8,64,128]{3,2,1,0:T(8,128)(2,1)S(1)} %get-tuple-element.20.anom_ref, f32[8,8,64,128]{3,2,1,0:T(8,128)S(1)} %get-tuple-element.21.mean_ref, bf16[18,2,128,128]{3,2,1,0:T(8,128)(2,1)S(1)} %first_points.1.first_ref, ...), custom_call_target="tpu_custom_call" | custom-call | tf_op jit(solution)/shard_map/apply_transforms/pallas_call | solution.py:400
  (7 shorter events, 0.1 us)
Async XLA Ops:
  2.1 1.8 %collective-permute-start.1 = (bf16[144,128]{1,0:T(8,128)(2,1)}, bf16[144,128]{1,0:T(8,128)(2,1)S(1)}, u32[]{:S(2)}, u32[]{:S(2)}) collective-permute-start(bf16[144,128]{1,0:T(8,128)(2,1)} %pack_slots.1.own_ref), channel_id=1, source_target_pairs={{1,0},{0,1},{3,2},{2,3},{5,4},{4,5},{7,6},{6,7},{9,8},{8,9},{11,10... | collective-permute-start | bytes 110600 | tf_op jit(solution)/shard_map/ppermute | solution.py:418
  3.9 0.8 %copy-start = (bf16[144,128]{1,0:T(8,128)(2,1)S(1)}, bf16[144,128]{1,0:T(8,128)(2,1)}, u32[]{:S(2)}) copy-start(bf16[144,128]{1,0:T(8,128)(2,1)} %pack_slots.1.own_ref) | copy-start | bytes 110596
  4.7 8.5 %collective-permute-start.2 = (bf16[272,128]{1,0:T(8,128)(2,1)S(1)}, bf16[272,128]{1,0:T(8,128)(2,1)S(1)}, u32[]{:S(2)}, u32[]{:S(2)}) collective-permute-start(bf16[272,128]{1,0:T(8,128)(2,1)S(1)} %pair_tiles.1.pair_ref), channel_id=1, source_target_pairs={{16,0},{241,1},{18,2},{243,3},{20,4},{245,5},{22,6},{247,7},{24,8}... | collective-permute-start | bytes 208904 | tf_op jit(solution)/shard_map/ppermute | solution.py:418
  11.3 6.2 %collective-permute-start.3 = (bf16[272,128]{1,0:T(8,128)(2,1)S(1)}, bf16[272,128]{1,0:T(8,128)(2,1)S(1)}, u32[]{:S(2)}, u32[]{:S(2)}) collective-permute-start(bf16[272,128]{1,0:T(8,128)(2,1)S(1)} %pair_tiles.1.pair_ref), channel_id=1, source_target_pairs={{32,0},{225,1},{34,2},{227,3},{36,4},{229,5},{38,6},{231,7},{40,8}... | collective-permute-start | bytes 208904 | tf_op jit(solution)/shard_map/ppermute | solution.py:418
  13.2 4.4 %collective-permute-start.4 = (bf16[272,128]{1,0:T(8,128)(2,1)S(1)}, bf16[272,128]{1,0:T(8,128)(2,1)S(1)}, u32[]{:S(2)}, u32[]{:S(2)}) collective-permute-start(bf16[272,128]{1,0:T(8,128)(2,1)S(1)} %collective-permute-done.2.a_ref), channel_id=1, source_target_pairs={{1,0},{0,1},{3,2},{2,3},{5,4},{4,5},{7,6},{6,7},{9,8},{8,9},{11,10... | collective-permute-start | bytes 208904 | tf_op jit(solution)/shard_map/ppermute | solution.py:418
  17.5 1.3 %collective-permute-start.5 = (bf16[272,128]{1,0:T(8,128)(2,1)S(1)}, bf16[272,128]{1,0:T(8,128)(2,1)S(1)}, u32[]{:S(2)}, u32[]{:S(2)}) collective-permute-start(bf16[272,128]{1,0:T(8,128)(2,1)S(1)} %collective-permute-done.3.b_ref), channel_id=1, source_target_pairs={{1,0},{0,1},{3,2},{2,3},{5,4},{4,5},{7,6},{6,7},{9,8},{8,9},{11,10... | collective-permute-start | bytes 208904 | tf_op jit(solution)/shard_map/ppermute | solution.py:418
  18.8 14.9 %collective-permute-start.7 = (bf16[672,128]{1,0:T(8,128)(2,1)S(1)}, bf16[672,128]{1,0:T(8,128)(2,1)S(1)}, u32[]{:S(2)}, u32[]{:S(2)}) collective-permute-start(bf16[672,128]{1,0:T(8,128)(2,1)S(1)} %get-tuple-element.22.own_ref), channel_id=1, source_target_pairs={{2,1},{1,2},{4,3},{3,4},{6,5},{5,6},{8,7},{7,8},{10,9},{9,10},{12,... | collective-permute-start | bytes 516104 | tf_op jit(solution)/shard_map/ppermute | solution.py:418
  25.1 19.2 %collective-permute-start.6 = (bf16[672,128]{1,0:T(8,128)(2,1)S(1)}, bf16[672,128]{1,0:T(8,128)(2,1)S(1)}, u32[]{:S(2)}, u32[]{:S(2)}) collective-permute-start(bf16[672,128]{1,0:T(8,128)(2,1)S(1)} %get-tuple-element.22.own_ref), channel_id=1, source_target_pairs={{3,0},{5,2},{0,3},{7,4},{2,5},{9,6},{4,7},{11,8},{6,9},{13,10},{8,... | collective-permute-start | bytes 516104 | tf_op jit(solution)/shard_map/ppermute | solution.py:418
  32.5 1.2 %copy-start.2 = (f32[24,128,128]{2,1,0:T(8,128)}, f32[24,128,128]{2,1,0:T(8,128)S(1)}, u32[]{:S(2)}) copy-start(f32[24,128,128]{2,1,0:T(8,128)S(1)} %get-tuple-element.26.refs_3_) | copy-start | bytes 4718596
  33.7 2.8 %collective-permute-start = (bf16[672,128]{1,0:T(8,128)(2,1)S(1)}, bf16[672,128]{1,0:T(8,128)(2,1)}, u32[]{:S(2)}, u32[]{:S(2)}) collective-permute-start(bf16[672,128]{1,0:T(8,128)(2,1)S(1)} %param.1), channel_id=1, source_target_pairs={{1,0},{0,1},{3,2},{2,3},{5,4},{4,5},{7,6},{6,7},{9,8},{8,9},{11,10... | collective-permute-start | bytes 516104 | tf_op jit(solution)/shard_map/cond/branch_1_fun/ppermute | solution.py:418
  36.6 1.4 %copy-start.3 = (f32[24,128,128]{2,1,0:T(8,128)S(1)}, f32[24,128,128]{2,1,0:T(8,128)}, u32[]{:S(2)}) copy-start(f32[24,128,128]{2,1,0:T(8,128)} %copy-done.2) | copy-start | bytes 4718596
  38.0 6.9 %copy-start.1 = (bf16[8,8,64,128]{3,2,1,0:T(8,128)(2,1)S(1)}, bf16[8,8,64,128]{3,2,1,0:T(8,128)(2,1)}, u32[]{:S(2)}) copy-start(bf16[8,8,64,128]{3,2,1,0:T(8,128)(2,1)} %ens_ref.1) | copy-start | bytes 3145732
  44.4 1.5 %collective-permute-start.8 = (bf16[672,128]{1,0:T(8,128)(2,1)S(1)}, bf16[672,128]{1,0:T(8,128)(2,1)S(1)}, u32[]{:S(2)}, u32[]{:S(2)}) collective-permute-start(bf16[672,128]{1,0:T(8,128)(2,1)S(1)} %collective-permute-done.6), channel_id=1, source_target_pairs={{1,0},{0,1},{3,2},{2,3},{5,4},{4,5},{7,6},{6,7},{9,8},{8,9},{11,10... | collective-permute-start | bytes 516104 | tf_op jit(solution)/shard_map/ppermute | solution.py:418
  45.3 9.6 %collective-permute-start.9 = (bf16[6,2,128,128]{3,2,1,0:T(8,128)(2,1)S(1)}, bf16[6,2,128,128]{3,2,1,0:T(8,128)(2,1)S(1)}, u32[]{:S(2)}, u32[]{:S(2)}) collective-permute-start(bf16[6,2,128,128]{3,2,1,0:T(8,128)(2,1)S(1)} %slice.4), channel_id=1, source_target_pairs={{1,0},{0,1},{3,2},{2,3},{5,4},{4,5},{7,6},{6,7},{9,8},{8,9},{11,10... | collective-permute-start | bytes 1179656 | tf_op jit(solution)/shard_map/ppermute | solution.py:418

commit v6 on v5

--- a/solution.py
+++ b/solution.py
@@ -17,8 +17,10 @@
 ROWS = K + 16
 PAIR = 2 * K + 16
 WIDE = 5 * K + 32
+ORDER = (-2, 2, -1, 0, 1)
+EDGES = 2
 SLOTS = 2
-FLOPS = 500_000_000
+REST = 1_000_000
 LAG = 10
 
 NT = (((1,), (1,)), ((), ()))
@@ -93,7 +95,7 @@
 
 def rows_kernel(pair_ref, a_ref, b_ref, ta_ref, tb_ref, *out_refs):
     for row, out_ref in enumerate(out_refs):
-        parts = [(tb_ref, 1 - row), (ta_ref, 1 - row), (pair_ref, row), (a_ref, row), (b_ref, row)]
+        parts = [(tb_ref, 1 - row), (b_ref, row), (ta_ref, 1 - row), (pair_ref, row), (a_ref, row)]
         meta = []
         for k, (ref, at) in enumerate(parts):
             out_ref[k * K : k * K + K, :] = ref[at * K : at * K + K, :]
@@ -134,14 +136,16 @@
     n = padded(len(points))
 
     def anom(t):
-        ref, k = block(t)
+        ref, ox = block(t)
+        k = ORDER.index(ox) - (WIDE - ref.shape[0]) // K
         return ref[k * K : k * K + K, :]
 
     metas = {}
     for t in seen:
-        ref, k = block(t)
+        ref, ox = block(t)
         if id(ref) not in metas:
-            metas[id(ref)] = ref[5 * K : WIDE, :].astype(F32)
+            metas[id(ref)] = ref[ref.shape[0] - 32 :, :].astype(F32)
+        k = ORDER.index(ox)
         meta = metas[id(ref)][k * META : k * META + META]
         w = point_weights(meta, frame_ref, t[0], t[1], points)
         lanes = slice(place[t] * K, place[t] * K + K)
@@ -181,7 +185,7 @@
 
 def near_kernel(frame_ref, own_ref, other_ref, first_ref, rest_ref, pull_ref, *scratch):
     def block(t):
-        return (own_ref, other_ref)[t[1]], 2 + t[0]
+        return (own_ref, other_ref)[t[1]], t[0]
 
     def put_gram(i, g, value):
         if i < FIRST:
@@ -206,7 +210,7 @@
 
     def block(t):
         ox, oy = t
-        return row_refs[oy], 2 + (-ox if oy == -1 else ox)
+        return row_refs[oy], -ox if oy == -1 else ox
 
     def put_gram(i, g, value):
         g_ref[2 * i + g] = gram_ref[2 * i + g] + value
@@ -313,13 +317,13 @@
         ],
         in_specs=specs(2),
         scratch_shapes=sum_scratch(POINTS, (0, 1)),
-        compiler_params=pltpu.CompilerParams(vmem_limit_bytes=12 << 20),
+        compiler_params=pltpu.CompilerParams(vmem_limit_bytes=16 << 20),
         cost_estimate=pl.CostEstimate(flops=6_000_000_000, bytes_accessed=5_000_000, transcendentals=0),
         name="near_sums",
     )(frame, own, other)
 
 
-def transforms(points, rows, batch, name, frame, *arrays):
+def transforms(points, rows, batch, flops, name, frame, *arrays):
     n = len(points)
     return pl.pallas_call(
         functools.partial(points_kernel, points, rows, batch),
@@ -327,8 +331,8 @@
         in_specs=specs(len(arrays)),
         scratch_shapes=sum_scratch(points, rows)
         + [pltpu.VMEM((2 * n, K, K), F32), pltpu.VMEM((2 * padded(n), K), F32)],
-        compiler_params=pltpu.CompilerParams(vmem_limit_bytes=16 << 20),
-        cost_estimate=pl.CostEstimate(flops=n * FLOPS, bytes_accessed=4_000_000, transcendentals=0),
+        compiler_params=pltpu.CompilerParams(vmem_limit_bytes=28 << 20),
+        cost_estimate=pl.CostEstimate(flops=flops, bytes_accessed=flops // 1000, transcendentals=0),
         name=name,
     )(frame, *arrays)
 
@@ -461,11 +465,10 @@
     anom, mean = anomalies(ensemble)
     gram_first, gram_rest, pull = near_sums(frame, near, next_row)
     y2 = moved(near, across, sizes)
-    y1, pull = lax.optimization_barrier((y1, pull))
-    z1 = lax.cond(obs_count[0, 0] >= 0, lambda v: moved(v, core, sizes), lambda v: v, y1)
-    rest = transforms(POINTS[FIRST:], (-1, 2), 12, "rest_points", frame, y1, z1, gram_rest, pull)
+    z1 = moved(lax.optimization_barrier((y1, pull))[0][EDGES * K :], core, sizes)
+    rest = transforms(POINTS[FIRST:], (-1, 2), 12, REST, "rest_points", frame, y1, z1, gram_rest, pull)
     z2 = moved(lax.optimization_barrier((y2, rest))[0], core, sizes)
-    first = transforms(POINTS[:FIRST], (-2, -1), 9, "first_points", frame, z2, y1, gram_first, pull)
+    first = transforms(POINTS[:FIRST], (-2, -1), 9, 9_000_000_000, "first_points", frame, z2, y1, gram_first, pull)
     high = moved(rest[-SIDE:], core, sizes)
     return apply(frame, anom, mean, first, rest, high)
 

time: 58.6 us -> 55.8 us (0.952)
  local copies, waits for them, and re-layouts: 3.38 us -> 0.81 us
    unnamed x8 -> x4, local copies, waits for them, and re-layouts: 3.35 us -> 0.77 us
  transfers between devices with their start and end apart: 10 -> 10, of which waited for: 6 -> 6; matrix products, arithmetic and copies ran while one was open for 0% -> 0% of each run, Pallas kernels for 36% -> 38%
where the time goes in v6:
time: 55.8 us; the launch traced here: 55.6 us
  Pallas kernels  26 us (47%)
  starting transfers between devices  18.5 us (33%)
  waiting for transfers between devices  9.5 us (17%)
  local copies, waits for them, and re-layouts  0.81 us (1%)
  between operations  0.75 us (1%)
    ppermute x10, starting transfers between devices, moved(): return lax.ppermute(block, ('gx', 'gy'), pairs)  18.5 us
    pallas_call x2, Pallas kernels, transforms(): pl.pallas_call(functools.partial(points_kernel, points, rows, batch), out...  15 us
    ppermute x10, waiting for transfers between devices, moved(): return lax.ppermute(block, ('gx', 'gy'), pairs)  9.5 us
    pallas_call x1, Pallas kernels, near_sums(): pl.pallas_call(near_kernel, out_shape=[jax.ShapeDtypeStruct((2 * FIRST, K...  5.57 us
    pallas_call x1, Pallas kernels, apply(): pl.pallas_call(apply_kernel, out_shape=jax.ShapeDtypeStruct(anom.shape, B...  3.45 us
    pallas_call x1, Pallas kernels, shards(): pl.pallas_call(pack_kernel, out_shape=jax.ShapeDtypeStruct((ROWS, K), BF1...  1.5 us
  transfers between devices with their start and end apart: 10, of which 6 were waited for; matrix products, arithmetic and copies ran while one was open for 0% of the time, Pallas kernels for 38%

profile of v6, /device:TPU:25, one launch (start us, length us, event | category | flops | bytes accessed | tf_op | source)
XLA Modules:
  0.0 55.6 jit_solution(1122782903252141397)
XLA Ops:
  0.7 1.5 %pack_slots.1.own_ref = bf16[144,128]{1,0:T(8,128)(2,1)} custom-call(s32[1,1]{1,0:T(1,128)S(6)} %copy.7.count_ref, bf16[128,128]{1,0:T(8,128)(2,1)} %bitcast.7, bf16[1,128]{1,0:T(2,128)(2,1)} %bitcast.9, bf16[1,128]{1,0:T(2,128)(2,1)} %bitcast.10, s32[2,128]{1,0:T(2,128)} %bitcast.8), custom_call_target="tpu_custom_call" | custom-call | tf_op jit(solution)/shard_map/pack_slots/pallas_call | solution.py:442
  2.1 0.7 %collective-permute-start = (bf16[144,128]{1,0:T(8,128)(2,1)}, bf16[144,128]{1,0:T(8,128)(2,1)S(1)}, u32[]{:S(2)}, u32[]{:S(2)}) collective-permute-start(bf16[144,128]{1,0:T(8,128)(2,1)} %pack_slots.1.own_ref), channel_id=1, source_target_pairs={{1,0},{0,1},{3,2},{2,3},{5,4},{4,5},{7,6},{6,7},{9,8},{8,9},{11,10... | collective-permute-start | bytes 110600 | tf_op jit(solution)/shard_map/ppermute | solution.py:422
  2.8 1.1 %collective-permute-done.other_ref = bf16[144,128]{1,0:T(8,128)(2,1)S(1)} collective-permute-done((bf16[144,128]{1,0:T(8,128)(2,1)}, bf16[144,128]{1,0:T(8,128)(2,1)S(1)}, u32[]{:S(2)}, u32[]{:S(2)}) %collective-permute-start) | collective-permute-done | bytes 36896 | tf_op jit(solution)/shard_map/ppermute | solution.py:422
  3.9 0.0 copy-start
  3.9 0.8 %copy-done = bf16[144,128]{1,0:T(8,128)(2,1)S(1)} copy-done((bf16[144,128]{1,0:T(8,128)(2,1)S(1)}, bf16[144,128]{1,0:T(8,128)(2,1)}, u32[]{:S(2)}) %copy-start) | copy-done | bytes 36888
  4.7 6.6 %collective-permute-start.1 = (bf16[272,128]{1,0:T(8,128)(2,1)S(1)}, bf16[272,128]{1,0:T(8,128)(2,1)S(1)}, u32[]{:S(2)}, u32[]{:S(2)}) collective-permute-start(bf16[272,128]{1,0:T(8,128)(2,1)S(1)} %pair_tiles.1.pair_ref), channel_id=1, source_target_pairs={{16,0},{241,1},{18,2},{243,3},{20,4},{245,5},{22,6},{247,7},{24,8}... | collective-permute-start | bytes 208904 | tf_op jit(solution)/shard_map/ppermute | solution.py:422
  11.3 0.0 collective-permute-start.2
  11.3 1.9 %collective-permute-done.1.a_ref = bf16[272,128]{1,0:T(8,128)(2,1)S(1)} collective-permute-done((bf16[272,128]{1,0:T(8,128)(2,1)S(1)}, bf16[272,128]{1,0:T(8,128)(2,1)S(1)}, u32[]{:S(2)}, u32[]{:S(2)}) %collective-permute-start.1) | collective-permute-done | bytes 69664 | tf_op jit(solution)/shard_map/ppermute | solution.py:422
  13.2 0.0 collective-permute-start.3
  13.2 4.3 %collective-permute-done.2.b_ref = bf16[272,128]{1,0:T(8,128)(2,1)S(1)} collective-permute-done((bf16[272,128]{1,0:T(8,128)(2,1)S(1)}, bf16[272,128]{1,0:T(8,128)(2,1)S(1)}, u32[]{:S(2)}, u32[]{:S(2)}) %collective-permute-start.2) | collective-permute-done | bytes 69664 | tf_op jit(solution)/shard_map/ppermute | solution.py:422
  17.5 0.0 collective-permute-start.4
  17.5 0.1 pad_add_fusion.frame_ref.refs_0_
  17.6 0.0 collective-permute-done.3.ta_ref
  17.6 1.2 %collective-permute-done.4.tb_ref = bf16[272,128]{1,0:T(8,128)(2,1)S(1)} collective-permute-done((bf16[272,128]{1,0:T(8,128)(2,1)S(1)}, bf16[272,128]{1,0:T(8,128)(2,1)S(1)}, u32[]{:S(2)}, u32[]{:S(2)}) %collective-permute-start.4) | collective-permute-done | bytes 69664 | tf_op jit(solution)/shard_map/ppermute | solution.py:422
  18.8 6.4 %collective-permute-start.6 = (bf16[672,128]{1,0:T(8,128)(2,1)S(1)}, bf16[672,128]{1,0:T(8,128)(2,1)S(1)}, u32[]{:S(2)}, u32[]{:S(2)}) collective-permute-start(bf16[672,128]{1,0:T(8,128)(2,1)S(1)} %get-tuple-element.16.own_ref), channel_id=1, source_target_pairs={{2,1},{1,2},{4,3},{3,4},{6,5},{5,6},{8,7},{7,8},{10,9},{9,10},{12,... | collective-permute-start | bytes 516104 | tf_op jit(solution)/shard_map/ppermute | solution.py:422
  25.1 1.9 %collective-permute-start.5 = (bf16[672,128]{1,0:T(8,128)(2,1)S(1)}, bf16[672,128]{1,0:T(8,128)(2,1)S(1)}, u32[]{:S(2)}, u32[]{:S(2)}) collective-permute-start(bf16[672,128]{1,0:T(8,128)(2,1)S(1)} %get-tuple-element.16.own_ref), channel_id=1, source_target_pairs={{3,0},{5,2},{0,3},{7,4},{2,5},{9,6},{4,7},{11,8},{6,9},{13,10},{8,... | collective-permute-start | bytes 516104 | tf_op jit(solution)/shard_map/ppermute | solution.py:422
  27.1 5.6 %near_sums.1 = (f32[36,128,128]{2,1,0:T(8,128)S(1)}, f32[24,128,128]{2,1,0:T(8,128)S(1)}, f32[64,128]{1,0:T(8,128)S(1)}) custom-call(s32[3]{0:T(128)S(1)} %pad_add_fusion.frame_ref.refs_0_, bf16[672,128]{1,0:T(8,128)(2,1)S(1)} %get-tuple-element.16.own_ref, bf16[672,128]{1,0:T(8,128)(2,1)S(1)} %get-tuple-element.17.other_ref), custom_call_target="tpu_custom_call" | custom-call | flops 6000000000 | bytes 5000000 | tf_op jit(solution)/shard_map/near_sums/pallas_call | solution.py:311
  32.6 0.0 copy-start.1
  32.7 0.0 collective-permute-done.6.refs_1_.refs_2_
  32.7 2.0 %collective-permute-start.7 = (bf16[416,128]{1,0:T(8,128)(2,1)S(1)}, bf16[416,128]{1,0:T(8,128)(2,1)S(1)}, u32[]{:S(2)}, u32[]{:S(2)}) collective-permute-start(bf16[416,128]{1,0:T(8,128)(2,1)S(1)} %slice.6), channel_id=1, source_target_pairs={{1,0},{0,1},{3,2},{2,3},{5,4},{4,5},{7,6},{6,7},{9,8},{8,9},{11,10... | collective-permute-start | bytes 319496 | tf_op jit(solution)/shard_map/ppermute | solution.py:422
  34.6 1.0 %collective-permute-done.7.refs_2_ = bf16[416,128]{1,0:T(8,128)(2,1)S(1)} collective-permute-done((bf16[416,128]{1,0:T(8,128)(2,1)S(1)}, bf16[416,128]{1,0:T(8,128)(2,1)S(1)}, u32[]{:S(2)}, u32[]{:S(2)}) %collective-permute-start.7) | collective-permute-done | bytes 106528 | tf_op jit(solution)/shard_map/ppermute | solution.py:422
  35.6 6.0 %rest_points.1.rest_ref = bf16[12,2,128,128]{3,2,1,0:T(8,128)(2,1)S(1)} custom-call(s32[3]{0:T(128)S(1)} %pad_add_fusion.frame_ref.refs_0_, bf16[672,128]{1,0:T(8,128)(2,1)S(1)} %collective-permute-done.6.refs_1_.refs_2_, bf16[416,128]{1,0:T(8,128)(2,1)S(1)} %collective-permute-done.7.refs_2_, f32[24,128,128]{2,1,0:T(8,128)S(1)} %get-tuple-element.20.refs_3_, ...), custom_call_target="tpu_custom_call" | custom-call | flops 1000000 | bytes 1000 | tf_op jit(solution)/shard_map/rest_points/pallas_call | solution.py:328
  41.6 0.0 collective-permute-done.5
  41.6 0.4 collective-permute-start.8
  42.1 0.0 copy-done.1
  42.1 0.4 anomalies.1
  42.5 0.5 collective-permute-start.9
  43.0 0.1 collective-permute-done.8.refs_1_
  43.1 9.0 %first_points.1.first_ref = bf16[18,2,128,128]{3,2,1,0:T(8,128)(2,1)S(1)} custom-call(s32[3]{0:T(128)S(1)} %pad_add_fusion.frame_ref.refs_0_, bf16[672,128]{1,0:T(8,128)(2,1)S(1)} %collective-permute-done.8.refs_1_, bf16[672,128]{1,0:T(8,128)(2,1)S(1)} %collective-permute-done.6.refs_1_.refs_2_, f32[36,128,128]{2,1,0:T(8,128)S(1)} %get-tuple-element.22.refs_3_, ...), custom_call_target="tpu_custom_call" | custom-call | flops 8999999488 | bytes 9000000 | tf_op jit(solution)/shard_map/first_points/pallas_call | solution.py:328
  52.1 0.0 collective-permute-done.9.high_ref
  52.1 3.4 %apply_transforms.1 = bf16[8,8,64,128]{3,2,1,0:T(8,128)(2,1)} custom-call(s32[3]{0:T(128)S(1)} %pad_add_fusion.frame_ref.refs_0_, bf16[8,8,64,128]{3,2,1,0:T(8,128)(2,1)S(1)} %get-tuple-element.14.anom_ref, f32[8,8,64,128]{3,2,1,0:T(8,128)S(1)} %get-tuple-element.15.mean_ref, bf16[18,2,128,128]{3,2,1,0:T(8,128)(2,1)S(1)} %first_points.1.first_ref, ...), custom_call_target="tpu_custom_call" | custom-call | tf_op jit(solution)/shard_map/apply_transforms/pallas_call | solution.py:404
  (4 shorter events, 0.1 us)
Async XLA Ops:
  2.1 1.8 %collective-permute-start = (bf16[144,128]{1,0:T(8,128)(2,1)}, bf16[144,128]{1,0:T(8,128)(2,1)S(1)}, u32[]{:S(2)}, u32[]{:S(2)}) collective-permute-start(bf16[144,128]{1,0:T(8,128)(2,1)} %pack_slots.1.own_ref), channel_id=1, source_target_pairs={{1,0},{0,1},{3,2},{2,3},{5,4},{4,5},{7,6},{6,7},{9,8},{8,9},{11,10... | collective-permute-start | bytes 110600 | tf_op jit(solution)/shard_map/ppermute | solution.py:422
  3.9 0.8 %copy-start = (bf16[144,128]{1,0:T(8,128)(2,1)S(1)}, bf16[144,128]{1,0:T(8,128)(2,1)}, u32[]{:S(2)}) copy-start(bf16[144,128]{1,0:T(8,128)(2,1)} %pack_slots.1.own_ref) | copy-start | bytes 110596
  4.7 8.5 %collective-permute-start.1 = (bf16[272,128]{1,0:T(8,128)(2,1)S(1)}, bf16[272,128]{1,0:T(8,128)(2,1)S(1)}, u32[]{:S(2)}, u32[]{:S(2)}) collective-permute-start(bf16[272,128]{1,0:T(8,128)(2,1)S(1)} %pair_tiles.1.pair_ref), channel_id=1, source_target_pairs={{16,0},{241,1},{18,2},{243,3},{20,4},{245,5},{22,6},{247,7},{24,8}... | collective-permute-start | bytes 208904 | tf_op jit(solution)/shard_map/ppermute | solution.py:422
  11.3 6.2 %collective-permute-start.2 = (bf16[272,128]{1,0:T(8,128)(2,1)S(1)}, bf16[272,128]{1,0:T(8,128)(2,1)S(1)}, u32[]{:S(2)}, u32[]{:S(2)}) collective-permute-start(bf16[272,128]{1,0:T(8,128)(2,1)S(1)} %pair_tiles.1.pair_ref), channel_id=1, source_target_pairs={{32,0},{225,1},{34,2},{227,3},{36,4},{229,5},{38,6},{231,7},{40,8}... | collective-permute-start | bytes 208904 | tf_op jit(solution)/shard_map/ppermute | solution.py:422
  13.2 4.4 %collective-permute-start.3 = (bf16[272,128]{1,0:T(8,128)(2,1)S(1)}, bf16[272,128]{1,0:T(8,128)(2,1)S(1)}, u32[]{:S(2)}, u32[]{:S(2)}) collective-permute-start(bf16[272,128]{1,0:T(8,128)(2,1)S(1)} %collective-permute-done.1.a_ref), channel_id=1, source_target_pairs={{1,0},{0,1},{3,2},{2,3},{5,4},{4,5},{7,6},{6,7},{9,8},{8,9},{11,10... | collective-permute-start | bytes 208904 | tf_op jit(solution)/shard_map/ppermute | solution.py:422
  17.5 1.3 %collective-permute-start.4 = (bf16[272,128]{1,0:T(8,128)(2,1)S(1)}, bf16[272,128]{1,0:T(8,128)(2,1)S(1)}, u32[]{:S(2)}, u32[]{:S(2)}) collective-permute-start(bf16[272,128]{1,0:T(8,128)(2,1)S(1)} %collective-permute-done.2.b_ref), channel_id=1, source_target_pairs={{1,0},{0,1},{3,2},{2,3},{5,4},{4,5},{7,6},{6,7},{9,8},{8,9},{11,10... | collective-permute-start | bytes 208904 | tf_op jit(solution)/shard_map/ppermute | solution.py:422
  18.8 13.9 %collective-permute-start.6 = (bf16[672,128]{1,0:T(8,128)(2,1)S(1)}, bf16[672,128]{1,0:T(8,128)(2,1)S(1)}, u32[]{:S(2)}, u32[]{:S(2)}) collective-permute-start(bf16[672,128]{1,0:T(8,128)(2,1)S(1)} %get-tuple-element.16.own_ref), channel_id=1, source_target_pairs={{2,1},{1,2},{4,3},{3,4},{6,5},{5,6},{8,7},{7,8},{10,9},{9,10},{12,... | collective-permute-start | bytes 516104 | tf_op jit(solution)/shard_map/ppermute | solution.py:422
  25.1 16.5 %collective-permute-start.5 = (bf16[672,128]{1,0:T(8,128)(2,1)S(1)}, bf16[672,128]{1,0:T(8,128)(2,1)S(1)}, u32[]{:S(2)}, u32[]{:S(2)}) collective-permute-start(bf16[672,128]{1,0:T(8,128)(2,1)S(1)} %get-tuple-element.16.own_ref), channel_id=1, source_target_pairs={{3,0},{5,2},{0,3},{7,4},{2,5},{9,6},{4,7},{11,8},{6,9},{13,10},{8,... | collective-permute-start | bytes 516104 | tf_op jit(solution)/shard_map/ppermute | solution.py:422
  32.6 9.4 %copy-start.1 = (bf16[8,8,64,128]{3,2,1,0:T(8,128)(2,1)S(1)}, bf16[8,8,64,128]{3,2,1,0:T(8,128)(2,1)}, u32[]{:S(2)}) copy-start(bf16[8,8,64,128]{3,2,1,0:T(8,128)(2,1)} %ens_ref.1) | copy-start | bytes 3145732
  32.7 2.9 %collective-permute-start.7 = (bf16[416,128]{1,0:T(8,128)(2,1)S(1)}, bf16[416,128]{1,0:T(8,128)(2,1)S(1)}, u32[]{:S(2)}, u32[]{:S(2)}) collective-permute-start(bf16[416,128]{1,0:T(8,128)(2,1)S(1)} %slice.6), channel_id=1, source_target_pairs={{1,0},{0,1},{3,2},{2,3},{5,4},{4,5},{7,6},{6,7},{9,8},{8,9},{11,10... | collective-permute-start | bytes 319496 | tf_op jit(solution)/shard_map/ppermute | solution.py:422
  41.6 1.5 %collective-permute-start.8 = (bf16[672,128]{1,0:T(8,128)(2,1)S(1)}, bf16[672,128]{1,0:T(8,128)(2,1)S(1)}, u32[]{:S(2)}, u32[]{:S(2)}) collective-permute-start(bf16[672,128]{1,0:T(8,128)(2,1)S(1)} %collective-permute-done.5), channel_id=1, source_target_pairs={{1,0},{0,1},{3,2},{2,3},{5,4},{4,5},{7,6},{6,7},{9,8},{8,9},{11,10... | collective-permute-start | bytes 516104 | tf_op jit(solution)/shard_map/ppermute | solution.py:422
  42.5 9.6 %collective-permute-start.9 = (bf16[6,2,128,128]{3,2,1,0:T(8,128)(2,1)S(1)}, bf16[6,2,128,128]{3,2,1,0:T(8,128)(2,1)S(1)}, u32[]{:S(2)}, u32[]{:S(2)}) collective-permute-start(bf16[6,2,128,128]{3,2,1,0:T(8,128)(2,1)S(1)} %slice.8), channel_id=1, source_target_pairs={{1,0},{0,1},{3,2},{2,3},{5,4},{4,5},{7,6},{6,7},{9,8},{8,9},{11,10... | collective-permute-start | bytes 1179656 | tf_op jit(solution)/shard_map/ppermute | solution.py:422

commit v7 on v6

--- a/solution.py
+++ b/solution.py
@@ -93,13 +93,26 @@
     out_ref[2 * K : PAIR, :] = jnp.concatenate(meta + [jnp.zeros((8, K), F32)], 0).astype(BF16)
 
 
-def rows_kernel(pair_ref, a_ref, b_ref, ta_ref, tb_ref, *out_refs):
+def rows_kernel(frame_ref, pair_ref, a_ref, b_ref, ta_ref, tb_ref, *out_refs):
+    same = frame_ref[3] != 0
     for row, out_ref in enumerate(out_refs):
-        parts = [(tb_ref, 1 - row), (b_ref, row), (ta_ref, 1 - row), (pair_ref, row), (a_ref, row)]
+        ends = [(tb_ref, 1 - row), (b_ref, row)]
+        middle = [(ta_ref, 1 - row), (pair_ref, row), (a_ref, row)]
+
+        def tile(part):
+            return part[0][part[1] * K : part[1] * K + K, :]
+
+        def info(part):
+            at = part[1] * META
+            return part[0][2 * K : PAIR, :].astype(F32)[at : at + META]
+
         meta = []
-        for k, (ref, at) in enumerate(parts):
-            out_ref[k * K : k * K + K, :] = ref[at * K : at * K + K, :]
-            meta.append(ref[2 * K : PAIR, :].astype(F32)[at * META : at * META + META])
+        for k, (left, right) in enumerate((ends, ends[::-1])):
+            out_ref[k * K : k * K + K, :] = jnp.where(same, tile(left), tile(right))
+            meta.append(jnp.where(same, info(left), info(right)))
+        for k, part in enumerate(middle, 2):
+            out_ref[k * K : k * K + K, :] = tile(part)
+            meta.append(info(part))
         meta.append(jnp.zeros((12, K), F32))
         out_ref[5 * K : WIDE, :] = jnp.concatenate(meta, 0).astype(BF16)
 
@@ -296,11 +309,11 @@
     return [pl.BlockSpec(memory_space=pltpu.SMEM)] * scalars + [pl.BlockSpec(memory_space=pltpu.VMEM)] * n
 
 
-def joined(kernel, rows, name, *blocks):
+def joined(kernel, rows, name, *blocks, scalars=0):
     return pl.pallas_call(
         kernel,
         out_shape=[jax.ShapeDtypeStruct((n, K), BF16) for n in rows],
-        in_specs=specs(len(blocks), 0),
+        in_specs=specs(len(blocks) - scalars, scalars),
         compiler_params=pltpu.CompilerParams(vmem_limit_bytes=2 << 20),
         name=name,
     )(*blocks)
@@ -428,8 +441,11 @@
     def core(x, y):
         return x, y ^ 1
 
-    def side(distance):
-        return lambda x, y: (x + distance * (1 - 2 * ((x ^ y) & 1)), y)
+    def side(x, y):
+        return x + 1 - 2 * ((x ^ y) & 1), y
+
+    def second(x, y):
+        return x - 2 + 4 * (((x >> 1) ^ y) & 1), y
 
     def beyond(x, y):
         at = y + 2 * (y & 1) - 1
@@ -453,14 +469,14 @@
     )
     col, row = lax.axis_index("gx"), lax.axis_index("gy")
     edge = jnp.where((row == 0) | (row == sizes[1] - 1), 1, 0)
-    frame = jnp.stack([(col ^ row) & 1, row & 1, edge]).astype(jnp.int32)
+    frame = jnp.stack([(col ^ row) & 1, row & 1, edge, ((col >> 1) ^ col) & 1]).astype(jnp.int32)
 
     (pair,) = joined(pair_kernel, [PAIR], "pair_tiles", own, moved(own, core, sizes))
-    a = moved(pair, side(1), sizes)
-    b = moved(pair, side(2), sizes)
+    a = moved(pair, side, sizes)
+    b = moved(pair, second, sizes)
     ta = moved(a, core, sizes)
     tb = moved(b, core, sizes)
-    near, next_row = joined(rows_kernel, [WIDE, WIDE], "two_rows", pair, a, b, ta, tb)
+    near, next_row = joined(rows_kernel, [WIDE, WIDE], "two_rows", frame, pair, a, b, ta, tb, scalars=1)
     y1 = moved(near, beyond, sizes)
     anom, mean = anomalies(ensemble)
     gram_first, gram_rest, pull = near_sums(frame, near, next_row)

time: 55.8 us -> 56.8 us (1.018)
  starting transfers between devices: 18.5 us -> 21 us
  waiting for transfers between devices: 9.5 us -> 7.34 us
    ppermute x10, starting transfers between devices: 18.5 us -> 21 us  [moved(): return lax.ppermute(block, ('gx', 'gy'), pairs)]
    ppermute x10, waiting for transfers between devices: 9.5 us -> 7.34 us  [moved(): return lax.ppermute(block, ('gx', 'gy'), pairs)]
  transfers between devices with their start and end apart: 10 -> 10, of which waited for: 6 -> 6; matrix products, arithmetic and copies ran while one was open for 0% -> 0% of each run, Pallas kernels for 38% -> 37%
where the time goes in v7:
time: 56.8 us; the launch traced here: 56.5 us
  Pallas kernels  26.5 us (47%)
  starting transfers between devices  21 us (37%)
  waiting for transfers between devices  7.34 us (13%)
  local copies, waits for them, and re-layouts  0.81 us (1%)
  between operations  0.76 us (1%)
    ppermute x10, starting transfers between devices, moved(): return lax.ppermute(block, ('gx', 'gy'), pairs)  21 us
    pallas_call x2, Pallas kernels, transforms(): pl.pallas_call(functools.partial(points_kernel, points, rows, batch), out...  15 us
    ppermute x10, waiting for transfers between devices, moved(): return lax.ppermute(block, ('gx', 'gy'), pairs)  7.34 us
    pallas_call x1, Pallas kernels, near_sums(): pl.pallas_call(near_kernel, out_shape=[jax.ShapeDtypeStruct((2 * FIRST, K...  5.59 us
    pallas_call x1, Pallas kernels, apply(): pl.pallas_call(apply_kernel, out_shape=jax.ShapeDtypeStruct(anom.shape, B...  3.45 us
    pallas_call x1, Pallas kernels, shards(): pl.pallas_call(pack_kernel, out_shape=jax.ShapeDtypeStruct((ROWS, K), BF1...  1.5 us
  transfers between devices with their start and end apart: 10, of which 6 were waited for; matrix products, arithmetic and copies ran while one was open for 0% of the time, Pallas kernels for 37%

profile of v7, /device:TPU:25, one launch (start us, length us, event | category | flops | bytes accessed | tf_op | source)
XLA Modules:
  0.0 56.5 jit_solution(17409797130388671871)
XLA Ops:
  0.7 1.5 %pack_slots.1.own_ref = bf16[144,128]{1,0:T(8,128)(2,1)} custom-call(s32[1,1]{1,0:T(1,128)S(6)} %copy.7.count_ref, bf16[128,128]{1,0:T(8,128)(2,1)} %bitcast.8, bf16[1,128]{1,0:T(2,128)(2,1)} %bitcast.10, bf16[1,128]{1,0:T(2,128)(2,1)} %bitcast.11, s32[2,128]{1,0:T(2,128)} %bitcast.9), custom_call_target="tpu_custom_call" | custom-call | tf_op jit(solution)/shard_map/pack_slots/pallas_call | solution.py:458
  2.1 0.7 %collective-permute-start = (bf16[144,128]{1,0:T(8,128)(2,1)}, bf16[144,128]{1,0:T(8,128)(2,1)S(1)}, u32[]{:S(2)}, u32[]{:S(2)}) collective-permute-start(bf16[144,128]{1,0:T(8,128)(2,1)} %pack_slots.1.own_ref), channel_id=1, source_target_pairs={{1,0},{0,1},{3,2},{2,3},{5,4},{4,5},{7,6},{6,7},{9,8},{8,9},{11,10... | collective-permute-start | bytes 110600 | tf_op jit(solution)/shard_map/ppermute | solution.py:435
  2.8 1.1 %collective-permute-done.other_ref = bf16[144,128]{1,0:T(8,128)(2,1)S(1)} collective-permute-done((bf16[144,128]{1,0:T(8,128)(2,1)}, bf16[144,128]{1,0:T(8,128)(2,1)S(1)}, u32[]{:S(2)}, u32[]{:S(2)}) %collective-permute-start) | collective-permute-done | bytes 36896 | tf_op jit(solution)/shard_map/ppermute | solution.py:435
  3.9 0.0 copy-start
  3.9 0.8 %copy-done = bf16[144,128]{1,0:T(8,128)(2,1)S(1)} copy-done((bf16[144,128]{1,0:T(8,128)(2,1)S(1)}, bf16[144,128]{1,0:T(8,128)(2,1)}, u32[]{:S(2)}) %copy-start) | copy-done | bytes 36888
  4.7 6.6 %collective-permute-start.1 = (bf16[272,128]{1,0:T(8,128)(2,1)S(1)}, bf16[272,128]{1,0:T(8,128)(2,1)S(1)}, u32[]{:S(2)}, u32[]{:S(2)}) collective-permute-start(bf16[272,128]{1,0:T(8,128)(2,1)S(1)} %pair_tiles.1.pair_ref), channel_id=1, source_target_pairs={{16,0},{241,1},{18,2},{243,3},{20,4},{245,5},{22,6},{247,7},{24,8}... | collective-permute-start | bytes 208904 | tf_op jit(solution)/shard_map/ppermute | solution.py:435
  11.3 0.0 collective-permute-start.2
  11.3 1.9 %collective-permute-done.1.a_ref = bf16[272,128]{1,0:T(8,128)(2,1)S(1)} collective-permute-done((bf16[272,128]{1,0:T(8,128)(2,1)S(1)}, bf16[272,128]{1,0:T(8,128)(2,1)S(1)}, u32[]{:S(2)}, u32[]{:S(2)}) %collective-permute-start.1) | collective-permute-done | bytes 69664 | tf_op jit(solution)/shard_map/ppermute | solution.py:435
  13.2 0.0 collective-permute-start.3
  13.2 2.5 %collective-permute-done.2.b_ref = bf16[272,128]{1,0:T(8,128)(2,1)S(1)} collective-permute-done((bf16[272,128]{1,0:T(8,128)(2,1)S(1)}, bf16[272,128]{1,0:T(8,128)(2,1)S(1)}, u32[]{:S(2)}, u32[]{:S(2)}) %collective-permute-start.2) | collective-permute-done | bytes 69664 | tf_op jit(solution)/shard_map/ppermute | solution.py:435
  15.7 0.7 %collective-permute-start.4 = (bf16[272,128]{1,0:T(8,128)(2,1)S(1)}, bf16[272,128]{1,0:T(8,128)(2,1)S(1)}, u32[]{:S(2)}, u32[]{:S(2)}) collective-permute-start(bf16[272,128]{1,0:T(8,128)(2,1)S(1)} %collective-permute-done.2.b_ref), channel_id=1, source_target_pairs={{1,0},{0,1},{3,2},{2,3},{5,4},{4,5},{7,6},{6,7},{9,8},{8,9},{11,10... | collective-permute-start | bytes 208904 | tf_op jit(solution)/shard_map/ppermute | solution.py:435
  16.4 0.1 pad_add_fusion.frame_ref.refs_0_
  16.5 0.0 collective-permute-done.3.ta_ref
  16.5 0.8 %collective-permute-done.4.tb_ref = bf16[272,128]{1,0:T(8,128)(2,1)S(1)} collective-permute-done((bf16[272,128]{1,0:T(8,128)(2,1)S(1)}, bf16[272,128]{1,0:T(8,128)(2,1)S(1)}, u32[]{:S(2)}, u32[]{:S(2)}) %collective-permute-start.4) | collective-permute-done | bytes 69664 | tf_op jit(solution)/shard_map/ppermute | solution.py:435
  17.3 0.6 %two_rows.1 = (bf16[672,128]{1,0:T(8,128)(2,1)S(1)}, bf16[672,128]{1,0:T(8,128)(2,1)S(1)}) custom-call(s32[4]{0:T(128)S(1)} %pad_add_fusion.frame_ref.refs_0_, bf16[272,128]{1,0:T(8,128)(2,1)S(1)} %pair_tiles.1.pair_ref, bf16[272,128]{1,0:T(8,128)(2,1)S(1)} %collective-permute-done.1.a_ref, bf16[272,128]{1,0:T(8,128)(2,1)S(1)} %collective-permute-done.2.b_ref, ...), custom_call_target="tpu_custom_call" | custom-call | tf_op jit(solution)/shard_map/two_rows/pallas_call | solution.py:313
  17.9 8.2 %collective-permute-start.6 = (bf16[672,128]{1,0:T(8,128)(2,1)S(1)}, bf16[672,128]{1,0:T(8,128)(2,1)S(1)}, u32[]{:S(2)}, u32[]{:S(2)}) collective-permute-start(bf16[672,128]{1,0:T(8,128)(2,1)S(1)} %get-tuple-element.16.own_ref), channel_id=1, source_target_pairs={{2,1},{1,2},{4,3},{3,4},{6,5},{5,6},{8,7},{7,8},{10,9},{9,10},{12,... | collective-permute-start | bytes 516104 | tf_op jit(solution)/shard_map/ppermute | solution.py:435
  26.1 1.9 %collective-permute-start.5 = (bf16[672,128]{1,0:T(8,128)(2,1)S(1)}, bf16[672,128]{1,0:T(8,128)(2,1)S(1)}, u32[]{:S(2)}, u32[]{:S(2)}) collective-permute-start(bf16[672,128]{1,0:T(8,128)(2,1)S(1)} %get-tuple-element.16.own_ref), channel_id=1, source_target_pairs={{3,0},{5,2},{0,3},{7,4},{2,5},{9,6},{4,7},{11,8},{6,9},{13,10},{8,... | collective-permute-start | bytes 516104 | tf_op jit(solution)/shard_map/ppermute | solution.py:435
  28.0 5.6 %near_sums.1 = (f32[36,128,128]{2,1,0:T(8,128)S(1)}, f32[24,128,128]{2,1,0:T(8,128)S(1)}, f32[64,128]{1,0:T(8,128)S(1)}) custom-call(s32[4]{0:T(128)S(1)} %pad_add_fusion.frame_ref.refs_0_, bf16[672,128]{1,0:T(8,128)(2,1)S(1)} %get-tuple-element.16.own_ref, bf16[672,128]{1,0:T(8,128)(2,1)S(1)} %get-tuple-element.17.other_ref), custom_call_target="tpu_custom_call" | custom-call | flops 6000000000 | bytes 5000000 | tf_op jit(solution)/shard_map/near_sums/pallas_call | solution.py:324
  33.6 0.0 copy-start.1
  33.6 0.0 collective-permute-done.6.refs_1_.refs_2_
  33.7 1.9 %collective-permute-start.7 = (bf16[416,128]{1,0:T(8,128)(2,1)S(1)}, bf16[416,128]{1,0:T(8,128)(2,1)S(1)}, u32[]{:S(2)}, u32[]{:S(2)}) collective-permute-start(bf16[416,128]{1,0:T(8,128)(2,1)S(1)} %slice.6), channel_id=1, source_target_pairs={{1,0},{0,1},{3,2},{2,3},{5,4},{4,5},{7,6},{6,7},{9,8},{8,9},{11,10... | collective-permute-start | bytes 319496 | tf_op jit(solution)/shard_map/ppermute | solution.py:435
  35.6 1.0 %collective-permute-done.7.refs_2_ = bf16[416,128]{1,0:T(8,128)(2,1)S(1)} collective-permute-done((bf16[416,128]{1,0:T(8,128)(2,1)S(1)}, bf16[416,128]{1,0:T(8,128)(2,1)S(1)}, u32[]{:S(2)}, u32[]{:S(2)}) %collective-permute-start.7) | collective-permute-done | bytes 106528 | tf_op jit(solution)/shard_map/ppermute | solution.py:435
  36.5 6.0 %rest_points.1.rest_ref = bf16[12,2,128,128]{3,2,1,0:T(8,128)(2,1)S(1)} custom-call(s32[4]{0:T(128)S(1)} %pad_add_fusion.frame_ref.refs_0_, bf16[672,128]{1,0:T(8,128)(2,1)S(1)} %collective-permute-done.6.refs_1_.refs_2_, bf16[416,128]{1,0:T(8,128)(2,1)S(1)} %collective-permute-done.7.refs_2_, f32[24,128,128]{2,1,0:T(8,128)S(1)} %get-tuple-element.20.refs_3_, ...), custom_call_target="tpu_custom_call" | custom-call | flops 1000000 | bytes 1000 | tf_op jit(solution)/shard_map/rest_points/pallas_call | solution.py:341
  42.6 0.0 collective-permute-done.5
  42.6 0.4 collective-permute-start.8
  43.0 0.0 copy-done.1
  43.0 0.4 anomalies.1
  43.5 0.5 collective-permute-start.9
  43.9 0.1 collective-permute-done.8.refs_1_
  44.1 9.0 %first_points.1.first_ref = bf16[18,2,128,128]{3,2,1,0:T(8,128)(2,1)S(1)} custom-call(s32[4]{0:T(128)S(1)} %pad_add_fusion.frame_ref.refs_0_, bf16[672,128]{1,0:T(8,128)(2,1)S(1)} %collective-permute-done.8.refs_1_, bf16[672,128]{1,0:T(8,128)(2,1)S(1)} %collective-permute-done.6.refs_1_.refs_2_, f32[36,128,128]{2,1,0:T(8,128)S(1)} %get-tuple-element.22.refs_3_, ...), custom_call_target="tpu_custom_call" | custom-call | flops 8999999488 | bytes 9000000 | tf_op jit(solution)/shard_map/first_points/pallas_call | solution.py:341
  53.0 0.0 collective-permute-done.9.high_ref
  53.1 3.4 %apply_transforms.1 = bf16[8,8,64,128]{3,2,1,0:T(8,128)(2,1)} custom-call(s32[4]{0:T(128)S(1)} %pad_add_fusion.frame_ref.refs_0_, bf16[8,8,64,128]{3,2,1,0:T(8,128)(2,1)S(1)} %get-tuple-element.14.anom_ref, f32[8,8,64,128]{3,2,1,0:T(8,128)S(1)} %get-tuple-element.15.mean_ref, bf16[18,2,128,128]{3,2,1,0:T(8,128)(2,1)S(1)} %first_points.1.first_ref, ...), custom_call_target="tpu_custom_call" | custom-call | tf_op jit(solution)/shard_map/apply_transforms/pallas_call | solution.py:417
  (3 shorter events, 0.0 us)
Async XLA Ops:
  2.1 1.8 %collective-permute-start = (bf16[144,128]{1,0:T(8,128)(2,1)}, bf16[144,128]{1,0:T(8,128)(2,1)S(1)}, u32[]{:S(2)}, u32[]{:S(2)}) collective-permute-start(bf16[144,128]{1,0:T(8,128)(2,1)} %pack_slots.1.own_ref), channel_id=1, source_target_pairs={{1,0},{0,1},{3,2},{2,3},{5,4},{4,5},{7,6},{6,7},{9,8},{8,9},{11,10... | collective-permute-start | bytes 110600 | tf_op jit(solution)/shard_map/ppermute | solution.py:435
  3.9 0.8 %copy-start = (bf16[144,128]{1,0:T(8,128)(2,1)S(1)}, bf16[144,128]{1,0:T(8,128)(2,1)}, u32[]{:S(2)}) copy-start(bf16[144,128]{1,0:T(8,128)(2,1)} %pack_slots.1.own_ref) | copy-start | bytes 110596
  4.7 8.5 %collective-permute-start.1 = (bf16[272,128]{1,0:T(8,128)(2,1)S(1)}, bf16[272,128]{1,0:T(8,128)(2,1)S(1)}, u32[]{:S(2)}, u32[]{:S(2)}) collective-permute-start(bf16[272,128]{1,0:T(8,128)(2,1)S(1)} %pair_tiles.1.pair_ref), channel_id=1, source_target_pairs={{16,0},{241,1},{18,2},{243,3},{20,4},{245,5},{22,6},{247,7},{24,8}... | collective-permute-start | bytes 208904 | tf_op jit(solution)/shard_map/ppermute | solution.py:435
  11.3 4.4 %collective-permute-start.2 = (bf16[272,128]{1,0:T(8,128)(2,1)S(1)}, bf16[272,128]{1,0:T(8,128)(2,1)S(1)}, u32[]{:S(2)}, u32[]{:S(2)}) collective-permute-start(bf16[272,128]{1,0:T(8,128)(2,1)S(1)} %pair_tiles.1.pair_ref), channel_id=1, source_target_pairs={{224,0},{33,1},{226,2},{35,3},{228,4},{37,5},{230,6},{39,7},{232,8... | collective-permute-start | bytes 208904 | tf_op jit(solution)/shard_map/ppermute | solution.py:435
  13.2 3.3 %collective-permute-start.3 = (bf16[272,128]{1,0:T(8,128)(2,1)S(1)}, bf16[272,128]{1,0:T(8,128)(2,1)S(1)}, u32[]{:S(2)}, u32[]{:S(2)}) collective-permute-start(bf16[272,128]{1,0:T(8,128)(2,1)S(1)} %collective-permute-done.1.a_ref), channel_id=1, source_target_pairs={{1,0},{0,1},{3,2},{2,3},{5,4},{4,5},{7,6},{6,7},{9,8},{8,9},{11,10... | collective-permute-start | bytes 208904 | tf_op jit(solution)/shard_map/ppermute | solution.py:435
  15.7 1.6 %collective-permute-start.4 = (bf16[272,128]{1,0:T(8,128)(2,1)S(1)}, bf16[272,128]{1,0:T(8,128)(2,1)S(1)}, u32[]{:S(2)}, u32[]{:S(2)}) collective-permute-start(bf16[272,128]{1,0:T(8,128)(2,1)S(1)} %collective-permute-done.2.b_ref), channel_id=1, source_target_pairs={{1,0},{0,1},{3,2},{2,3},{5,4},{4,5},{7,6},{6,7},{9,8},{8,9},{11,10... | collective-permute-start | bytes 208904 | tf_op jit(solution)/shard_map/ppermute | solution.py:435
  17.9 15.8 %collective-permute-start.6 = (bf16[672,128]{1,0:T(8,128)(2,1)S(1)}, bf16[672,128]{1,0:T(8,128)(2,1)S(1)}, u32[]{:S(2)}, u32[]{:S(2)}) collective-permute-start(bf16[672,128]{1,0:T(8,128)(2,1)S(1)} %get-tuple-element.16.own_ref), channel_id=1, source_target_pairs={{2,1},{1,2},{4,3},{3,4},{6,5},{5,6},{8,7},{7,8},{10,9},{9,10},{12,... | collective-permute-start | bytes 516104 | tf_op jit(solution)/shard_map/ppermute | solution.py:435
  26.1 16.5 %collective-permute-start.5 = (bf16[672,128]{1,0:T(8,128)(2,1)S(1)}, bf16[672,128]{1,0:T(8,128)(2,1)S(1)}, u32[]{:S(2)}, u32[]{:S(2)}) collective-permute-start(bf16[672,128]{1,0:T(8,128)(2,1)S(1)} %get-tuple-element.16.own_ref), channel_id=1, source_target_pairs={{3,0},{5,2},{0,3},{7,4},{2,5},{9,6},{4,7},{11,8},{6,9},{13,10},{8,... | collective-permute-start | bytes 516104 | tf_op jit(solution)/shard_map/ppermute | solution.py:435
  33.6 9.4 %copy-start.1 = (bf16[8,8,64,128]{3,2,1,0:T(8,128)(2,1)S(1)}, bf16[8,8,64,128]{3,2,1,0:T(8,128)(2,1)}, u32[]{:S(2)}) copy-start(bf16[8,8,64,128]{3,2,1,0:T(8,128)(2,1)} %ens_ref.1) | copy-start | bytes 3145732
  33.7 2.9 %collective-permute-start.7 = (bf16[416,128]{1,0:T(8,128)(2,1)S(1)}, bf16[416,128]{1,0:T(8,128)(2,1)S(1)}, u32[]{:S(2)}, u32[]{:S(2)}) collective-permute-start(bf16[416,128]{1,0:T(8,128)(2,1)S(1)} %slice.6), channel_id=1, source_target_pairs={{1,0},{0,1},{3,2},{2,3},{5,4},{4,5},{7,6},{6,7},{9,8},{8,9},{11,10... | collective-permute-start | bytes 319496 | tf_op jit(solution)/shard_map/ppermute | solution.py:435
  42.6 1.5 %collective-permute-start.8 = (bf16[672,128]{1,0:T(8,128)(2,1)S(1)}, bf16[672,128]{1,0:T(8,128)(2,1)S(1)}, u32[]{:S(2)}, u32[]{:S(2)}) collective-permute-start(bf16[672,128]{1,0:T(8,128)(2,1)S(1)} %collective-permute-done.5), channel_id=1, source_target_pairs={{1,0},{0,1},{3,2},{2,3},{5,4},{4,5},{7,6},{6,7},{9,8},{8,9},{11,10... | collective-permute-start | bytes 516104 | tf_op jit(solution)/shard_map/ppermute | solution.py:435
  43.5 9.6 %collective-permute-start.9 = (bf16[6,2,128,128]{3,2,1,0:T(8,128)(2,1)S(1)}, bf16[6,2,128,128]{3,2,1,0:T(8,128)(2,1)S(1)}, u32[]{:S(2)}, u32[]{:S(2)}) collective-permute-start(bf16[6,2,128,128]{3,2,1,0:T(8,128)(2,1)S(1)} %slice.8), channel_id=1, source_target_pairs={{1,0},{0,1},{3,2},{2,3},{5,4},{4,5},{7,6},{6,7},{9,8},{8,9},{11,10... | collective-permute-start | bytes 1179656 | tf_op jit(solution)/shard_map/ppermute | solution.py:435

commit v8 on v6

--- a/solution.py
+++ b/solution.py
@@ -21,7 +21,7 @@
 EDGES = 2
 SLOTS = 2
 REST = 1_000_000
-LAG = 10
+LAG = 8
 
 NT = (((1,), (1,)), ((), ()))
 NN = (((1,), (0,)), ((), ()))
@@ -222,6 +222,7 @@
     row = lax.broadcasted_iota(jnp.int32, (K, K), 0)
     col = lax.broadcasted_iota(jnp.int32, (K, K), 1)
     eye = jnp.where(row == col, 1.0, 0.0).astype(F32)
+    c0_eye = jnp.where(row == col, C0, 0.0).astype(F32)
 
     def steps(first):
         ids = [(p, g) for p in range(first, min(first + batch, len(points))) for g in range(2)]
@@ -251,7 +252,7 @@
             def run():
                 high = [times(parts(q), parts(C3 * v + C4 * q)) for v, q in zip(now[x], now[sq])]
                 now[out] = [
-                    split(C0 * eye + C1 * v + C2 * q + h) for v, q, h in zip(now[x], now[sq], high)
+                    split((c0_eye + C1 * v) + (C2 * q + h)) for v, q, h in zip(now[x], now[sq], high)
                 ]
 
             return run

time: 55.8 us -> 55.6 us (level)
  no operation moved by 1% of the time
where the time goes in v8:
time: 55.6 us; the launch traced here: 55.4 us
  Pallas kernels  25.8 us (46%)
  starting transfers between devices  18.5 us (33%)
  waiting for transfers between devices  9.5 us (17%)
  local copies, waits for them, and re-layouts  0.81 us (1%)
  between operations  0.75 us (1%)
    ppermute x10, starting transfers between devices, moved(): return lax.ppermute(block, ('gx', 'gy'), pairs)  18.5 us
    pallas_call x2, Pallas kernels, transforms(): pl.pallas_call(functools.partial(points_kernel, points, rows, batch), out...  14.8 us
    ppermute x10, waiting for transfers between devices, moved(): return lax.ppermute(block, ('gx', 'gy'), pairs)  9.5 us
    pallas_call x1, Pallas kernels, near_sums(): pl.pallas_call(near_kernel, out_shape=[jax.ShapeDtypeStruct((2 * FIRST, K...  5.57 us
    pallas_call x1, Pallas kernels, apply(): pl.pallas_call(apply_kernel, out_shape=jax.ShapeDtypeStruct(anom.shape, B...  3.44 us
    pallas_call x1, Pallas kernels, shards(): pl.pallas_call(pack_kernel, out_shape=jax.ShapeDtypeStruct((ROWS, K), BF1...  1.5 us
  transfers between devices with their start and end apart: 10, of which 6 were waited for; matrix products, arithmetic and copies ran while one was open for 0% of the time, Pallas kernels for 38%

profile of v8, /device:TPU:25, one launch (start us, length us, event | category | flops | bytes accessed | tf_op | source)
XLA Modules:
  0.0 55.4 jit_solution(3593856393139713991)
XLA Ops:
  0.7 1.5 %pack_slots.1.own_ref = bf16[144,128]{1,0:T(8,128)(2,1)} custom-call(s32[1,1]{1,0:T(1,128)S(6)} %copy.7.count_ref, bf16[128,128]{1,0:T(8,128)(2,1)} %bitcast.7, bf16[1,128]{1,0:T(2,128)(2,1)} %bitcast.9, bf16[1,128]{1,0:T(2,128)(2,1)} %bitcast.10, s32[2,128]{1,0:T(2,128)} %bitcast.8), custom_call_target="tpu_custom_call" | custom-call | tf_op jit(solution)/shard_map/pack_slots/pallas_call | solution.py:443
  2.1 0.7 %collective-permute-start = (bf16[144,128]{1,0:T(8,128)(2,1)}, bf16[144,128]{1,0:T(8,128)(2,1)S(1)}, u32[]{:S(2)}, u32[]{:S(2)}) collective-permute-start(bf16[144,128]{1,0:T(8,128)(2,1)} %pack_slots.1.own_ref), channel_id=1, source_target_pairs={{1,0},{0,1},{3,2},{2,3},{5,4},{4,5},{7,6},{6,7},{9,8},{8,9},{11,10... | collective-permute-start | bytes 110600 | tf_op jit(solution)/shard_map/ppermute | solution.py:423
  2.8 1.1 %collective-permute-done.other_ref = bf16[144,128]{1,0:T(8,128)(2,1)S(1)} collective-permute-done((bf16[144,128]{1,0:T(8,128)(2,1)}, bf16[144,128]{1,0:T(8,128)(2,1)S(1)}, u32[]{:S(2)}, u32[]{:S(2)}) %collective-permute-start) | collective-permute-done | bytes 36896 | tf_op jit(solution)/shard_map/ppermute | solution.py:423
  3.9 0.0 copy-start
  3.9 0.8 %copy-done = bf16[144,128]{1,0:T(8,128)(2,1)S(1)} copy-done((bf16[144,128]{1,0:T(8,128)(2,1)S(1)}, bf16[144,128]{1,0:T(8,128)(2,1)}, u32[]{:S(2)}) %copy-start) | copy-done | bytes 36888
  4.7 6.6 %collective-permute-start.1 = (bf16[272,128]{1,0:T(8,128)(2,1)S(1)}, bf16[272,128]{1,0:T(8,128)(2,1)S(1)}, u32[]{:S(2)}, u32[]{:S(2)}) collective-permute-start(bf16[272,128]{1,0:T(8,128)(2,1)S(1)} %pair_tiles.1.pair_ref), channel_id=1, source_target_pairs={{16,0},{241,1},{18,2},{243,3},{20,4},{245,5},{22,6},{247,7},{24,8}... | collective-permute-start | bytes 208904 | tf_op jit(solution)/shard_map/ppermute | solution.py:423
  11.3 0.0 collective-permute-start.2
  11.3 1.9 %collective-permute-done.1.a_ref = bf16[272,128]{1,0:T(8,128)(2,1)S(1)} collective-permute-done((bf16[272,128]{1,0:T(8,128)(2,1)S(1)}, bf16[272,128]{1,0:T(8,128)(2,1)S(1)}, u32[]{:S(2)}, u32[]{:S(2)}) %collective-permute-start.1) | collective-permute-done | bytes 69664 | tf_op jit(solution)/shard_map/ppermute | solution.py:423
  13.2 0.0 collective-permute-start.3
  13.2 4.3 %collective-permute-done.2.b_ref = bf16[272,128]{1,0:T(8,128)(2,1)S(1)} collective-permute-done((bf16[272,128]{1,0:T(8,128)(2,1)S(1)}, bf16[272,128]{1,0:T(8,128)(2,1)S(1)}, u32[]{:S(2)}, u32[]{:S(2)}) %collective-permute-start.2) | collective-permute-done | bytes 69664 | tf_op jit(solution)/shard_map/ppermute | solution.py:423
  17.5 0.0 collective-permute-start.4
  17.5 0.1 pad_add_fusion.frame_ref.refs_0_
  17.6 0.0 collective-permute-done.3.ta_ref
  17.6 1.2 %collective-permute-done.4.tb_ref = bf16[272,128]{1,0:T(8,128)(2,1)S(1)} collective-permute-done((bf16[272,128]{1,0:T(8,128)(2,1)S(1)}, bf16[272,128]{1,0:T(8,128)(2,1)S(1)}, u32[]{:S(2)}, u32[]{:S(2)}) %collective-permute-start.4) | collective-permute-done | bytes 69664 | tf_op jit(solution)/shard_map/ppermute | solution.py:423
  18.8 6.4 %collective-permute-start.6 = (bf16[672,128]{1,0:T(8,128)(2,1)S(1)}, bf16[672,128]{1,0:T(8,128)(2,1)S(1)}, u32[]{:S(2)}, u32[]{:S(2)}) collective-permute-start(bf16[672,128]{1,0:T(8,128)(2,1)S(1)} %get-tuple-element.16.own_ref), channel_id=1, source_target_pairs={{2,1},{1,2},{4,3},{3,4},{6,5},{5,6},{8,7},{7,8},{10,9},{9,10},{12,... | collective-permute-start | bytes 516104 | tf_op jit(solution)/shard_map/ppermute | solution.py:423
  25.1 1.9 %collective-permute-start.5 = (bf16[672,128]{1,0:T(8,128)(2,1)S(1)}, bf16[672,128]{1,0:T(8,128)(2,1)S(1)}, u32[]{:S(2)}, u32[]{:S(2)}) collective-permute-start(bf16[672,128]{1,0:T(8,128)(2,1)S(1)} %get-tuple-element.16.own_ref), channel_id=1, source_target_pairs={{3,0},{5,2},{0,3},{7,4},{2,5},{9,6},{4,7},{11,8},{6,9},{13,10},{8,... | collective-permute-start | bytes 516104 | tf_op jit(solution)/shard_map/ppermute | solution.py:423
  27.1 5.6 %near_sums.1 = (f32[36,128,128]{2,1,0:T(8,128)S(1)}, f32[24,128,128]{2,1,0:T(8,128)S(1)}, f32[64,128]{1,0:T(8,128)S(1)}) custom-call(s32[3]{0:T(128)S(1)} %pad_add_fusion.frame_ref.refs_0_, bf16[672,128]{1,0:T(8,128)(2,1)S(1)} %get-tuple-element.16.own_ref, bf16[672,128]{1,0:T(8,128)(2,1)S(1)} %get-tuple-element.17.other_ref), custom_call_target="tpu_custom_call" | custom-call | flops 6000000000 | bytes 5000000 | tf_op jit(solution)/shard_map/near_sums/pallas_call | solution.py:312
  32.6 0.0 copy-start.1
  32.7 0.0 collective-permute-done.6.refs_1_.refs_2_
  32.7 2.0 %collective-permute-start.7 = (bf16[416,128]{1,0:T(8,128)(2,1)S(1)}, bf16[416,128]{1,0:T(8,128)(2,1)S(1)}, u32[]{:S(2)}, u32[]{:S(2)}) collective-permute-start(bf16[416,128]{1,0:T(8,128)(2,1)S(1)} %slice.6), channel_id=1, source_target_pairs={{1,0},{0,1},{3,2},{2,3},{5,4},{4,5},{7,6},{6,7},{9,8},{8,9},{11,10... | collective-permute-start | bytes 319496 | tf_op jit(solution)/shard_map/ppermute | solution.py:423
  34.6 1.0 %collective-permute-done.7.refs_2_ = bf16[416,128]{1,0:T(8,128)(2,1)S(1)} collective-permute-done((bf16[416,128]{1,0:T(8,128)(2,1)S(1)}, bf16[416,128]{1,0:T(8,128)(2,1)S(1)}, u32[]{:S(2)}, u32[]{:S(2)}) %collective-permute-start.7) | collective-permute-done | bytes 106528 | tf_op jit(solution)/shard_map/ppermute | solution.py:423
  35.6 6.0 %rest_points.1.rest_ref = bf16[12,2,128,128]{3,2,1,0:T(8,128)(2,1)S(1)} custom-call(s32[3]{0:T(128)S(1)} %pad_add_fusion.frame_ref.refs_0_, bf16[672,128]{1,0:T(8,128)(2,1)S(1)} %collective-permute-done.6.refs_1_.refs_2_, bf16[416,128]{1,0:T(8,128)(2,1)S(1)} %collective-permute-done.7.refs_2_, f32[24,128,128]{2,1,0:T(8,128)S(1)} %get-tuple-element.20.refs_3_, ...), custom_call_target="tpu_custom_call" | custom-call | flops 1000000 | bytes 1000 | tf_op jit(solution)/shard_map/rest_points/pallas_call | solution.py:329
  41.6 0.0 collective-permute-done.5
  41.6 0.4 collective-permute-start.8
  42.0 0.0 copy-done.1
  42.0 0.4 anomalies.1
  42.5 0.5 collective-permute-start.9
  42.9 0.1 collective-permute-done.8.refs_1_
  43.1 8.8 %first_points.1.first_ref = bf16[18,2,128,128]{3,2,1,0:T(8,128)(2,1)S(1)} custom-call(s32[3]{0:T(128)S(1)} %pad_add_fusion.frame_ref.refs_0_, bf16[672,128]{1,0:T(8,128)(2,1)S(1)} %collective-permute-done.8.refs_1_, bf16[672,128]{1,0:T(8,128)(2,1)S(1)} %collective-permute-done.6.refs_1_.refs_2_, f32[36,128,128]{2,1,0:T(8,128)S(1)} %get-tuple-element.22.refs_3_, ...), custom_call_target="tpu_custom_call" | custom-call | flops 8999999488 | bytes 9000000 | tf_op jit(solution)/shard_map/first_points/pallas_call | solution.py:329
  51.9 0.0 collective-permute-done.9.high_ref
  51.9 3.4 %apply_transforms.1 = bf16[8,8,64,128]{3,2,1,0:T(8,128)(2,1)} custom-call(s32[3]{0:T(128)S(1)} %pad_add_fusion.frame_ref.refs_0_, bf16[8,8,64,128]{3,2,1,0:T(8,128)(2,1)S(1)} %get-tuple-element.14.anom_ref, f32[8,8,64,128]{3,2,1,0:T(8,128)S(1)} %get-tuple-element.15.mean_ref, bf16[18,2,128,128]{3,2,1,0:T(8,128)(2,1)S(1)} %first_points.1.first_ref, ...), custom_call_target="tpu_custom_call" | custom-call | tf_op jit(solution)/shard_map/apply_transforms/pallas_call | solution.py:405
  (4 shorter events, 0.1 us)
Async XLA Ops:
  2.1 1.8 %collective-permute-start = (bf16[144,128]{1,0:T(8,128)(2,1)}, bf16[144,128]{1,0:T(8,128)(2,1)S(1)}, u32[]{:S(2)}, u32[]{:S(2)}) collective-permute-start(bf16[144,128]{1,0:T(8,128)(2,1)} %pack_slots.1.own_ref), channel_id=1, source_target_pairs={{1,0},{0,1},{3,2},{2,3},{5,4},{4,5},{7,6},{6,7},{9,8},{8,9},{11,10... | collective-permute-start | bytes 110600 | tf_op jit(solution)/shard_map/ppermute | solution.py:423
  3.9 0.8 %copy-start = (bf16[144,128]{1,0:T(8,128)(2,1)S(1)}, bf16[144,128]{1,0:T(8,128)(2,1)}, u32[]{:S(2)}) copy-start(bf16[144,128]{1,0:T(8,128)(2,1)} %pack_slots.1.own_ref) | copy-start | bytes 110596
  4.7 8.5 %collective-permute-start.1 = (bf16[272,128]{1,0:T(8,128)(2,1)S(1)}, bf16[272,128]{1,0:T(8,128)(2,1)S(1)}, u32[]{:S(2)}, u32[]{:S(2)}) collective-permute-start(bf16[272,128]{1,0:T(8,128)(2,1)S(1)} %pair_tiles.1.pair_ref), channel_id=1, source_target_pairs={{16,0},{241,1},{18,2},{243,3},{20,4},{245,5},{22,6},{247,7},{24,8}... | collective-permute-start | bytes 208904 | tf_op jit(solution)/shard_map/ppermute | solution.py:423
  11.3 6.2 %collective-permute-start.2 = (bf16[272,128]{1,0:T(8,128)(2,1)S(1)}, bf16[272,128]{1,0:T(8,128)(2,1)S(1)}, u32[]{:S(2)}, u32[]{:S(2)}) collective-permute-start(bf16[272,128]{1,0:T(8,128)(2,1)S(1)} %pair_tiles.1.pair_ref), channel_id=1, source_target_pairs={{32,0},{225,1},{34,2},{227,3},{36,4},{229,5},{38,6},{231,7},{40,8}... | collective-permute-start | bytes 208904 | tf_op jit(solution)/shard_map/ppermute | solution.py:423
  13.2 4.4 %collective-permute-start.3 = (bf16[272,128]{1,0:T(8,128)(2,1)S(1)}, bf16[272,128]{1,0:T(8,128)(2,1)S(1)}, u32[]{:S(2)}, u32[]{:S(2)}) collective-permute-start(bf16[272,128]{1,0:T(8,128)(2,1)S(1)} %collective-permute-done.1.a_ref), channel_id=1, source_target_pairs={{1,0},{0,1},{3,2},{2,3},{5,4},{4,5},{7,6},{6,7},{9,8},{8,9},{11,10... | collective-permute-start | bytes 208904 | tf_op jit(solution)/shard_map/ppermute | solution.py:423
  17.5 1.3 %collective-permute-start.4 = (bf16[272,128]{1,0:T(8,128)(2,1)S(1)}, bf16[272,128]{1,0:T(8,128)(2,1)S(1)}, u32[]{:S(2)}, u32[]{:S(2)}) collective-permute-start(bf16[272,128]{1,0:T(8,128)(2,1)S(1)} %collective-permute-done.2.b_ref), channel_id=1, source_target_pairs={{1,0},{0,1},{3,2},{2,3},{5,4},{4,5},{7,6},{6,7},{9,8},{8,9},{11,10... | collective-permute-start | bytes 208904 | tf_op jit(solution)/shard_map/ppermute | solution.py:423
  18.8 13.9 %collective-permute-start.6 = (bf16[672,128]{1,0:T(8,128)(2,1)S(1)}, bf16[672,128]{1,0:T(8,128)(2,1)S(1)}, u32[]{:S(2)}, u32[]{:S(2)}) collective-permute-start(bf16[672,128]{1,0:T(8,128)(2,1)S(1)} %get-tuple-element.16.own_ref), channel_id=1, source_target_pairs={{2,1},{1,2},{4,3},{3,4},{6,5},{5,6},{8,7},{7,8},{10,9},{9,10},{12,... | collective-permute-start | bytes 516104 | tf_op jit(solution)/shard_map/ppermute | solution.py:423
  25.1 16.4 %collective-permute-start.5 = (bf16[672,128]{1,0:T(8,128)(2,1)S(1)}, bf16[672,128]{1,0:T(8,128)(2,1)S(1)}, u32[]{:S(2)}, u32[]{:S(2)}) collective-permute-start(bf16[672,128]{1,0:T(8,128)(2,1)S(1)} %get-tuple-element.16.own_ref), channel_id=1, source_target_pairs={{3,0},{5,2},{0,3},{7,4},{2,5},{9,6},{4,7},{11,8},{6,9},{13,10},{8,... | collective-permute-start | bytes 516104 | tf_op jit(solution)/shard_map/ppermute | solution.py:423
  32.6 9.4 %copy-start.1 = (bf16[8,8,64,128]{3,2,1,0:T(8,128)(2,1)S(1)}, bf16[8,8,64,128]{3,2,1,0:T(8,128)(2,1)}, u32[]{:S(2)}) copy-start(bf16[8,8,64,128]{3,2,1,0:T(8,128)(2,1)} %ens_ref.1) | copy-start | bytes 3145732
  32.7 2.9 %collective-permute-start.7 = (bf16[416,128]{1,0:T(8,128)(2,1)S(1)}, bf16[416,128]{1,0:T(8,128)(2,1)S(1)}, u32[]{:S(2)}, u32[]{:S(2)}) collective-permute-start(bf16[416,128]{1,0:T(8,128)(2,1)S(1)} %slice.6), channel_id=1, source_target_pairs={{1,0},{0,1},{3,2},{2,3},{5,4},{4,5},{7,6},{6,7},{9,8},{8,9},{11,10... | collective-permute-start | bytes 319496 | tf_op jit(solution)/shard_map/ppermute | solution.py:423
  41.6 1.5 %collective-permute-start.8 = (bf16[672,128]{1,0:T(8,128)(2,1)S(1)}, bf16[672,128]{1,0:T(8,128)(2,1)S(1)}, u32[]{:S(2)}, u32[]{:S(2)}) collective-permute-start(bf16[672,128]{1,0:T(8,128)(2,1)S(1)} %collective-permute-done.5), channel_id=1, source_target_pairs={{1,0},{0,1},{3,2},{2,3},{5,4},{4,5},{7,6},{6,7},{9,8},{8,9},{11,10... | collective-permute-start | bytes 516104 | tf_op jit(solution)/shard_map/ppermute | solution.py:423
  42.5 9.4 %collective-permute-start.9 = (bf16[6,2,128,128]{3,2,1,0:T(8,128)(2,1)S(1)}, bf16[6,2,128,128]{3,2,1,0:T(8,128)(2,1)S(1)}, u32[]{:S(2)}, u32[]{:S(2)}) collective-permute-start(bf16[6,2,128,128]{3,2,1,0:T(8,128)(2,1)S(1)} %slice.8), channel_id=1, source_target_pairs={{1,0},{0,1},{3,2},{2,3},{5,4},{4,5},{7,6},{6,7},{9,8},{8,9},{11,10... | collective-permute-start | bytes 1179656 | tf_op jit(solution)/shard_map/ppermute | solution.py:423
